TPU v7x, 256 devices: a whole 4x4x8 slice. The times are simulated.
256 devices in a mesh: gx: 16 (over z, y_hi), gy: 16 (over y_lo, x, core).
Axes of the slice: x: 4, y: 4 (y_hi: 2, y_lo: 2; y = y_hi * 2 + y_lo), z: 8, core: 2. Of those that a mesh axis runs over, the one named last changes fastest.
Arguments:
- populations: float32 [19, 256, 256, 256], P(None, 'gx', 'gy'), may hold values from 0.022 to 0.4, as said below
- concentrations: float32 [2, 256, 256, 256], P(None, 'gx', 'gy'), may hold values from 0.5 to 1.5
- potential: float32 [256, 256, 256], P('gx', 'gy'), may hold values from -4 to 4
- mobility: float32 [256, 256, 256], P('gx', 'gy'), may hold values from 0.5 to 2
- solid: int32 [256, 256, 256], P('gx', 'gy'), may hold values from 0 to 1, as said below
- wall_class: int32 [256, 256, 256], P('gx', 'gy'), may hold values from 0 to 3
- wall_charge: float32 [4], replicated, may hold values from -2 to -0.25
Outputs:
- populations_out: float32 [19, 256, 256, 256], P(None, 'gx', 'gy')
- concentrations_out: float32 [2, 256, 256, 256], P(None, 'gx', 'gy')
- potential_out: float32 [256, 256, 256], P('gx', 'gy')
Inputs may be any that keep to these rules, and one draw needn't show every extreme that they name: populations[i] lies within 0.8 w_i to 1.2 w_i. 1 marks a solid node.
All inputs are finite; a program needn't handle non-finite values.
Results may differ from a plain program's by a relative error of at most 0.00002.
Values sent between devices are 32-bit elements; how exact they have to be, the bound alone decides.
No kernel may reach another device: no remote copies, remote signals or barrier semaphores. Data moves between devices by JAX's collectives and lax.ppermute only.
A program may use at most 128 MiB of HBM per device.

v0:
```python
import jax
import jax.numpy as jnp
from jax import lax
from jax.experimental import pallas as pl
from jax.experimental.pallas import tpu as pltpu
from jax.sharding import PartitionSpec as P

C = [(0, 0, 0), (1, 0, 0), (-1, 0, 0), (0, 1, 0), (0, -1, 0), (0, 0, 1), (0, 0, -1),
     (1, 1, 0), (-1, -1, 0), (1, -1, 0), (-1, 1, 0), (1, 0, 1), (-1, 0, -1), (1, 0, -1), (-1, 0, 1),
     (0, 1, 1), (0, -1, -1), (0, 1, -1), (0, -1, 1)]
W = [1.0 / 3.0] + [1.0 / 18.0] * 6 + [1.0 / 36.0] * 12
XPOS = [i for i in range(19) if C[i][0] == 1]
XNEG = [i for i in range(19) if C[i][0] == -1]
YPOS = [i for i in range(19) if C[i][1] == 1]
YNEG = [i for i in range(19) if C[i][1] == -1]
RATES = (0.06, 0.08)
VAL = (1.0, -1.0)
N = 16
Z = 256
CHUNK = 4
RING = 6
OFF = 8
ROWS = 7 * N + 8
LINE = 7 * N
F32 = jnp.float32
VM = pltpu.VMEM


def sds(*shape):
    return jax.ShapeDtypeStruct(shape, F32)


def params(mib):
    return pltpu.CompilerParams(vmem_limit_bytes=mib * 1024 * 1024)


def rows():
    return lax.broadcasted_iota(jnp.int32, (N, Z), 0)


def roll_y(v, s):
    return pltpu.roll(v, s % v.shape[0], 0)


def roll_z(v, s):
    return pltpu.roll(v, s % v.shape[1], 1)


def row_of(v, y):
    return v[y:y + 1, :]


def spread(row):
    return jnp.broadcast_to(row, (N, Z))


def shift_up(v):
    return jnp.where(rows() == 0, 0.0, roll_y(v, 1))


def shift_down(v):
    return jnp.where(rows() == N - 1, 0.0, roll_y(v, -1))


def shift_by(v, c):
    return shift_up(v) if c == 1 else shift_down(v) if c == -1 else v


def call(kernel, outs, name, specs, scratch=(), mib=16, flops=0, out_specs=None, moved=0):
    return pl.pallas_call(
        kernel,
        in_specs=[pl.BlockSpec(memory_space={"v": VM, "h": pltpu.HBM, "s": pltpu.SMEM}[c]) for c in specs],
        out_specs=[pl.BlockSpec(memory_space={"v": VM, "h": pltpu.HBM}[c]) for c in out_specs or "v" * len(outs)],
        out_shape=outs,
        scratch_shapes=list(scratch),
        compiler_params=params(mib),
        cost_estimate=pl.CostEstimate(flops=flops, bytes_accessed=moved, transcendentals=0),
        name=name,
    )


def faces_kernel(pot_h, conc_h, mob_h, solid_h, gx_hi, gx_lo, gy_hi, gy_lo, pot, conc, cond, mob, solid, sems):
    pairs = ((pot_h, pot), (conc_h, conc), (mob_h, mob), (solid_h, solid))
    copies = [pltpu.make_async_copy(a, b, sems.at[q]) for q, (a, b) in enumerate(pairs)]
    for c in copies:
        c.start()
    for c in copies:
        c.wait()

    def step(x, carry):
        here = pl.ds(x, 1)
        cond[x] = jnp.where(solid[x] == 0, jnp.sqrt(mob[x]), 0.0)
        for r in range(RING):
            gy_hi[r, here, :] = pot[x, N - 1 - r:N - r, :]
            gy_lo[r, here, :] = pot[x, r:r + 1, :]
        for q, v in ((0, conc.at[0]), (1, conc.at[1]), (2, cond)):
            gy_hi[RING + q, here, :] = v[x, N - 1:N, :]
            gy_lo[RING + q, here, :] = v[x, 0:1, :]
        return carry

    lax.fori_loop(0, N, step, 0, unroll=2)
    for x, face in ((N - 1, gx_hi), (0, gx_lo)):
        face[0] = pot[x]
        face[1] = conc[0, x]
        face[2] = conc[1, x]
        face[3] = cond[x]


def post_of(p, fluid, q, slopes):
    pull = jnp.where(fluid, q * (-0.001), 0.0)
    force = [pull * d for d in slopes]
    density = p[0]
    for i in range(1, 19):
        density = density + p[i]
    inv = 1.0 / density
    u = []
    for a in range(3):
        total = 0.9 * force[a]
        for i in range(1, 19, 2):
            if C[i][a]:
                term = p[i] - p[i + 1]
                total = total + term if C[i][a] == 1 else total - term
        u.append(total * inv)
    base = 1.0 - 1.5 * (u[0] * u[0] + u[1] * u[1] + u[2] * u[2])
    scaled = density * (10.0 / 9.0)
    out = [jnp.where(fluid, (W[0] * scaled) * base - p[0] * (1.0 / 9.0), p[0])]
    for i in range(1, 19, 2):
        along = None
        for a in range(3):
            if C[i][a]:
                term = u[a] if C[i][a] == 1 else -u[a]
                along = term if along is None else along + term
        even = base + 4.5 * along * along
        odd = 3.0 * along
        ws = W[i] * scaled
        fwd = ws * (even + odd) - p[i] * (1.0 / 9.0)
        bwd = ws * (even - odd) - p[i + 1] * (1.0 / 9.0)
        out.append(jnp.where(fluid, fwd, p[i + 1]))
        out.append(jnp.where(fluid, bwd, p[i]))
    return out, force


def sums(values, keep):
    total = [None] * 4
    for cy in (0, 1, -1):
        part = [None] * 4
        for i, v in values:
            if C[i][1] != cy:
                continue
            for m, c in enumerate((1,) + C[i]):
                if c and m != 2:
                    w = v if c == 1 else -v
                    part[m] = w if part[m] is None else part[m] + w
        for m in (0, 1, 3):
            if part[m] is None:
                continue
            w = part[m] if keep[cy] is None else jnp.where(keep[cy], part[m], 0.0)
            total[m] = w if total[m] is None else total[m] + w
            if m == 0 and cy:
                w = w if cy == 1 else -w
                total[2] = w if total[2] is None else total[2] + w
    return total


def collide_kernel(pops, pot, conc, cond, buf, mom, px_lo, px_hi, pr_lo, pr_hi, held, sems, psems):
    chunks = [pltpu.make_async_copy(pops.at[:, pl.ds(CHUNK * s, CHUNK)], held.at[:, pl.ds(CHUNK * s, CHUNK)], sems.at[s])
              for s in range(N // CHUNK)]
    ends = [pltpu.make_async_copy(pops.at[:, 0], px_lo, psems.at[0]),
            pltpu.make_async_copy(pops.at[:, N - 1], px_hi, psems.at[1])]
    for c in chunks + ends:
        c.start()
    row = rows()
    zero = jnp.zeros((N, Z), F32)
    keep = {0: (row >= 1) & (row <= N - 2), 1: row >= 2, -1: row <= N - 3}
    for m in range(4):
        mom[m, 0] = zero
        mom[m, 1] = zero

    def step(x, carry):
        here = pl.ds(x, 1)
        p = [held[i, x] for i in range(19)]
        for i in range(19):
            pr_lo[i, here, :] = row_of(p[i], 0)
            pr_hi[i, here, :] = row_of(p[i], N - 1)
        centre = pot[x]
        slopes = (pot[x + 1] - pot[x - 1], roll_y(centre, -1) - roll_y(centre, 1), roll_z(centre, -1) - roll_z(centre, 1))
        post, force = post_of(p, cond[x] > 0.0, conc[0, x] - conc[1, x], slopes)
        moved = []
        for i in range(19):
            v = post[i]
            if C[i][2]:
                v = roll_z(v, C[i][2])
            if C[i][1]:
                v = roll_y(v, C[i][1])
            buf[i, x + C[i][0]] = v
            moved.append(v)
        g = sums([(i, moved[i]) for i in range(19) if C[i][0] == 0], keep)
        mom[0, x] += g[0]
        for m in (1, 2, 3):
            w = jnp.where(keep[0], 0.5 * force[m - 1], 0.0)
            mom[m, x] += w if g[m] is None else g[m] + w
        g = sums([(i, moved[i]) for i in XPOS], keep)
        for m in range(4):
            mom[m, x + 1] = g[m]
        g = sums([(i, moved[i]) for i in XNEG], keep)
        for m in range(4):
            mom[m, x - 1] += g[m]
        return carry

    for s in range(N // CHUNK):
        chunks[s].wait()
        lax.fori_loop(max(CHUNK * s, 1), min(CHUNK * s + CHUNK, N - 1), step, 0)
    for c in ends:
        c.wait()


def edge_kernel(px_lo, px_hi, pr_lo, pr_hi, gx_lo, gx_hi, gy_lo, gy_hi, fx_lo, fx_hi, fy_lo, fy_hi, pot, mom0,
                mom, ex_lo, ex_hi, ey_lo, ey_hi, yb_lo, yb_hi):
    row = rows()
    inner = (row >= 1) & (row <= N - 2)
    keep = {0: None, 1: row >= 1, -1: row <= N - 2}
    lines = {}
    for pr, gy, fy, ey, low in ((pr_lo, gy_lo, fy_lo, ey_lo, True), (pr_hi, gy_hi, fy_hi, ey_hi, False)):
        centre = gy[0]
        y_slope = gy[1] - fy[0] if low else fy[0] - gy[1]
        slopes = (roll_y(centre, -1) - roll_y(centre, 1), y_slope, roll_z(centre, -1) - roll_z(centre, 1))
        post, force = post_of([pr[i] for i in range(19)], gy[RING + 2] > 0.0, gy[RING] - gy[RING + 1], slopes)
        for i in range(19):
            v = roll_z(post[i], C[i][2]) if C[i][2] else post[i]
            v = jnp.where(inner, v, 0.0)
            ey[i] = v
            if low and C[i][1] == -1:
                q = YNEG.index(i)
                yb_lo[q * N:(q + 1) * N, :] = v
            if not low and C[i][1] == 1:
                q = YPOS.index(i)
                yb_hi[q * N:(q + 1) * N, :] = v
            post[i] = shift_by(v, C[i][0])
        for cy in (0, 1 if low else -1):
            y = (0 if low else N - 1) + cy
            total = [None] * 4
            for i in range(19):
                if C[i][1] == cy:
                    for m, c in enumerate((1,) + C[i]):
                        if c:
                            w = post[i] if c == 1 else -post[i]
                            total[m] = w if total[m] is None else total[m] + w
            if cy == 0:
                for a in range(3):
                    w = jnp.where(inner, 0.5 * force[a], 0.0)
                    total[a + 1] = w if total[a + 1] is None else total[a + 1] + w
            lines[y] = total
    for x in range(N):
        for m in range(4):
            v = mom0[m, x]
            for y in (0, 1, N - 2, N - 1):
                v = v + jnp.where(row == y, spread(row_of(lines[y][m], x)), 0.0)
            mom[m, x] = v
    for px, gx, fx, ex, low in ((px_lo, gx_lo, fx_lo, ex_lo, True), (px_hi, gx_hi, fx_hi, ex_hi, False)):
        at = 0 if low else N - 1
        centre = gx[0]
        x_slope = pot[1] - fx[0] if low else fx[0] - pot[N - 2]
        y_up = jnp.where(row == N - 1, spread(fy_hi[0, at:at + 1, :]), roll_y(centre, -1))
        y_dn = jnp.where(row == 0, spread(fy_lo[0, at:at + 1, :]), roll_y(centre, 1))
        slopes = (x_slope, y_up - y_dn, roll_z(centre, -1) - roll_z(centre, 1))
        post, force = post_of([px[i] for i in range(19)], gx[3] > 0.0, gx[1] - gx[2], slopes)
        for i in range(19):
            v = roll_z(post[i], C[i][2]) if C[i][2] else post[i]
            if C[i][1] == 1:
                v = roll_y(v, 1)
                at_row = YPOS.index(i) * N + at
                yb_hi[at_row:at_row + 1, :] = row_of(v, 0)
                v = jnp.where(row == 0, 0.0, v)
            elif C[i][1] == -1:
                v = roll_y(v, -1)
                at_row = YNEG.index(i) * N + at
                yb_lo[at_row:at_row + 1, :] = row_of(v, N - 1)
                v = jnp.where(row == N - 1, 0.0, v)
            ex[i] = v
            post[i] = v
        none = {0: None, 1: None, -1: None}
        g = sums([(i, post[i]) for i in range(19) if C[i][0] == 0], none)
        mom[0, at] += g[0]
        for m in (1, 2, 3):
            w = 0.5 * force[m - 1]
            mom[m, at] += w if g[m] is None else g[m] + w
        g = sums([(i, post[i]) for i in (XPOS if low else XNEG)], none)
        for m in range(4):
            mom[m, 1 if low else N - 2] += g[m]
        g = sums([(i, post[i]) for i in (XNEG if low else XPOS)], none)
        k = LINE + (2 if low else 0)
        yb_hi[k:k + 1, :] = row_of(g[0], N - 1)
        yb_hi[k + 1:k + 2, :] = row_of(g[2], N - 1)
        yb_lo[k:k + 1, :] = row_of(g[0], 0)
        yb_lo[k + 1:k + 2, :] = row_of(g[2], 0)
    for x in range(N):
        for q, m in ((5, 0), (6, 2)):
            yb_lo[q * N + x:q * N + x + 1, :] = mom[m, x, 0:1, :]
            yb_hi[q * N + x:q * N + x + 1, :] = mom[m, x, N - 1:N, :]
    yb_lo[LINE + 4:, :] = jnp.zeros((4, Z), F32)
    yb_hi[LINE + 4:, :] = jnp.zeros((4, Z), F32)


def plane(ref, q):
    return ref[q * N:(q + 1) * N, :]


def line(ref, q, x):
    return ref[q * N + x:q * N + x + 1, :]


def y_terms(lo, hi):
    s3, s7, s10, s15, s17 = (plane(lo, q) for q in range(5))
    s7, s10 = shift_up(s7), shift_down(s10)
    total = s3 + s7 + s10 + s15 + s17
    below = (total, s7 - s10, total, s15 - s17)
    s4, s8, s9, s16, s18 = (plane(hi, q) for q in range(5))
    s8, s9 = shift_down(s8), shift_up(s9)
    total = s4 + s8 + s9 + s16 + s18
    return below, (total, s9 - s8, -total, s18 - s16)


def corner_kernel(ex_lo, ex_hi, yh_lo, yh_hi, yb_lo, yb_hi, mom, xb_lo, xb_hi):
    row = rows()
    below, above = y_terms(yh_lo, yh_hi)
    for ex, xb, slots, at in ((ex_hi, xb_hi, XPOS, N - 1), (ex_lo, xb_lo, XNEG, 0)):
        for q, i in enumerate(slots):
            v = ex[i]
            if C[i][1] == 1:
                v = jnp.where(row == 0, spread(line(yh_lo, YPOS.index(i), at)), v)
            elif C[i][1] == -1:
                v = jnp.where(row == N - 1, spread(line(yh_hi, YNEG.index(i), at)), v)
            xb[q * N:(q + 1) * N, :] = v
        for q, m in ((5, 0), (6, 1)):
            v = mom[m, at] + jnp.where(row == 0, spread(row_of(below[m], at)), 0.0)
            xb[q * N:(q + 1) * N, :] = v + jnp.where(row == N - 1, spread(row_of(above[m], at)), 0.0)
        c = 1 if at else -1
        k = LINE if at else LINE + 2
        down = line(yb_lo, YNEG.index(9 if c == 1 else 8), at)
        up = line(yb_hi, YPOS.index(7 if c == 1 else 10), at)
        xb[LINE:LINE + 1, :] = yh_lo[k:k + 1, :] + down
        xb[LINE + 1:LINE + 2, :] = yh_lo[k + 1:k + 2, :] - down
        xb[LINE + 2:LINE + 3, :] = yh_hi[k:k + 1, :] + up
        xb[LINE + 3:LINE + 4, :] = yh_hi[k + 1:k + 2, :] + up
        xb[LINE + 4:, :] = jnp.zeros((4, Z), F32)


def pack_pot_kernel(pot, fy_lo, fy_hi, o_hi, o_lo):
    for k in range(RING):
        o_hi[k * N:(k + 1) * N, :] = pot[N - 1 - k]
        o_lo[k * N:(k + 1) * N, :] = pot[k]
    for at, a, side, b in POT_ROWS:
        halo = fy_hi if side else fy_lo
        o_hi[at:at + 1, :] = halo[b - 1, N - a:N - a + 1, :]
        o_lo[at:at + 1, :] = halo[b - 1, a - 1:a, :]
    end = POT_ROWS[-1][0] + 1
    o_hi[end:, :] = jnp.zeros((POT_LEN - end, Z), F32)
    o_lo[end:, :] = jnp.zeros((POT_LEN - end, Z), F32)


def transport_kernel(charge, classes_h, mom, cond, conc, pot, yh_lo, yh_hi, xh_lo, xh_hi, yb_lo, yb_hi, xb_lo, xb_hi,
                     fx_lo, fx_hi, fy_lo, fy_hi, gy_lo, conc_out, src, sy_lo, sy_hi,
                     drift, lines, low, dy_hi, own_dy, classes, sem):
    fetch = pltpu.make_async_copy(classes_h, classes, sem)
    fetch.start()
    row = rows()
    below, above = y_terms(yh_lo, yh_hi)
    for m in range(4):
        lines[m] = below[m]
        lines[4 + m] = above[m]

    def step(x, extra):
        here = pl.ds(x, 1)

        def full(m):
            v = mom[m, x]
            if extra is not None:
                v = v + extra[m]
            v = v + jnp.where(row == 0, spread(lines[m, here, :]), 0.0)
            return v + jnp.where(row == N - 1, spread(lines[4 + m, here, :]), 0.0)

        scale = jnp.where(cond[x] > 0.0, 1.0 / full(0), 0.0)
        drift[0, x] = full(1) * scale
        v = full(2) * scale
        drift[1, x] = v
        drift[2, x] = full(3) * scale
        own_dy[here, :] = row_of(v, 0)

    a = [plane(xh_lo, q) for q in range(5)]
    total = a[0] + a[1] + a[2] + a[3] + a[4]
    step(0, (total, total, a[1] - a[2], a[3] - a[4]))
    b = [plane(xh_hi, q) for q in range(5)]
    total = b[0] + b[1] + b[2] + b[3] + b[4]
    step(N - 1, (total, -total, b[2] - b[1], b[4] - b[3]))

    def loop(x, carry):
        step(x, None)
        return carry

    lax.fori_loop(1, N - 1, loop, 0, unroll=2)

    def velocity(conductance, density, momentum):
        return jnp.where(conductance > 0.0, momentum / density, 0.0)

    def x_face(fx, xh, xb, sign):
        out = plane(xb, 0) + plane(xb, 1) + plane(xb, 2) + plane(xb, 3) + plane(xb, 4)
        d = velocity(fx[3], plane(xh, 5) + out, plane(xh, 6) + sign * out)
        return (fx[1], fx[2], fx[3], fx[0], d)

    from_hi, from_lo = y_terms(yb_hi, yb_lo)

    def y_face(fy, yh, terms, k):
        density = plane(yh, 5) + terms[0]
        momentum = plane(yh, 6) + terms[2]
        for xh, x in ((xh_lo, 0), (xh_hi, N - 1)):
            density = density + jnp.where(row == x, spread(xh[k:k + 1, :]), 0.0)
            momentum = momentum + jnp.where(row == x, spread(xh[k + 1:k + 2, :]), 0.0)
        d = velocity(fy[RING + 2], density, momentum)
        return (fy[RING], fy[RING + 1], fy[RING + 2], fy[0], d)

    left = y_face(fy_lo, yh_lo, from_lo, LINE)
    first = flux(left, (gy_lo[RING], gy_lo[RING + 1], gy_lo[RING + 2], gy_lo[0], own_dy[...]))
    low[0] = first[0]
    low[1] = first[1]
    dy_hi[...] = y_face(fy_hi, yh_hi, from_hi, LINE + 2)[4]
    fetch.wait()

    def fields(x, d):
        return (conc[0, x], conc[1, x], cond[x], pot[x], drift[d, x])

    def one(x, behind, ahead):
        here = pl.ds(x, 1)
        me = fields(x, 0)
        fx = flux(me, ahead)
        tot = [fx[s] - behind[s] for s in range(2)]
        mine = me[:4] + (drift[1, x],)
        halo = (fy_hi[RING, here, :], fy_hi[RING + 1, here, :], fy_hi[RING + 2, here, :], fy_hi[0, here, :], dy_hi[here, :])
        nxt = tuple(jnp.where(row == N - 1, spread(halo[q]), roll_y(mine[q], -1)) for q in range(5))
        fy = flux(mine, nxt)
        for s in range(2):
            before = jnp.where(row == 0, spread(low[s, here, :]), roll_y(fy[s], 1))
            tot[s] = tot[s] + (fy[s] - before)
        mine = me[:4] + (drift[2, x],)
        fz = flux(mine, tuple(roll_z(v, -1) for v in mine))
        for s in range(2):
            tot[s] = tot[s] + (fz[s] - roll_z(fz[s], 1))
        c0 = me[0] - tot[0]
        c1 = me[1] - tot[1]
        conc_out[0, x] = c0
        conc_out[1, x] = c1
        cls = classes[x]
        wall = jnp.zeros((N, Z), F32)
        for q in range(4):
            wall = wall + jnp.where(cls == q, charge[q], 0.0)
        s_val = jnp.where(me[2] > 0.0, c0 - c1, wall)
        src[x] = s_val
        for r in range(RING - 1):
            sy_lo[r, here, :] = row_of(s_val, r)
            sy_hi[r, here, :] = row_of(s_val, N - 1 - r)
        return tuple(fx)

    carry = tuple(flux(x_face(fx_lo, xh_lo, xb_lo, -1.0), fields(0, 0)))
    carry = lax.fori_loop(0, N - 1, lambda x, c: one(x, c, fields(x + 1, 0)), carry)
    one(N - 1, carry, x_face(fx_hi, xh_hi, xb_hi, 1.0))


def sweep_kernel(pot, src, fy_lo, fy_hi, xa_lo, xa_hi, ys_lo, ys_hi, xs_lo, xs_hi, out, ext, even, odd, s_even, s_odd):
    mid = slice(OFF, OFF + N)
    top = RING + N
    half = (N + 2 * RING) // 2
    shape = (N + 2 * OFF, Z)
    mask = (lax.broadcasted_iota(jnp.int32, shape, 0) + lax.broadcasted_iota(jnp.int32, shape, 1)) % 2 == 0

    def fill(centre, y_lo, y_hi, x_lo, x_hi, depth, listed):
        def own(x, carry):
            here = pl.ds(x, 1)
            ext[RING + x, mid] = centre[x]
            for r in range(depth):
                ext[RING + x, OFF - 1 - r:OFF - r, :] = y_lo[r, here, :]
                ext[RING + x, OFF + N + r:OFF + N + r + 1, :] = y_hi[r, here, :]
            return carry

        lax.fori_loop(0, N, own, 0, unroll=2)
        for r in range(depth):
            ext[RING - 1 - r, mid] = x_lo[r * N:(r + 1) * N, :]
            ext[top + r, mid] = x_hi[r * N:(r + 1) * N, :]
        for at, a, side, b in listed:
            y = OFF + N + b - 1 if side else OFF - b
            ext[RING - a, y:y + 1, :] = x_lo[at:at + 1, :]
            ext[top + a - 1, y:y + 1, :] = x_hi[at:at + 1, :]

    def split(a, b):
        def pack(k, carry):
            p, q = ext[2 * k], ext[2 * k + 1]
            a[k + 1] = jnp.where(mask, p, q)
            b[k + 1] = jnp.where(mask, q, p)
            return carry

        lax.fori_loop(0, half, pack, 0, unroll=2)

    zero = jnp.zeros(shape, F32)
    for ref in (even, odd):
        ref[0] = zero
        ref[half + 1] = zero
    fill(pot, fy_lo, fy_hi, xa_lo, xa_hi, RING, POT_ROWS)
    split(even, odd)
    fill(src, ys_lo, ys_hi, xs_lo, xs_hi, RING - 1, SRC_ROWS)
    split(s_even, s_odd)
    for h in range(6):
        this, other, s = (even, odd, s_even) if h % 2 == 0 else (odd, even, s_odd)

        def update(k, carry, h=h, this=this, other=other, s=s):
            c = other[k]
            before, after = other[k - 1], other[k + 1]
            far = jnp.where(mask, before, after) if h % 2 == 0 else jnp.where(mask, after, before)
            nb = (c + far) + (roll_y(c, 1) + roll_y(c, -1)) + (roll_z(c, 1) + roll_z(c, -1))
            this[k] = -0.6 * this[k] + (1.6 / 6.0) * (nb + s[k])
            return carry

        lo = (h + 1) // 2
        lax.fori_loop(lo + 1, half - lo + 1, update, 0, unroll=2)

    def last(k, carry):
        p, q = even[k], odd[k]
        out[2 * (k - 1) - RING] = jnp.where(mask, p, q)[OFF:OFF + N]
        out[2 * (k - 1) - RING + 1] = jnp.where(mask, q, p)[OFF:OFF + N]
        return carry

    lax.fori_loop(RING // 2 + 1, RING // 2 + N // 2 + 1, last, 0)


def patch_kernel(buf, ex_lo, ex_hi, ey_lo, ey_hi, yh_lo, yh_hi, xh_lo, xh_hi, out, done, sems):
    row = rows()
    copies = []
    for i in range(19):
        cx, cy, _ = C[i]

        def halo(v, src, i=i, cy=cy):
            if cy == 1:
                return jnp.where(row == 0, spread(yh_lo[pl.ds(YPOS.index(i) * N + src, 1), :]), v)
            if cy == -1:
                return jnp.where(row == N - 1, spread(yh_hi[pl.ds(YNEG.index(i) * N + src, 1), :]), v)
            return v

        def inner(src, carry, i=i, cx=cx, cy=cy, halo=halo):
            here = pl.ds(src, 1)
            v = buf[i, src + cx]
            if cy != -1:
                v = jnp.where(row == cy, spread(ey_lo[i, here, :]), v)
            if cy != 1:
                v = jnp.where(row == N - 1 + cy, spread(ey_hi[i, here, :]), v)
            done[i, src + cx] = halo(v, src)
            return carry

        lax.fori_loop(1, N - 1, inner, 0, unroll=2)
        if cx != -1:
            done[i, cx] = halo(ex_lo[i], 0)
        if cx != 1:
            done[i, N - 1 + cx] = halo(ex_hi[i], N - 1)
        if cx == 1:
            done[i, 0] = plane(xh_lo, XPOS.index(i))
        if cx == -1:
            done[i, N - 1] = plane(xh_hi, XNEG.index(i))
        copy = pltpu.make_async_copy(done.at[i], out.at[i], sems.at[i])
        copy.start()
        copies.append(copy)
    for copy in copies:
        copy.wait()


def flux(a, b):
    link = a[2] * b[2]
    carried = 0.5 * (a[4] + b[4])
    drop = a[3] - b[3]
    got = []
    for s in range(2):
        mean = 0.5 * (a[s] + b[s])
        got.append(link * (RATES[s] * ((a[s] - b[s]) + (VAL[s] * mean) * drop) + mean * carried))
    return got


def ring_rows(depth, total):
    listed = []
    at = depth
    for a in range(1, total):
        for side in (0, 1):
            for b in range(1, total - a + 1):
                listed.append((at, a, side, b))
                at += 1
    return listed


POT_ROWS = ring_rows(RING * N, RING)
SRC_ROWS = ring_rows((RING - 1) * N, RING - 1)
POT_LEN = 128
SRC_LEN = 104


def pack_src_kernel(src, ys_lo, ys_hi, o_hi, o_lo):
    for k in range(RING - 1):
        o_hi[k * N:(k + 1) * N, :] = src[N - 1 - k]
        o_lo[k * N:(k + 1) * N, :] = src[k]
    for at, a, side, b in SRC_ROWS:
        halo = ys_hi if side else ys_lo
        o_hi[at:at + 1, :] = halo[b - 1, N - a:N - a + 1, :]
        o_lo[at:at + 1, :] = halo[b - 1, a - 1:a, :]
    end = SRC_ROWS[-1][0] + 1
    o_hi[end:, :] = jnp.zeros((SRC_LEN - end, Z), F32)
    o_lo[end:, :] = jnp.zeros((SRC_LEN - end, Z), F32)


def swap(axis, hi, lo):
    n = lax.axis_size(axis)
    up = [(i, (i + 1) % n) for i in range(n)]
    down = [(b, a) for a, b in up]
    return lax.ppermute(hi, axis, up), lax.ppermute(lo, axis, down)


def body(pops, conc, pot, mob, solid, classes, charge):
    cube = sds(N, N, Z)
    msg = sds(ROWS, Z)
    gx_hi, gx_lo, gy_hi, gy_lo, pot, conc, cond = call(
        faces_kernel, [sds(4, N, Z)] * 2 + [sds(RING + 3, N, Z)] * 2 + [cube, sds(2, N, N, Z), cube], "faces", "hhhh",
        scratch=[VM((N, N, Z), F32), VM((N, N, Z), jnp.int32), pltpu.SemaphoreType.DMA((4,))], moved=2600000)(
        pot, conc, mob, solid)
    fx_lo, fx_hi = swap("gx", gx_hi, gx_lo)
    fy_lo, fy_hi = swap("gy", gy_hi, gy_lo)
    chunks = N // CHUNK
    buf, mom, px_lo, px_hi, pr_lo, pr_hi = call(
        collide_kernel, [sds(19, N, N, Z), sds(4, N, N, Z)] + [sds(19, N, Z)] * 4, "collide", "hvvv",
        scratch=[VM((19, N, N, Z), F32), pltpu.SemaphoreType.DMA((chunks,)), pltpu.SemaphoreType.DMA((2,))],
        mib=24, flops=20000000, moved=14000000)(pops, pot, conc, cond)
    mom, ex_lo, ex_hi, ey_lo, ey_hi, yb_lo, yb_hi = call(
        edge_kernel, [sds(4, N, N, Z)] + [sds(19, N, Z)] * 4 + [msg, msg], "edge", "v" * 14, moved=3000000)(
        px_lo, px_hi, pr_lo, pr_hi, gx_lo, gx_hi, gy_lo, gy_hi, fx_lo, fx_hi, fy_lo, fy_hi, pot, mom)
    yh_lo, yh_hi = swap("gy", yb_hi, yb_lo)
    xb_lo, xb_hi = call(corner_kernel, [msg, msg], "corner", "v" * 7)(ex_lo, ex_hi, yh_lo, yh_hi, yb_lo, yb_hi, mom)
    xh_lo, xh_hi = swap("gx", xb_hi, xb_lo)
    fy_lo2, fy_hi2, _, _ = lax.optimization_barrier((fy_lo, fy_hi, yh_lo, yh_hi))
    bx_hi, bx_lo = call(pack_pot_kernel, [sds(POT_LEN, Z)] * 2, "pack_pot", "vvv")(pot, fy_lo2, fy_hi2)
    xa_lo, xa_hi = swap("gx", bx_hi, bx_lo)
    face = VM((N, Z), F32)
    conc_out, src, sy_lo, sy_hi = call(
        transport_kernel, [sds(2, N, N, Z), cube, sds(RING - 1, N, Z), sds(RING - 1, N, Z)], "transport", "sh" + "v" * 17,
        scratch=[VM((3, N, N, Z), F32), VM((8, N, Z), F32), VM((2, N, Z), F32), face, face, VM((N, N, Z), jnp.int32),
                 pltpu.SemaphoreType.DMA], flops=10000000, moved=8000000)(
        charge, classes, mom, cond, conc, pot, yh_lo, yh_hi, xh_lo, xh_hi, yb_lo, yb_hi, xb_lo, xb_hi,
        fx_lo, fx_hi, fy_lo, fy_hi, gy_lo)
    ys_lo, ys_hi = swap("gy", sy_hi, sy_lo)
    bs_hi, bs_lo = call(pack_src_kernel, [sds(SRC_LEN, Z)] * 2, "pack_src", "vvv")(src, ys_lo, ys_hi)
    xs_lo, xs_hi = swap("gx", bs_hi, bs_lo)
    packed = VM(((N + 2 * RING) // 2 + 2, N + 2 * OFF, Z), F32)
    potential_out = call(
        sweep_kernel, [cube], "sweep", "v" * 10,
        scratch=[VM((N + 2 * RING, N + 2 * OFF, Z), F32)] + [packed] * 4, flops=20000000, moved=4000000)(
        pot, src, fy_lo, fy_hi, xa_lo, xa_hi, ys_lo, ys_hi, xs_lo, xs_hi)[0]
    pop = call(
        patch_kernel, [sds(19, N, N, Z)], "patch", "v" * 9, out_specs="h",
        scratch=[VM((19, N, N, Z), F32), pltpu.SemaphoreType.DMA((19,))], mib=16, moved=10000000)(
        buf, ex_lo, ex_hi, ey_lo, ey_hi, yh_lo, yh_hi, xh_lo, xh_hi)[0]
    return (pop, conc_out, potential_out)


def solution(mesh):
    lattice = P(None, "gx", "gy", None)
    flat = P("gx", "gy", None)
    return jax.shard_map(
        body, mesh=mesh, in_specs=(lattice, lattice, flat, flat, flat, flat, P()),
        out_specs=(lattice, lattice, flat), check_vma=False)
```

profile of v0, /device:TPU:112, one launch (start us, length us, event | category | flops | bytes accessed | tf_op | source)
XLA Modules:
  0.0 66.6 jit_solution(13826707948941484858)
XLA Ops:
  0.6 1.0 %copy-done.1 = f32[2,16,16,256]{3,2,1,0:T(8,128)S(1)} copy-done((f32[2,16,16,256]{3,2,1,0:T(8,128)S(1)}, f32[2,16,16,256]{3,2,1,0:T(8,128)}, u32[]{:S(2)}) %copy-start.1) | copy-done | bytes 524312
  1.7 0.9 %copy-done.2 = f32[16,16,256]{2,1,0:T(8,128)S(1)} copy-done((f32[16,16,256]{2,1,0:T(8,128)S(1)}, f32[16,16,256]{2,1,0:T(8,128)}, u32[]{:S(2)}) %copy-start.2) | copy-done | bytes 262168
  2.6 0.9 %copy-done.3 = f32[16,16,256]{2,1,0:T(8,128)S(1)} copy-done((f32[16,16,256]{2,1,0:T(8,128)S(1)}, f32[16,16,256]{2,1,0:T(8,128)}, u32[]{:S(2)}) %copy-start.3) | copy-done | bytes 262168
  3.6 0.9 %copy-done.4 = s32[16,16,256]{2,1,0:T(8,128)S(1)} copy-done((s32[16,16,256]{2,1,0:T(8,128)S(1)}, s32[16,16,256]{2,1,0:T(8,128)}, u32[]{:S(2)}) %copy-start.4) | copy-done | bytes 262168
  4.5 0.4 faces.1
  5.0 3.0 %collective-permute-start.3 = (f32[9,16,256]{2,1,0:T(8,128)S(1)}, f32[9,16,256]{2,1,0:T(8,128)S(1)}, u32[]{:S(2)}, u32[]{:S(2)}) collective-permute-start(f32[9,16,256]{2,1,0:T(8,128)S(1)} %get-tuple-element.45.gy_lo), channel_id=1, source_target_pairs={{1,0},{2,1},{3,2},{4,3},{5,4},{6,5},{7,6},{8,7},{9,8},{10,9},{11,1... | collective-permute-start | bytes 442376 | tf_op jit(solution)/shard_map/ppermute | solution.py:616
  7.9 0.0 collective-permute-start.2
  8.0 3.2 %collective-permute-start = (f32[4,16,256]{2,1,0:T(8,128)S(1)}, f32[4,16,256]{2,1,0:T(8,128)S(1)}, u32[]{:S(2)}, u32[]{:S(2)}) collective-permute-start(f32[4,16,256]{2,1,0:T(8,128)S(1)} %get-tuple-element.44.gx_hi), channel_id=1, source_target_pairs={{0,16},{16,32},{32,48},{48,64},{64,80},{80,96},{96,112},{112,128},... | collective-permute-start | bytes 196616 | tf_op jit(solution)/shard_map/ppermute | solution.py:616
  11.1 0.3 collective-permute-start.1
  11.5 2.4 %copy-done = f32[19,16,16,256]{3,2,1,0:T(8,128)S(1)} copy-done((f32[19,16,16,256]{3,2,1,0:T(8,128)S(1)}, f32[19,16,16,256]{3,2,1,0:T(8,128)}, u32[]{:S(2)}) %copy-start) | copy-done | bytes 4980760
  13.9 3.6 %collide.1 = (f32[19,16,16,256]{3,2,1,0:T(8,128)S(1)}, f32[4,16,16,256]{3,2,1,0:T(8,128)S(1)}, f32[19,16,256]{2,1,0:T(8,128)S(1)}, f32[19,16,256]{2,1,0:T(8,128)...) custom-call(f32[19,16,16,256]{3,2,1,0:T(8,128)S(1)} %copy-done, f32[16,16,256]{2,1,0:T(8,128)S(1)} %get-tuple-element.35.pot, ...), custom_call_target="tpu_custom_call" | custom-call | flops 20000000 | bytes 14000000 | tf_op jit(solution)/shard_map/collide/pallas_call | solution.py:629
  17.5 1.5 %collective-permute-done.1.fx_hi = f32[4,16,256]{2,1,0:T(8,128)S(1)} collective-permute-done((f32[4,16,256]{2,1,0:T(8,128)S(1)}, f32[4,16,256]{2,1,0:T(8,128)S(1)}, u32[]{:S(2)}, u32[]{:S(2)}) %collective-permute-start.1) | collective-permute-done | bytes 65568 | tf_op jit(solution)/shard_map/ppermute | solution.py:616
  19.0 0.0 collective-permute-done.3.fy_hi
  19.0 1.0 %edge.1 = (f32[4,16,16,256]{3,2,1,0:T(8,128)S(1)}, f32[19,16,256]{2,1,0:T(8,128)S(1)}, f32[19,16,256]{2,1,0:T(8,128)S(1)}, f32[19,16,256]{2,1,0:T(8,128)S(1)}, f...) custom-call(f32[19,16,256]{2,1,0:T(8,128)S(1)} %get-tuple-element.39.px_lo, ...), custom_call_target="tpu_custom_call" | custom-call | bytes 3000000 | tf_op jit(solution)/shard_map/edge/pallas_call | solution.py:633
  20.0 0.1 collective-permute-start.4
  20.1 3.8 %collective-permute-start.5 = (f32[120,256]{1,0:T(8,128)S(1)}, f32[120,256]{1,0:T(8,128)S(1)}, u32[]{:S(2)}, u32[]{:S(2)}) collective-permute-start(f32[120,256]{1,0:T(8,128)S(1)} %get-tuple-element.53.yb_lo), channel_id=1, source_target_pairs={{1,0},{2,1},{3,2},{4,3},{5,4},{6,5},{7,6},{8,7},{9,8},{10,9},{11,1... | collective-permute-start | bytes 368648 | tf_op jit(solution)/shard_map/ppermute | solution.py:616
  23.9 2.6 %collective-permute-done.4.yh_lo = f32[120,256]{1,0:T(8,128)S(1)} collective-permute-done((f32[120,256]{1,0:T(8,128)S(1)}, f32[120,256]{1,0:T(8,128)S(1)}, u32[]{:S(2)}, u32[]{:S(2)}) %collective-permute-start.4) | collective-permute-done | bytes 122912 | tf_op jit(solution)/shard_map/ppermute | solution.py:616
  26.5 3.9 %collective-permute-start.6 = (f32[120,256]{1,0:T(8,128)S(1)}, f32[120,256]{1,0:T(8,128)S(1)}, u32[]{:S(2)}, u32[]{:S(2)}) collective-permute-start(f32[120,256]{1,0:T(8,128)S(1)} %get-tuple-element.55.xb_hi), channel_id=1, source_target_pairs={{0,16},{16,32},{32,48},{48,64},{64,80},{80,96},{96,112},{112,128},... | collective-permute-start | bytes 368648 | tf_op jit(solution)/shard_map/ppermute | solution.py:616
  30.5 2.5 %collective-permute-done.6.xh_lo = f32[120,256]{1,0:T(8,128)S(1)} collective-permute-done((f32[120,256]{1,0:T(8,128)S(1)}, f32[120,256]{1,0:T(8,128)S(1)}, u32[]{:S(2)}, u32[]{:S(2)}) %collective-permute-start.6) | collective-permute-done | bytes 122912 | tf_op jit(solution)/shard_map/ppermute | solution.py:616
  33.0 6.0 %collective-permute-done.7.xh_hi = f32[120,256]{1,0:T(8,128)S(1)} collective-permute-done((f32[120,256]{1,0:T(8,128)S(1)}, f32[120,256]{1,0:T(8,128)S(1)}, u32[]{:S(2)}, u32[]{:S(2)}) %collective-permute-start.7) | collective-permute-done | bytes 122912 | tf_op jit(solution)/shard_map/ppermute | solution.py:616
  39.0 4.5 %transport.1 = (f32[2,16,16,256]{3,2,1,0:T(8,128)}, f32[16,16,256]{2,1,0:T(8,128)S(1)}, f32[5,16,256]{2,1,0:T(8,128)S(1)}, f32[5,16,256]{2,1,0:T(8,128)S(1)}) custom-call(f32[4]{0:T(128)S(1)} %copy-done.6, s32[16,16,256]{2,1,0:T(8,128)S(1)} %copy-done.5, f32[4,16,16,256]{3,2,1,0:T(8,128)S(1)} %get-tuple-element.54.mom, ...), custom_call_target="tpu_custom_call" | custom-call | flops 10000000 | bytes 8000000 | tf_op jit(solution)/shard_map/transport/pallas_call | solution.py:643
  43.5 0.1 collective-permute-start.10
  43.6 3.8 %collective-permute-start.11 = (f32[5,16,256]{2,1,0:T(8,128)S(1)}, f32[5,16,256]{2,1,0:T(8,128)S(1)}, u32[]{:S(2)}, u32[]{:S(2)}) collective-permute-start(f32[5,16,256]{2,1,0:T(8,128)S(1)} %get-tuple-element.64), channel_id=1, source_target_pairs={{1,0},{2,1},{3,2},{4,3},{5,4},{6,5},{7,6},{8,7},{9,8},{10,9},{11,1... | collective-permute-start | bytes 245768 | tf_op jit(solution)/shard_map/ppermute | solution.py:616
  47.5 0.1 collective-permute-start.8
  47.6 3.5 %collective-permute-start.9 = (f32[128,256]{1,0:T(8,128)S(1)}, f32[128,256]{1,0:T(8,128)S(1)}, u32[]{:S(2)}, u32[]{:S(2)}) collective-permute-start(f32[128,256]{1,0:T(8,128)S(1)} %get-tuple-element.62), channel_id=1, source_target_pairs={{16,0},{32,16},{48,32},{64,48},{80,64},{96,80},{112,96},{128,112},... | collective-permute-start | bytes 393224 | tf_op jit(solution)/shard_map/ppermute | solution.py:616
  51.1 0.0 collective-permute-done.10.ys_lo
  51.1 2.3 %collective-permute-start.12 = (f32[104,256]{1,0:T(8,128)S(1)}, f32[104,256]{1,0:T(8,128)S(1)}, u32[]{:S(2)}, u32[]{:S(2)}) collective-permute-start(f32[104,256]{1,0:T(8,128)S(1)} %get-tuple-element.65), channel_id=1, source_target_pairs={{0,16},{16,32},{32,48},{48,64},{64,80},{80,96},{96,112},{112,128},... | collective-permute-start | bytes 319496 | tf_op jit(solution)/shard_map/ppermute | solution.py:616
  53.4 1.3 %collective-permute-start.13 = (f32[104,256]{1,0:T(8,128)S(1)}, f32[104,256]{1,0:T(8,128)S(1)}, u32[]{:S(2)}, u32[]{:S(2)}) collective-permute-start(f32[104,256]{1,0:T(8,128)S(1)} %get-tuple-element.66), channel_id=1, source_target_pairs={{16,0},{32,16},{48,32},{64,48},{80,64},{96,80},{112,96},{128,112},... | collective-permute-start | bytes 319496 | tf_op jit(solution)/shard_map/ppermute | solution.py:616
  54.7 2.5 %patch.1 = f32[19,16,16,256]{3,2,1,0:T(8,128)} custom-call(f32[19,16,16,256]{3,2,1,0:T(8,128)S(1)} %get-tuple-element.38.buf, f32[19,16,256]{2,1,0:T(8,128)S(1)} %get-tuple-element.48.ex_lo, f32[19,16,256]{2,1,0:T(8,128)S(1)} %get-tuple-element.49.ex_hi, f32[19,16,256]{2,1,0:T(8,128)S(1)} %get-tuple-element.50.ey_lo, ...), custom_call_target="tpu_custom_call" | custom-call | bytes 10000000 | tf_op jit(solution)/shard_map/patch/pallas_call | solution.py:657
  57.2 1.3 %collective-permute-done.12.xs_lo = f32[104,256]{1,0:T(8,128)S(1)} collective-permute-done((f32[104,256]{1,0:T(8,128)S(1)}, f32[104,256]{1,0:T(8,128)S(1)}, u32[]{:S(2)}, u32[]{:S(2)}) %collective-permute-start.12) | collective-permute-done | bytes 106528 | tf_op jit(solution)/shard_map/ppermute | solution.py:616
  58.5 3.2 %collective-permute-done.13.xs_hi = f32[104,256]{1,0:T(8,128)S(1)} collective-permute-done((f32[104,256]{1,0:T(8,128)S(1)}, f32[104,256]{1,0:T(8,128)S(1)}, u32[]{:S(2)}, u32[]{:S(2)}) %collective-permute-start.13) | collective-permute-done | bytes 106528 | tf_op jit(solution)/shard_map/ppermute | solution.py:616
  61.7 4.9 %sweep.1 = f32[16,16,256]{2,1,0:T(8,128)} custom-call(f32[16,16,256]{2,1,0:T(8,128)S(1)} %get-tuple-element.35.pot, f32[16,16,256]{2,1,0:T(8,128)S(1)} %get-tuple-element.58.src, f32[9,16,256]{2,1,0:T(8,128)S(1)} %collective-permute-done.2.fy_lo, f32[9,16,256]{2,1,0:T(8,128)S(1)} %collective-permute-done.3.fy_hi, ...), custom_call_target="tpu_custom_call" | custom-call | flops 20000000 | bytes 4000000 | tf_op jit(solution)/shard_map/sweep/pallas_call | solution.py:653
  (19 shorter events, 0.2 us)
Async XLA Ops:
  0.6 1.0 %copy-start.1 = (f32[2,16,16,256]{3,2,1,0:T(8,128)S(1)}, f32[2,16,16,256]{3,2,1,0:T(8,128)}, u32[]{:S(2)}) copy-start(f32[2,16,16,256]{3,2,1,0:T(8,128)} %conc_h.1) | copy-start | bytes 1572868
  1.7 0.9 %copy-start.2 = (f32[16,16,256]{2,1,0:T(8,128)S(1)}, f32[16,16,256]{2,1,0:T(8,128)}, u32[]{:S(2)}) copy-start(f32[16,16,256]{2,1,0:T(8,128)} %pot_h.1) | copy-start | bytes 786436
  2.6 0.9 %copy-start.3 = (f32[16,16,256]{2,1,0:T(8,128)S(1)}, f32[16,16,256]{2,1,0:T(8,128)}, u32[]{:S(2)}) copy-start(f32[16,16,256]{2,1,0:T(8,128)} %mob_h.1) | copy-start | bytes 786436
  3.6 0.9 %copy-start.4 = (s32[16,16,256]{2,1,0:T(8,128)S(1)}, s32[16,16,256]{2,1,0:T(8,128)}, u32[]{:S(2)}) copy-start(s32[16,16,256]{2,1,0:T(8,128)} %solid_h.1) | copy-start | bytes 786436
  5.0 14.1 %collective-permute-start.3 = (f32[9,16,256]{2,1,0:T(8,128)S(1)}, f32[9,16,256]{2,1,0:T(8,128)S(1)}, u32[]{:S(2)}, u32[]{:S(2)}) collective-permute-start(f32[9,16,256]{2,1,0:T(8,128)S(1)} %get-tuple-element.45.gy_lo), channel_id=1, source_target_pairs={{1,0},{2,1},{3,2},{4,3},{5,4},{6,5},{7,6},{8,7},{9,8},{10,9},{11,1... | collective-permute-start | bytes 442376 | tf_op jit(solution)/shard_map/ppermute | solution.py:616
  7.9 11.1 %collective-permute-start.2 = (f32[9,16,256]{2,1,0:T(8,128)S(1)}, f32[9,16,256]{2,1,0:T(8,128)S(1)}, u32[]{:S(2)}, u32[]{:S(2)}) collective-permute-start(f32[9,16,256]{2,1,0:T(8,128)S(1)} %get-tuple-element.46.gy_hi), channel_id=1, source_target_pairs={{0,1},{1,2},{2,3},{3,4},{4,5},{5,6},{6,7},{7,8},{8,9},{9,10},{10,1... | collective-permute-start | bytes 442376 | tf_op jit(solution)/shard_map/ppermute | solution.py:616
  8.0 9.5 %collective-permute-start = (f32[4,16,256]{2,1,0:T(8,128)S(1)}, f32[4,16,256]{2,1,0:T(8,128)S(1)}, u32[]{:S(2)}, u32[]{:S(2)}) collective-permute-start(f32[4,16,256]{2,1,0:T(8,128)S(1)} %get-tuple-element.44.gx_hi), channel_id=1, source_target_pairs={{0,16},{16,32},{32,48},{48,64},{64,80},{80,96},{96,112},{112,128},... | collective-permute-start | bytes 196616 | tf_op jit(solution)/shard_map/ppermute | solution.py:616
  11.1 7.9 %collective-permute-start.1 = (f32[4,16,256]{2,1,0:T(8,128)S(1)}, f32[4,16,256]{2,1,0:T(8,128)S(1)}, u32[]{:S(2)}, u32[]{:S(2)}) collective-permute-start(f32[4,16,256]{2,1,0:T(8,128)S(1)} %get-tuple-element.43.gx_lo), channel_id=1, source_target_pairs={{16,0},{32,16},{48,32},{64,48},{80,64},{96,80},{112,96},{128,112},... | collective-permute-start | bytes 196616 | tf_op jit(solution)/shard_map/ppermute | solution.py:616
  11.5 2.4 %copy-start = (f32[19,16,16,256]{3,2,1,0:T(8,128)S(1)}, f32[19,16,16,256]{3,2,1,0:T(8,128)}, u32[]{:S(2)}) copy-start(f32[19,16,16,256]{3,2,1,0:T(8,128)} %pops.1) | copy-start | bytes 14942212
  13.9 25.1 %copy-start.5 = (s32[16,16,256]{2,1,0:T(8,128)S(1)}, s32[16,16,256]{2,1,0:T(8,128)}, u32[]{:S(2)}) copy-start(s32[16,16,256]{2,1,0:T(8,128)} %classes_h.1) | copy-start | bytes 786436
  13.9 25.1 %copy-start.6 = (f32[4]{0:T(128)S(1)}, f32[4]{0:T(128)}, u32[]{:S(2)}) copy-start(f32[4]{0:T(128)} %charge.1) | copy-start | bytes 52
  20.0 6.5 %collective-permute-start.4 = (f32[120,256]{1,0:T(8,128)S(1)}, f32[120,256]{1,0:T(8,128)S(1)}, u32[]{:S(2)}, u32[]{:S(2)}) collective-permute-start(f32[120,256]{1,0:T(8,128)S(1)} %get-tuple-element.52.yb_hi), channel_id=1, source_target_pairs={{0,1},{1,2},{2,3},{3,4},{4,5},{5,6},{6,7},{7,8},{8,9},{9,10},{10,1... | collective-permute-start | bytes 368648 | tf_op jit(solution)/shard_map/ppermute | solution.py:616
  20.1 6.4 %collective-permute-start.5 = (f32[120,256]{1,0:T(8,128)S(1)}, f32[120,256]{1,0:T(8,128)S(1)}, u32[]{:S(2)}, u32[]{:S(2)}) collective-permute-start(f32[120,256]{1,0:T(8,128)S(1)} %get-tuple-element.53.yb_lo), channel_id=1, source_target_pairs={{1,0},{2,1},{3,2},{4,3},{5,4},{6,5},{7,6},{8,7},{9,8},{10,9},{11,1... | collective-permute-start | bytes 368648 | tf_op jit(solution)/shard_map/ppermute | solution.py:616
  26.5 6.5 %collective-permute-start.6 = (f32[120,256]{1,0:T(8,128)S(1)}, f32[120,256]{1,0:T(8,128)S(1)}, u32[]{:S(2)}, u32[]{:S(2)}) collective-permute-start(f32[120,256]{1,0:T(8,128)S(1)} %get-tuple-element.55.xb_hi), channel_id=1, source_target_pairs={{0,16},{16,32},{32,48},{48,64},{64,80},{80,96},{96,112},{112,128},... | collective-permute-start | bytes 368648 | tf_op jit(solution)/shard_map/ppermute | solution.py:616
  30.5 8.5 %collective-permute-start.7 = (f32[120,256]{1,0:T(8,128)S(1)}, f32[120,256]{1,0:T(8,128)S(1)}, u32[]{:S(2)}, u32[]{:S(2)}) collective-permute-start(f32[120,256]{1,0:T(8,128)S(1)} %get-tuple-element.56.xb_lo), channel_id=1, source_target_pairs={{16,0},{32,16},{48,32},{64,48},{80,64},{96,80},{112,96},{128,112},... | collective-permute-start | bytes 368648 | tf_op jit(solution)/shard_map/ppermute | solution.py:616
  43.5 7.6 %collective-permute-start.10 = (f32[5,16,256]{2,1,0:T(8,128)S(1)}, f32[5,16,256]{2,1,0:T(8,128)S(1)}, u32[]{:S(2)}, u32[]{:S(2)}) collective-permute-start(f32[5,16,256]{2,1,0:T(8,128)S(1)} %get-tuple-element.63), channel_id=1, source_target_pairs={{0,1},{1,2},{2,3},{3,4},{4,5},{5,6},{6,7},{7,8},{8,9},{9,10},{10,1... | collective-permute-start | bytes 245768 | tf_op jit(solution)/shard_map/ppermute | solution.py:616
  43.6 7.5 %collective-permute-start.11 = (f32[5,16,256]{2,1,0:T(8,128)S(1)}, f32[5,16,256]{2,1,0:T(8,128)S(1)}, u32[]{:S(2)}, u32[]{:S(2)}) collective-permute-start(f32[5,16,256]{2,1,0:T(8,128)S(1)} %get-tuple-element.64), channel_id=1, source_target_pairs={{1,0},{2,1},{3,2},{4,3},{5,4},{6,5},{7,6},{8,7},{9,8},{10,9},{11,1... | collective-permute-start | bytes 245768 | tf_op jit(solution)/shard_map/ppermute | solution.py:616
  47.5 9.7 %collective-permute-start.8 = (f32[128,256]{1,0:T(8,128)S(1)}, f32[128,256]{1,0:T(8,128)S(1)}, u32[]{:S(2)}, u32[]{:S(2)}) collective-permute-start(f32[128,256]{1,0:T(8,128)S(1)} %get-tuple-element.61), channel_id=1, source_target_pairs={{0,16},{16,32},{32,48},{48,64},{64,80},{80,96},{96,112},{112,128},... | collective-permute-start | bytes 393224 | tf_op jit(solution)/shard_map/ppermute | solution.py:616
  47.6 9.6 %collective-permute-start.9 = (f32[128,256]{1,0:T(8,128)S(1)}, f32[128,256]{1,0:T(8,128)S(1)}, u32[]{:S(2)}, u32[]{:S(2)}) collective-permute-start(f32[128,256]{1,0:T(8,128)S(1)} %get-tuple-element.62), channel_id=1, source_target_pairs={{16,0},{32,16},{48,32},{64,48},{80,64},{96,80},{112,96},{128,112},... | collective-permute-start | bytes 393224 | tf_op jit(solution)/shard_map/ppermute | solution.py:616
  51.1 7.4 %collective-permute-start.12 = (f32[104,256]{1,0:T(8,128)S(1)}, f32[104,256]{1,0:T(8,128)S(1)}, u32[]{:S(2)}, u32[]{:S(2)}) collective-permute-start(f32[104,256]{1,0:T(8,128)S(1)} %get-tuple-element.65), channel_id=1, source_target_pairs={{0,16},{16,32},{32,48},{48,64},{64,80},{80,96},{96,112},{112,128},... | collective-permute-start | bytes 319496 | tf_op jit(solution)/shard_map/ppermute | solution.py:616
  53.4 8.3 %collective-permute-start.13 = (f32[104,256]{1,0:T(8,128)S(1)}, f32[104,256]{1,0:T(8,128)S(1)}, u32[]{:S(2)}, u32[]{:S(2)}) collective-permute-start(f32[104,256]{1,0:T(8,128)S(1)} %get-tuple-element.66), channel_id=1, source_target_pairs={{16,0},{32,16},{48,32},{64,48},{80,64},{96,80},{112,96},{128,112},... | collective-permute-start | bytes 319496 | tf_op jit(solution)/shard_map/ppermute | solution.py:616
where the time goes:
time: 66.9 us; the launch traced here: 66.6 us
  starting transfers between devices  25.5 us (38%)
  waiting for transfers between devices  17.1 us (26%)
  Pallas kernels  16.9 us (25%)
  local copies, waits for them, and re-layouts  6.3 us (9%)
  between operations  0.75 us (1%)
    ppermute x14, starting transfers between devices, swap(): return (lax.ppermute(hi, axis, up), lax.ppermute(lo, axis, down))  25.5 us
    ppermute x14, waiting for transfers between devices, swap(): return (lax.ppermute(hi, axis, up), lax.ppermute(lo, axis, down))  17.1 us
    unnamed x14, local copies, waits for them, and re-layouts  6.3 us
    pallas_call x1, Pallas kernels, body(): call(sweep_kernel, [cube], 'sweep', 'v' * 10, scratch=[VM((N + 2 * RING,...  4.87 us
    pallas_call x1, Pallas kernels, body(): call(transport_kernel, [sds(2, N, N, Z), cube, sds(RING - 1, N, Z), sds(R...  4.52 us
    pallas_call x1, Pallas kernels, body(): call(collide_kernel, [sds(19, N, N, Z), sds(4, N, N, Z)] + [sds(19, N, Z)...  3.56 us
    pallas_call x1, Pallas kernels, body(): call(patch_kernel, [sds(19, N, N, Z)], 'patch', 'v' * 9, out_specs='h', s...  2.46 us
  transfers between devices with their start and end apart: 14, of which 6 were waited for; matrix products, arithmetic and copies ran while one was open for 0% of the time, Pallas kernels for 9%

commit v1 on v0

--- a/solution.py
+++ b/solution.py
@@ -79,7 +79,7 @@
     )
 
 
-def faces_kernel(pot_h, conc_h, mob_h, solid_h, gx_hi, gx_lo, gy_hi, gy_lo, pot, conc, cond, mob, solid, sems):
+def faces_kernel(pot_h, conc_h, mob_h, solid_h, gx_hi, gx_lo, gy_hi, gy_lo, cond, pot, conc, mob, solid, sems):
     pairs = ((pot_h, pot), (conc_h, conc), (mob_h, mob), (solid_h, solid))
     copies = [pltpu.make_async_copy(a, b, sems.at[q]) for q, (a, b) in enumerate(pairs)]
     for c in copies:
@@ -100,10 +100,11 @@
 
     lax.fori_loop(0, N, step, 0, unroll=2)
     for x, face in ((N - 1, gx_hi), (0, gx_lo)):
-        face[0] = pot[x]
-        face[1] = conc[0, x]
-        face[2] = conc[1, x]
-        face[3] = cond[x]
+        for r in range(RING):
+            face[r] = pot[abs(x - r)]
+        face[RING] = conc[0, x]
+        face[RING + 1] = conc[1, x]
+        face[RING + 2] = cond[x]
 
 
 def post_of(p, fluid, q, slopes):
@@ -162,12 +163,13 @@
     return total
 
 
-def collide_kernel(pops, pot, conc, cond, buf, mom, px_lo, px_hi, pr_lo, pr_hi, held, sems, psems):
+def collide_kernel(pops, pot_h, conc_h, cond, buf, mom, px_lo, px_hi, pr_lo, pr_hi, held, pot, conc, sems, psems):
     chunks = [pltpu.make_async_copy(pops.at[:, pl.ds(CHUNK * s, CHUNK)], held.at[:, pl.ds(CHUNK * s, CHUNK)], sems.at[s])
               for s in range(N // CHUNK)]
     ends = [pltpu.make_async_copy(pops.at[:, 0], px_lo, psems.at[0]),
             pltpu.make_async_copy(pops.at[:, N - 1], px_hi, psems.at[1])]
-    for c in chunks + ends:
+    fields = [pltpu.make_async_copy(pot_h, pot, psems.at[2]), pltpu.make_async_copy(conc_h, conc, psems.at[3])]
+    for c in fields + chunks + ends:
         c.start()
     row = rows()
     zero = jnp.zeros((N, Z), F32)
@@ -207,6 +209,8 @@
             mom[m, x - 1] += g[m]
         return carry
 
+    for c in fields:
+        c.wait()
     for s in range(N // CHUNK):
         chunks[s].wait()
         lax.fori_loop(max(CHUNK * s, 1), min(CHUNK * s + CHUNK, N - 1), step, 0)
@@ -214,7 +218,7 @@
         c.wait()
 
 
-def edge_kernel(px_lo, px_hi, pr_lo, pr_hi, gx_lo, gx_hi, gy_lo, gy_hi, fx_lo, fx_hi, fy_lo, fy_hi, pot, mom0,
+def edge_kernel(px_lo, px_hi, pr_lo, pr_hi, gx_lo, gx_hi, gy_lo, gy_hi, fx_lo, fx_hi, fy_lo, fy_hi, mom0,
                 mom, ex_lo, ex_hi, ey_lo, ey_hi, yb_lo, yb_hi):
     row = rows()
     inner = (row >= 1) & (row <= N - 2)
@@ -259,11 +263,11 @@
     for px, gx, fx, ex, low in ((px_lo, gx_lo, fx_lo, ex_lo, True), (px_hi, gx_hi, fx_hi, ex_hi, False)):
         at = 0 if low else N - 1
         centre = gx[0]
-        x_slope = pot[1] - fx[0] if low else fx[0] - pot[N - 2]
+        x_slope = gx[1] - fx[0] if low else fx[0] - gx[1]
         y_up = jnp.where(row == N - 1, spread(fy_hi[0, at:at + 1, :]), roll_y(centre, -1))
         y_dn = jnp.where(row == 0, spread(fy_lo[0, at:at + 1, :]), roll_y(centre, 1))
         slopes = (x_slope, y_up - y_dn, roll_z(centre, -1) - roll_z(centre, 1))
-        post, force = post_of([px[i] for i in range(19)], gx[3] > 0.0, gx[1] - gx[2], slopes)
+        post, force = post_of([px[i] for i in range(19)], gx[RING + 2] > 0.0, gx[RING] - gx[RING + 1], slopes)
         for i in range(19):
             v = roll_z(post[i], C[i][2]) if C[i][2] else post[i]
             if C[i][1] == 1:
@@ -345,19 +349,6 @@
         xb[LINE + 4:, :] = jnp.zeros((4, Z), F32)
 
 
-def pack_pot_kernel(pot, fy_lo, fy_hi, o_hi, o_lo):
-    for k in range(RING):
-        o_hi[k * N:(k + 1) * N, :] = pot[N - 1 - k]
-        o_lo[k * N:(k + 1) * N, :] = pot[k]
-    for at, a, side, b in POT_ROWS:
-        halo = fy_hi if side else fy_lo
-        o_hi[at:at + 1, :] = halo[b - 1, N - a:N - a + 1, :]
-        o_lo[at:at + 1, :] = halo[b - 1, a - 1:a, :]
-    end = POT_ROWS[-1][0] + 1
-    o_hi[end:, :] = jnp.zeros((POT_LEN - end, Z), F32)
-    o_lo[end:, :] = jnp.zeros((POT_LEN - end, Z), F32)
-
-
 def transport_kernel(charge, classes_h, mom, cond, conc, pot, yh_lo, yh_hi, xh_lo, xh_hi, yb_lo, yb_hi, xb_lo, xb_hi,
                      fx_lo, fx_hi, fy_lo, fy_hi, gy_lo, conc_out, src, sy_lo, sy_hi,
                      drift, lines, low, dy_hi, own_dy, classes, sem):
@@ -404,8 +395,8 @@
 
     def x_face(fx, xh, xb, sign):
         out = plane(xb, 0) + plane(xb, 1) + plane(xb, 2) + plane(xb, 3) + plane(xb, 4)
-        d = velocity(fx[3], plane(xh, 5) + out, plane(xh, 6) + sign * out)
-        return (fx[1], fx[2], fx[3], fx[0], d)
+        d = velocity(fx[RING + 2], plane(xh, 5) + out, plane(xh, 6) + sign * out)
+        return (fx[RING], fx[RING + 1], fx[RING + 2], fx[0], d)
 
     from_hi, from_lo = y_terms(yb_hi, yb_lo)
 
@@ -460,11 +451,12 @@
         return tuple(fx)
 
     carry = tuple(flux(x_face(fx_lo, xh_lo, xb_lo, -1.0), fields(0, 0)))
-    carry = lax.fori_loop(0, N - 1, lambda x, c: one(x, c, fields(x + 1, 0)), carry)
+    for x in range(N - 1):
+        carry = one(x, carry, fields(x + 1, 0))
     one(N - 1, carry, x_face(fx_hi, xh_hi, xb_hi, 1.0))
 
 
-def sweep_kernel(pot, src, fy_lo, fy_hi, xa_lo, xa_hi, ys_lo, ys_hi, xs_lo, xs_hi, out, ext, even, odd, s_even, s_odd):
+def sweep_kernel(pot, src, fy_lo, fy_hi, fx_lo, fx_hi, ys_lo, ys_hi, xs_lo, xs_hi, out, ext, even, odd, s_even, s_odd):
     mid = slice(OFF, OFF + N)
     top = RING + N
     half = (N + 2 * RING) // 2
@@ -482,12 +474,12 @@
 
         lax.fori_loop(0, N, own, 0, unroll=2)
         for r in range(depth):
-            ext[RING - 1 - r, mid] = x_lo[r * N:(r + 1) * N, :]
-            ext[top + r, mid] = x_hi[r * N:(r + 1) * N, :]
+            ext[RING - 1 - r, mid] = x_lo(r)
+            ext[top + r, mid] = x_hi(r)
         for at, a, side, b in listed:
             y = OFF + N + b - 1 if side else OFF - b
-            ext[RING - a, y:y + 1, :] = x_lo[at:at + 1, :]
-            ext[top + a - 1, y:y + 1, :] = x_hi[at:at + 1, :]
+            ext[RING - a, y:y + 1, :] = xs_lo[at:at + 1, :]
+            ext[top + a - 1, y:y + 1, :] = xs_hi[at:at + 1, :]
 
     def split(a, b):
         def pack(k, carry):
@@ -502,9 +494,9 @@
     for ref in (even, odd):
         ref[0] = zero
         ref[half + 1] = zero
-    fill(pot, fy_lo, fy_hi, xa_lo, xa_hi, RING, POT_ROWS)
+    fill(pot, fy_lo, fy_hi, lambda r: fx_lo[r], lambda r: fx_hi[r], RING, POT_ROWS)
     split(even, odd)
-    fill(src, ys_lo, ys_hi, xs_lo, xs_hi, RING - 1, SRC_ROWS)
+    fill(src, ys_lo, ys_hi, lambda r: plane(xs_lo, r), lambda r: plane(xs_hi, r), RING - 1, SRC_ROWS)
     split(s_even, s_odd)
     for h in range(6):
         this, other, s = (even, odd, s_even) if h % 2 == 0 else (odd, even, s_odd)
@@ -590,55 +582,55 @@
     return listed
 
 
-POT_ROWS = ring_rows(RING * N, RING)
 SRC_ROWS = ring_rows((RING - 1) * N, RING - 1)
-POT_LEN = 128
-SRC_LEN = 104
-
-
-def pack_src_kernel(src, ys_lo, ys_hi, o_hi, o_lo):
+POT_ROWS = ring_rows(SRC_ROWS[-1][0] + 1, RING)
+SRC_LEN = 136
+
+
+def pack_src_kernel(src, ys_lo, ys_hi, fy_lo, fy_hi, o_hi, o_lo):
     for k in range(RING - 1):
         o_hi[k * N:(k + 1) * N, :] = src[N - 1 - k]
         o_lo[k * N:(k + 1) * N, :] = src[k]
-    for at, a, side, b in SRC_ROWS:
-        halo = ys_hi if side else ys_lo
-        o_hi[at:at + 1, :] = halo[b - 1, N - a:N - a + 1, :]
-        o_lo[at:at + 1, :] = halo[b - 1, a - 1:a, :]
-    end = SRC_ROWS[-1][0] + 1
+    for listed, lo, hi in ((SRC_ROWS, ys_lo, ys_hi), (POT_ROWS, fy_lo, fy_hi)):
+        for at, a, side, b in listed:
+            halo = hi if side else lo
+            o_hi[at:at + 1, :] = halo[b - 1, N - a:N - a + 1, :]
+            o_lo[at:at + 1, :] = halo[b - 1, a - 1:a, :]
+    end = POT_ROWS[-1][0] + 1
     o_hi[end:, :] = jnp.zeros((SRC_LEN - end, Z), F32)
     o_lo[end:, :] = jnp.zeros((SRC_LEN - end, Z), F32)
 
 
 def swap(axis, hi, lo):
     n = lax.axis_size(axis)
-    up = [(i, (i + 1) % n) for i in range(n)]
-    down = [(b, a) for a, b in up]
-    return lax.ppermute(hi, axis, up), lax.ppermute(lo, axis, down)
+    even = lax.axis_index(axis) % 2 == 0
+    first = lax.ppermute(jnp.where(even, hi, lo), axis, [(i, i + 1 - 2 * (i % 2)) for i in range(n)])
+    second = lax.ppermute(jnp.where(even, lo, hi), axis, [(i, (i - 1 + 2 * (i % 2)) % n) for i in range(n)])
+    return jnp.where(even, second, first), jnp.where(even, first, second)
 
 
 def body(pops, conc, pot, mob, solid, classes, charge):
     cube = sds(N, N, Z)
     msg = sds(ROWS, Z)
-    gx_hi, gx_lo, gy_hi, gy_lo, pot, conc, cond = call(
-        faces_kernel, [sds(4, N, Z)] * 2 + [sds(RING + 3, N, Z)] * 2 + [cube, sds(2, N, N, Z), cube], "faces", "hhhh",
-        scratch=[VM((N, N, Z), F32), VM((N, N, Z), jnp.int32), pltpu.SemaphoreType.DMA((4,))], moved=2600000)(
+    gx_hi, gx_lo, gy_hi, gy_lo, cond = call(
+        faces_kernel, [sds(RING + 3, N, Z)] * 4 + [cube], "faces", "hhhh",
+        scratch=[VM((N, N, Z), F32), VM((2, N, N, Z), F32), VM((N, N, Z), F32), VM((N, N, Z), jnp.int32),
+                 pltpu.SemaphoreType.DMA((4,))], mib=53, moved=2600000)(
         pot, conc, mob, solid)
     fx_lo, fx_hi = swap("gx", gx_hi, gx_lo)
     fy_lo, fy_hi = swap("gy", gy_hi, gy_lo)
     chunks = N // CHUNK
     buf, mom, px_lo, px_hi, pr_lo, pr_hi = call(
-        collide_kernel, [sds(19, N, N, Z), sds(4, N, N, Z)] + [sds(19, N, Z)] * 4, "collide", "hvvv",
-        scratch=[VM((19, N, N, Z), F32), pltpu.SemaphoreType.DMA((chunks,)), pltpu.SemaphoreType.DMA((2,))],
-        mib=24, flops=20000000, moved=14000000)(pops, pot, conc, cond)
+        collide_kernel, [sds(19, N, N, Z), sds(4, N, N, Z)] + [sds(19, N, Z)] * 4, "collide", "hhhv",
+        scratch=[VM((19, N, N, Z), F32), VM((N, N, Z), F32), VM((2, N, N, Z), F32),
+                 pltpu.SemaphoreType.DMA((chunks,)), pltpu.SemaphoreType.DMA((4,))],
+        mib=43, flops=20000000, moved=14000000)(pops, pot, conc, cond)
     mom, ex_lo, ex_hi, ey_lo, ey_hi, yb_lo, yb_hi = call(
-        edge_kernel, [sds(4, N, N, Z)] + [sds(19, N, Z)] * 4 + [msg, msg], "edge", "v" * 14, moved=3000000)(
-        px_lo, px_hi, pr_lo, pr_hi, gx_lo, gx_hi, gy_lo, gy_hi, fx_lo, fx_hi, fy_lo, fy_hi, pot, mom)
+        edge_kernel, [sds(4, N, N, Z)] + [sds(19, N, Z)] * 4 + [msg, msg], "edge", "v" * 13, moved=3000000)(
+        px_lo, px_hi, pr_lo, pr_hi, gx_lo, gx_hi, gy_lo, gy_hi, fx_lo, fx_hi, fy_lo, fy_hi, mom)
     yh_lo, yh_hi = swap("gy", yb_hi, yb_lo)
     xb_lo, xb_hi = call(corner_kernel, [msg, msg], "corner", "v" * 7)(ex_lo, ex_hi, yh_lo, yh_hi, yb_lo, yb_hi, mom)
     xh_lo, xh_hi = swap("gx", xb_hi, xb_lo)
-    fy_lo2, fy_hi2, _, _ = lax.optimization_barrier((fy_lo, fy_hi, yh_lo, yh_hi))
-    bx_hi, bx_lo = call(pack_pot_kernel, [sds(POT_LEN, Z)] * 2, "pack_pot", "vvv")(pot, fy_lo2, fy_hi2)
-    xa_lo, xa_hi = swap("gx", bx_hi, bx_lo)
     face = VM((N, Z), F32)
     conc_out, src, sy_lo, sy_hi = call(
         transport_kernel, [sds(2, N, N, Z), cube, sds(RING - 1, N, Z), sds(RING - 1, N, Z)], "transport", "sh" + "v" * 17,
@@ -647,13 +639,13 @@
         charge, classes, mom, cond, conc, pot, yh_lo, yh_hi, xh_lo, xh_hi, yb_lo, yb_hi, xb_lo, xb_hi,
         fx_lo, fx_hi, fy_lo, fy_hi, gy_lo)
     ys_lo, ys_hi = swap("gy", sy_hi, sy_lo)
-    bs_hi, bs_lo = call(pack_src_kernel, [sds(SRC_LEN, Z)] * 2, "pack_src", "vvv")(src, ys_lo, ys_hi)
+    bs_hi, bs_lo = call(pack_src_kernel, [sds(SRC_LEN, Z)] * 2, "pack_src", "v" * 5)(src, ys_lo, ys_hi, fy_lo, fy_hi)
     xs_lo, xs_hi = swap("gx", bs_hi, bs_lo)
     packed = VM(((N + 2 * RING) // 2 + 2, N + 2 * OFF, Z), F32)
     potential_out = call(
         sweep_kernel, [cube], "sweep", "v" * 10,
         scratch=[VM((N + 2 * RING, N + 2 * OFF, Z), F32)] + [packed] * 4, flops=20000000, moved=4000000)(
-        pot, src, fy_lo, fy_hi, xa_lo, xa_hi, ys_lo, ys_hi, xs_lo, xs_hi)[0]
+        pot, src, fy_lo, fy_hi, fx_lo, fx_hi, ys_lo, ys_hi, xs_lo, xs_hi)[0]
     pop = call(
         patch_kernel, [sds(19, N, N, Z)], "patch", "v" * 9, out_specs="h",
         scratch=[VM((19, N, N, Z), F32), pltpu.SemaphoreType.DMA((19,))], mib=16, moved=10000000)(

time: 66.9 us -> 62 us (0.927)
  the two profiles are of different devices: /device:TPU:112 before, /device:TPU:7 now
where the time goes in v1:
time: 62 us; the launch traced here: 61.6 us
  starting transfers between devices  22.4 us (36%)
  waiting for transfers between devices  18.4 us (30%)
  Pallas kernels  17.7 us (29%)
  local copies, waits for them, and re-layouts  2 us (3%)
  between operations  0.84 us (1%)
    ppermute x6, starting transfers between devices, swap(): lax.ppermute(jnp.where(even, lo, hi), axis, [(i, (i - 1 + 2 * (i % 2)) %...  22.3 us
    ppermute x6, waiting for transfers between devices, swap(): lax.ppermute(jnp.where(even, lo, hi), axis, [(i, (i - 1 + 2 * (i % 2)) %...  12.6 us
    ppermute x6, waiting for transfers between devices, swap(): lax.ppermute(jnp.where(even, hi, lo), axis, [(i, i + 1 - 2 * (i % 2)) for...  5.84 us
    pallas_call x1, Pallas kernels, body(): call(sweep_kernel, [cube], 'sweep', 'v' * 10, scratch=[VM((N + 2 * RING,...  4.88 us
    pallas_call x1, Pallas kernels, body(): call(collide_kernel, [sds(19, N, N, Z), sds(4, N, N, Z)] + [sds(19, N, Z)...  4.55 us
    pallas_call x1, Pallas kernels, body(): call(transport_kernel, [sds(2, N, N, Z), cube, sds(RING - 1, N, Z), sds(R...  3.17 us
    pallas_call x1, Pallas kernels, body(): call(patch_kernel, [sds(19, N, N, Z)], 'patch', 'v' * 9, out_specs='h', s...  2.46 us
    unnamed x8, local copies, waits for them, and re-layouts  2 us
  transfers between devices with their start and end apart: 12, of which 6 were waited for; matrix products, arithmetic and copies ran while one was open for 0% of the time, Pallas kernels for 11%

profile of v1, /device:TPU:7, one launch (start us, length us, event | category | flops | bytes accessed | tf_op | source)
XLA Modules:
  0.0 61.6 jit_solution(11909791659049949116)
XLA Ops:
  0.6 1.6 %faces.1 = (f32[9,16,256]{2,1,0:T(8,128)S(1)}, f32[9,16,256]{2,1,0:T(8,128)S(1)}, f32[9,16,256]{2,1,0:T(8,128)S(1)}, f32[9,16,256]{2,1,0:T(8,128)S(1)}, f32[16,16,256]{2,1,0:T(8,128)S(1)}) custom-call(f32[16,16,256]{2,1,0:T(8,128)} %pot.3, f32[2,16,16,256]{3,2,1,0:T(8,128)} %conc.1, f32[16,16,256]{2,1,0:T(8,128)} %mob_h.1, s32[16,16,256]{2,1,0:T(8,128)} %solid_h.1), custom_call_target="tpu_custom_call" | custom-call | bytes 2600000 | tf_op jit(solution)/shard_map/faces/pallas_call | solution.py:615
  2.3 8.3 %collective-permute-start = (f32[9,16,256]{2,1,0:T(8,128)S(1)}, f32[9,16,256]{2,1,0:T(8,128)S(1)}, u32[]{:S(2)}, u32[]{:S(2)}) collective-permute-start(f32[9,16,256]{2,1,0:T(8,128)S(1)} %get-tuple-element.62), channel_id=1, source_target_pairs={{0,240},{16,32},{32,16},{48,64},{64,48},{80,96},{96,80},{112,128},... | collective-permute-start | bytes 442376 | tf_op jit(solution)/shard_map/ppermute | solution.py:608
  10.6 0.0 collective-permute-start.1
  10.6 1.2 %collective-permute-start.2 = (f32[9,16,256]{2,1,0:T(8,128)S(1)}, f32[9,16,256]{2,1,0:T(8,128)S(1)}, u32[]{:S(2)}, u32[]{:S(2)}) collective-permute-start(f32[9,16,256]{2,1,0:T(8,128)S(1)} %get-tuple-element.58), channel_id=1, source_target_pairs={{0,15},{1,2},{2,1},{3,4},{4,3},{5,6},{6,5},{7,8},{8,7},{9,10},{10,... | collective-permute-start | bytes 442376 | tf_op jit(solution)/shard_map/ppermute | solution.py:608
  11.8 0.0 collective-permute-start.3
  11.9 1.0 %copy-done = f32[2,16,16,256]{3,2,1,0:T(8,128)S(1)} copy-done((f32[2,16,16,256]{3,2,1,0:T(8,128)S(1)}, f32[2,16,16,256]{3,2,1,0:T(8,128)}, u32[]{:S(2)}) %copy-start) | copy-done | bytes 524312
  12.9 0.9 %copy-done.1 = f32[16,16,256]{2,1,0:T(8,128)S(1)} copy-done((f32[16,16,256]{2,1,0:T(8,128)S(1)}, f32[16,16,256]{2,1,0:T(8,128)}, u32[]{:S(2)}) %copy-start.1) | copy-done | bytes 262168
  13.8 4.5 %collide.1 = (f32[19,16,16,256]{3,2,1,0:T(8,128)S(1)}, f32[4,16,16,256]{3,2,1,0:T(8,128)S(1)}, f32[19,16,256]{2,1,0:T(8,128)S(1)}, f32[19,16,256]{2,1,0:T(8,128)...) custom-call(f32[19,16,16,256]{3,2,1,0:T(8,128)} %pops.1, f32[16,16,256]{2,1,0:T(8,128)S(1)} %copy-done.1, ...), custom_call_target="tpu_custom_call" | custom-call | flops 20000000 | bytes 14000000 | tf_op jit(solution)/shard_map/collide/pallas_call | solution.py:623
  18.4 0.0 copy-start.2
  18.4 0.0 copy-start.3
  18.4 0.0 collective-permute-done
  18.4 0.0 collective-permute-done.1
  18.5 0.0 collective-permute-done.2
  18.5 1.0 %edge.1 = (f32[4,16,16,256]{3,2,1,0:T(8,128)S(1)}, f32[19,16,256]{2,1,0:T(8,128)S(1)}, f32[19,16,256]{2,1,0:T(8,128)S(1)}, f32[19,16,256]{2,1,0:T(8,128)S(1)}, f...) custom-call(f32[19,16,256]{2,1,0:T(8,128)S(1)} %get-tuple-element.31.px_lo, ...), custom_call_target="tpu_custom_call" | custom-call | bytes 3000000 | tf_op jit(solution)/shard_map/edge/pallas_call | solution.py:628
  19.5 2.8 %collective-permute-start.4 = (f32[120,256]{1,0:T(8,128)S(1)}, f32[120,256]{1,0:T(8,128)S(1)}, u32[]{:S(2)}, u32[]{:S(2)}) collective-permute-start(f32[120,256]{1,0:T(8,128)S(1)} %get-tuple-element.74), channel_id=1, source_target_pairs={{0,15},{1,2},{2,1},{3,4},{4,3},{5,6},{6,5},{7,8},{8,7},{9,10},{10,... | collective-permute-start | bytes 368648 | tf_op jit(solution)/shard_map/ppermute | solution.py:608
  22.3 3.7 %collective-permute-done.4 = f32[120,256]{1,0:T(8,128)S(1)} collective-permute-done((f32[120,256]{1,0:T(8,128)S(1)}, f32[120,256]{1,0:T(8,128)S(1)}, u32[]{:S(2)}, u32[]{:S(2)}) %collective-permute-start.4) | collective-permute-done | bytes 122912 | tf_op jit(solution)/shard_map/ppermute | solution.py:608
  26.0 0.0 collective-permute-done.5
  26.1 4.4 %collective-permute-start.6 = (f32[120,256]{1,0:T(8,128)S(1)}, f32[120,256]{1,0:T(8,128)S(1)}, u32[]{:S(2)}, u32[]{:S(2)}) collective-permute-start(f32[120,256]{1,0:T(8,128)S(1)} %get-tuple-element.70), channel_id=1, source_target_pairs={{0,240},{16,32},{32,16},{48,64},{64,48},{80,96},{96,80},{112,128},... | collective-permute-start | bytes 368648 | tf_op jit(solution)/shard_map/ppermute | solution.py:608
  30.5 0.0 collective-permute-start.7
  30.5 3.2 %collective-permute-done.6 = f32[120,256]{1,0:T(8,128)S(1)} collective-permute-done((f32[120,256]{1,0:T(8,128)S(1)}, f32[120,256]{1,0:T(8,128)S(1)}, u32[]{:S(2)}, u32[]{:S(2)}) %collective-permute-start.6) | collective-permute-done | bytes 122912 | tf_op jit(solution)/shard_map/ppermute | solution.py:608
  33.7 2.7 %collective-permute-done.7 = f32[120,256]{1,0:T(8,128)S(1)} collective-permute-done((f32[120,256]{1,0:T(8,128)S(1)}, f32[120,256]{1,0:T(8,128)S(1)}, u32[]{:S(2)}, u32[]{:S(2)}) %collective-permute-start.7) | collective-permute-done | bytes 122912 | tf_op jit(solution)/shard_map/ppermute | solution.py:607
  36.5 3.2 %transport.1 = (f32[2,16,16,256]{3,2,1,0:T(8,128)}, f32[16,16,256]{2,1,0:T(8,128)S(1)}, f32[5,16,256]{2,1,0:T(8,128)S(1)}, f32[5,16,256]{2,1,0:T(8,128)S(1)}) custom-call(f32[4]{0:T(128)S(1)} %copy-done.3, s32[16,16,256]{2,1,0:T(8,128)S(1)} %copy-done.2, f32[4,16,16,256]{3,2,1,0:T(8,128)S(1)} %get-tuple-element.46.mom, ...), custom_call_target="tpu_custom_call" | custom-call | flops 10000000 | bytes 8000000 | tf_op jit(solution)/shard_map/transport/pallas_call | solution.py:635
  39.7 2.4 %collective-permute-start.8 = (f32[5,16,256]{2,1,0:T(8,128)S(1)}, f32[5,16,256]{2,1,0:T(8,128)S(1)}, u32[]{:S(2)}, u32[]{:S(2)}) collective-permute-start(f32[5,16,256]{2,1,0:T(8,128)S(1)} %get-tuple-element.78), channel_id=1, source_target_pairs={{0,15},{1,2},{2,1},{3,4},{4,3},{5,6},{6,5},{7,8},{8,7},{9,10},{10,... | collective-permute-start | bytes 245768 | tf_op jit(solution)/shard_map/ppermute | solution.py:608
  42.1 0.0 collective-permute-start.9
  42.1 3.7 %collective-permute-done.8 = f32[5,16,256]{2,1,0:T(8,128)S(1)} collective-permute-done((f32[5,16,256]{2,1,0:T(8,128)S(1)}, f32[5,16,256]{2,1,0:T(8,128)S(1)}, u32[]{:S(2)}, u32[]{:S(2)}) %collective-permute-start.8) | collective-permute-done | bytes 81952 | tf_op jit(solution)/shard_map/ppermute | solution.py:608
  45.8 0.1 pack_src.1
  45.9 3.2 %collective-permute-start.10 = (f32[136,256]{1,0:T(8,128)S(1)}, f32[136,256]{1,0:T(8,128)S(1)}, u32[]{:S(2)}, u32[]{:S(2)}) collective-permute-start(f32[136,256]{1,0:T(8,128)S(1)} %get-tuple-element.66), channel_id=1, source_target_pairs={{0,240},{16,32},{32,16},{48,64},{64,48},{80,96},{96,80},{112,128},... | collective-permute-start | bytes 417800 | tf_op jit(solution)/shard_map/ppermute | solution.py:608
  49.2 0.0 collective-permute-start.11
  49.2 2.5 %patch.1 = f32[19,16,16,256]{3,2,1,0:T(8,128)} custom-call(f32[19,16,16,256]{3,2,1,0:T(8,128)S(1)} %get-tuple-element.30.buf, f32[19,16,256]{2,1,0:T(8,128)S(1)} %get-tuple-element.40.ex_lo, f32[19,16,256]{2,1,0:T(8,128)S(1)} %get-tuple-element.41.ex_hi, f32[19,16,256]{2,1,0:T(8,128)S(1)} %get-tuple-element.42.ey_lo, ...), custom_call_target="tpu_custom_call" | custom-call | bytes 10000000 | tf_op jit(solution)/shard_map/patch/pallas_call | solution.py:649
  51.6 2.0 %collective-permute-done.10 = f32[136,256]{1,0:T(8,128)S(1)} collective-permute-done((f32[136,256]{1,0:T(8,128)S(1)}, f32[136,256]{1,0:T(8,128)S(1)}, u32[]{:S(2)}, u32[]{:S(2)}) %collective-permute-start.10) | collective-permute-done | bytes 139296 | tf_op jit(solution)/shard_map/ppermute | solution.py:608
  53.6 3.1 %collective-permute-done.11 = f32[136,256]{1,0:T(8,128)S(1)} collective-permute-done((f32[136,256]{1,0:T(8,128)S(1)}, f32[136,256]{1,0:T(8,128)S(1)}, u32[]{:S(2)}, u32[]{:S(2)}) %collective-permute-start.11) | collective-permute-done | bytes 139296 | tf_op jit(solution)/shard_map/ppermute | solution.py:607
  56.7 4.9 %sweep.1 = f32[16,16,256]{2,1,0:T(8,128)} custom-call(f32[16,16,256]{2,1,0:T(8,128)S(1)} %copy-done.1, f32[16,16,256]{2,1,0:T(8,128)S(1)} %get-tuple-element.50.src, f32[9,16,256]{2,1,0:T(8,128)S(1)} %get-tuple-element.56.fy_lo, f32[9,16,256]{2,1,0:T(8,128)S(1)} %get-tuple-element.55.fy_hi, f32[9,16,256]{2,1,0:T(8,128)S(1)} %get-tuple-element.60.fx_lo, ...), custom_call_target="tpu_custom_call" | custom-call | flops 20000000 | bytes 4000000 | tf_op jit(solution)/shard_map/sweep/pallas_call | solution.py:645
  (20 shorter events, 0.3 us)
Async XLA Ops:
  2.3 16.1 %collective-permute-start = (f32[9,16,256]{2,1,0:T(8,128)S(1)}, f32[9,16,256]{2,1,0:T(8,128)S(1)}, u32[]{:S(2)}, u32[]{:S(2)}) collective-permute-start(f32[9,16,256]{2,1,0:T(8,128)S(1)} %get-tuple-element.62), channel_id=1, source_target_pairs={{0,240},{16,32},{32,16},{48,64},{64,48},{80,96},{96,80},{112,128},... | collective-permute-start | bytes 442376 | tf_op jit(solution)/shard_map/ppermute | solution.py:608
  10.6 7.9 %collective-permute-start.1 = (f32[9,16,256]{2,1,0:T(8,128)S(1)}, f32[9,16,256]{2,1,0:T(8,128)S(1)}, u32[]{:S(2)}, u32[]{:S(2)}) collective-permute-start(f32[9,16,256]{2,1,0:T(8,128)S(1)} %get-tuple-element.61), channel_id=1, source_target_pairs={{0,16},{16,0},{32,48},{48,32},{64,80},{80,64},{96,112},{112,96},{1... | collective-permute-start | bytes 442376 | tf_op jit(solution)/shard_map/ppermute | solution.py:607
  10.6 7.9 %collective-permute-start.2 = (f32[9,16,256]{2,1,0:T(8,128)S(1)}, f32[9,16,256]{2,1,0:T(8,128)S(1)}, u32[]{:S(2)}, u32[]{:S(2)}) collective-permute-start(f32[9,16,256]{2,1,0:T(8,128)S(1)} %get-tuple-element.58), channel_id=1, source_target_pairs={{0,15},{1,2},{2,1},{3,4},{4,3},{5,6},{6,5},{7,8},{8,7},{9,10},{10,... | collective-permute-start | bytes 442376 | tf_op jit(solution)/shard_map/ppermute | solution.py:608
  11.8 6.6 %collective-permute-start.3 = (f32[9,16,256]{2,1,0:T(8,128)S(1)}, f32[9,16,256]{2,1,0:T(8,128)S(1)}, u32[]{:S(2)}, u32[]{:S(2)}) collective-permute-start(f32[9,16,256]{2,1,0:T(8,128)S(1)} %get-tuple-element.57), channel_id=1, source_target_pairs={{0,1},{1,0},{2,3},{3,2},{4,5},{5,4},{6,7},{7,6},{8,9},{9,8},{10,11... | collective-permute-start | bytes 442376 | tf_op jit(solution)/shard_map/ppermute | solution.py:607
  11.9 1.0 %copy-start = (f32[2,16,16,256]{3,2,1,0:T(8,128)S(1)}, f32[2,16,16,256]{3,2,1,0:T(8,128)}, u32[]{:S(2)}) copy-start(f32[2,16,16,256]{3,2,1,0:T(8,128)} %conc.1) | copy-start | bytes 1572868
  12.9 0.9 %copy-start.1 = (f32[16,16,256]{2,1,0:T(8,128)S(1)}, f32[16,16,256]{2,1,0:T(8,128)}, u32[]{:S(2)}) copy-start(f32[16,16,256]{2,1,0:T(8,128)} %pot.3) | copy-start | bytes 786436
  18.4 18.1 %copy-start.2 = (s32[16,16,256]{2,1,0:T(8,128)S(1)}, s32[16,16,256]{2,1,0:T(8,128)}, u32[]{:S(2)}) copy-start(s32[16,16,256]{2,1,0:T(8,128)} %classes_h.1) | copy-start | bytes 786436
  18.4 18.1 %copy-start.3 = (f32[4]{0:T(128)S(1)}, f32[4]{0:T(128)}, u32[]{:S(2)}) copy-start(f32[4]{0:T(128)} %charge.1) | copy-start | bytes 52
  19.5 6.5 %collective-permute-start.4 = (f32[120,256]{1,0:T(8,128)S(1)}, f32[120,256]{1,0:T(8,128)S(1)}, u32[]{:S(2)}, u32[]{:S(2)}) collective-permute-start(f32[120,256]{1,0:T(8,128)S(1)} %get-tuple-element.74), channel_id=1, source_target_pairs={{0,15},{1,2},{2,1},{3,4},{4,3},{5,6},{6,5},{7,8},{8,7},{9,10},{10,... | collective-permute-start | bytes 368648 | tf_op jit(solution)/shard_map/ppermute | solution.py:608
  22.3 3.7 %collective-permute-start.5 = (f32[120,256]{1,0:T(8,128)S(1)}, f32[120,256]{1,0:T(8,128)S(1)}, u32[]{:S(2)}, u32[]{:S(2)}) collective-permute-start(f32[120,256]{1,0:T(8,128)S(1)} %get-tuple-element.73), channel_id=1, source_target_pairs={{0,1},{1,0},{2,3},{3,2},{4,5},{5,4},{6,7},{7,6},{8,9},{9,8},{10,11... | collective-permute-start | bytes 368648 | tf_op jit(solution)/shard_map/ppermute | solution.py:607
  26.1 7.6 %collective-permute-start.6 = (f32[120,256]{1,0:T(8,128)S(1)}, f32[120,256]{1,0:T(8,128)S(1)}, u32[]{:S(2)}, u32[]{:S(2)}) collective-permute-start(f32[120,256]{1,0:T(8,128)S(1)} %get-tuple-element.70), channel_id=1, source_target_pairs={{0,240},{16,32},{32,16},{48,64},{64,48},{80,96},{96,80},{112,128},... | collective-permute-start | bytes 368648 | tf_op jit(solution)/shard_map/ppermute | solution.py:608
  30.5 6.0 %collective-permute-start.7 = (f32[120,256]{1,0:T(8,128)S(1)}, f32[120,256]{1,0:T(8,128)S(1)}, u32[]{:S(2)}, u32[]{:S(2)}) collective-permute-start(f32[120,256]{1,0:T(8,128)S(1)} %get-tuple-element.69), channel_id=1, source_target_pairs={{0,16},{16,0},{32,48},{48,32},{64,80},{80,64},{96,112},{112,96},{1... | collective-permute-start | bytes 368648 | tf_op jit(solution)/shard_map/ppermute | solution.py:607
  39.7 6.1 %collective-permute-start.8 = (f32[5,16,256]{2,1,0:T(8,128)S(1)}, f32[5,16,256]{2,1,0:T(8,128)S(1)}, u32[]{:S(2)}, u32[]{:S(2)}) collective-permute-start(f32[5,16,256]{2,1,0:T(8,128)S(1)} %get-tuple-element.78), channel_id=1, source_target_pairs={{0,15},{1,2},{2,1},{3,4},{4,3},{5,6},{6,5},{7,8},{8,7},{9,10},{10,... | collective-permute-start | bytes 245768 | tf_op jit(solution)/shard_map/ppermute | solution.py:608
  42.1 3.7 %collective-permute-start.9 = (f32[5,16,256]{2,1,0:T(8,128)S(1)}, f32[5,16,256]{2,1,0:T(8,128)S(1)}, u32[]{:S(2)}, u32[]{:S(2)}) collective-permute-start(f32[5,16,256]{2,1,0:T(8,128)S(1)} %get-tuple-element.77), channel_id=1, source_target_pairs={{0,1},{1,0},{2,3},{3,2},{4,5},{5,4},{6,7},{7,6},{8,9},{9,8},{10,11... | collective-permute-start | bytes 245768 | tf_op jit(solution)/shard_map/ppermute | solution.py:607
  45.9 7.7 %collective-permute-start.10 = (f32[136,256]{1,0:T(8,128)S(1)}, f32[136,256]{1,0:T(8,128)S(1)}, u32[]{:S(2)}, u32[]{:S(2)}) collective-permute-start(f32[136,256]{1,0:T(8,128)S(1)} %get-tuple-element.66), channel_id=1, source_target_pairs={{0,240},{16,32},{32,16},{48,64},{64,48},{80,96},{96,80},{112,128},... | collective-permute-start | bytes 417800 | tf_op jit(solution)/shard_map/ppermute | solution.py:608
  49.2 7.6 %collective-permute-start.11 = (f32[136,256]{1,0:T(8,128)S(1)}, f32[136,256]{1,0:T(8,128)S(1)}, u32[]{:S(2)}, u32[]{:S(2)}) collective-permute-start(f32[136,256]{1,0:T(8,128)S(1)} %get-tuple-element.65), channel_id=1, source_target_pairs={{0,16},{16,0},{32,48},{48,32},{64,80},{80,64},{96,112},{112,96},{1... | collective-permute-start | bytes 417800 | tf_op jit(solution)/shard_map/ppermute | solution.py:607

commit v2 on v1

--- a/solution.py
+++ b/solution.py
@@ -213,7 +213,7 @@
         c.wait()
     for s in range(N // CHUNK):
         chunks[s].wait()
-        lax.fori_loop(max(CHUNK * s, 1), min(CHUNK * s + CHUNK, N - 1), step, 0)
+        lax.fori_loop(max(CHUNK * s, 1), min(CHUNK * s + CHUNK, N - 1), step, 0, unroll=True)
     for c in ends:
         c.wait()
 
@@ -349,11 +349,8 @@
         xb[LINE + 4:, :] = jnp.zeros((4, Z), F32)
 
 
-def transport_kernel(charge, classes_h, mom, cond, conc, pot, yh_lo, yh_hi, xh_lo, xh_hi, yb_lo, yb_hi, xb_lo, xb_hi,
-                     fx_lo, fx_hi, fy_lo, fy_hi, gy_lo, conc_out, src, sy_lo, sy_hi,
-                     drift, lines, low, dy_hi, own_dy, classes, sem):
-    fetch = pltpu.make_async_copy(classes_h, classes, sem)
-    fetch.start()
+def transport_kernel(mom, cond, base, wx, wy, wy_low, wz, wall, yh_lo, yh_hi, xh_lo, xh_hi, yb_lo, yb_hi, xb_lo, xb_hi,
+                     fx_lo, fx_hi, fy_lo, fy_hi, conc_out, src, sy_lo, sy_hi, drift, lines, low, dy_hi, own_dy):
     row = rows()
     below, above = y_terms(yh_lo, yh_hi)
     for m in range(4):
@@ -395,8 +392,7 @@
 
     def x_face(fx, xh, xb, sign):
         out = plane(xb, 0) + plane(xb, 1) + plane(xb, 2) + plane(xb, 3) + plane(xb, 4)
-        d = velocity(fx[RING + 2], plane(xh, 5) + out, plane(xh, 6) + sign * out)
-        return (fx[RING], fx[RING + 1], fx[RING + 2], fx[0], d)
+        return velocity(fx[RING + 2], plane(xh, 5) + out, plane(xh, 6) + sign * out)
 
     from_hi, from_lo = y_terms(yb_hi, yb_lo)
 
@@ -406,98 +402,86 @@
         for xh, x in ((xh_lo, 0), (xh_hi, N - 1)):
             density = density + jnp.where(row == x, spread(xh[k:k + 1, :]), 0.0)
             momentum = momentum + jnp.where(row == x, spread(xh[k + 1:k + 2, :]), 0.0)
-        d = velocity(fy[RING + 2], density, momentum)
-        return (fy[RING], fy[RING + 1], fy[RING + 2], fy[0], d)
-
-    left = y_face(fy_lo, yh_lo, from_lo, LINE)
-    first = flux(left, (gy_lo[RING], gy_lo[RING + 1], gy_lo[RING + 2], gy_lo[0], own_dy[...]))
-    low[0] = first[0]
-    low[1] = first[1]
-    dy_hi[...] = y_face(fy_hi, yh_hi, from_hi, LINE + 2)[4]
-    fetch.wait()
-
-    def fields(x, d):
-        return (conc[0, x], conc[1, x], cond[x], pot[x], drift[d, x])
-
-    def one(x, behind, ahead):
-        here = pl.ds(x, 1)
-        me = fields(x, 0)
-        fx = flux(me, ahead)
-        tot = [fx[s] - behind[s] for s in range(2)]
-        mine = me[:4] + (drift[1, x],)
-        halo = (fy_hi[RING, here, :], fy_hi[RING + 1, here, :], fy_hi[RING + 2, here, :], fy_hi[0, here, :], dy_hi[here, :])
-        nxt = tuple(jnp.where(row == N - 1, spread(halo[q]), roll_y(mine[q], -1)) for q in range(5))
-        fy = flux(mine, nxt)
+        return velocity(fy[RING + 2], density, momentum)
+
+    carried = y_face(fy_lo, yh_lo, from_lo, LINE) + own_dy[...]
+    for s in range(2):
+        low[s] = wy_low[s] * carried
+    dy_hi[...] = y_face(fy_hi, yh_hi, from_hi, LINE + 2)
+    carried = x_face(fx_lo, xh_lo, xb_lo, -1.0) + drift[0, 0]
+    behind = [wx[s, 0] * carried for s in range(2)]
+    last = x_face(fx_hi, xh_hi, xb_hi, 1.0)
+    for x in range(N):
+        carried = drift[0, x] + (drift[0, x + 1] if x < N - 1 else last)
+        ahead = [wx[s, x + 1] * carried for s in range(2)]
+        tot = [ahead[s] - behind[s] for s in range(2)]
+        behind = ahead
+        v = drift[1, x]
+        carried = v + jnp.where(row == N - 1, spread(dy_hi[x:x + 1, :]), roll_y(v, -1))
         for s in range(2):
-            before = jnp.where(row == 0, spread(low[s, here, :]), roll_y(fy[s], 1))
-            tot[s] = tot[s] + (fy[s] - before)
-        mine = me[:4] + (drift[2, x],)
-        fz = flux(mine, tuple(roll_z(v, -1) for v in mine))
+            f = wy[s, x] * carried
+            tot[s] = tot[s] + (f - jnp.where(row == 0, spread(low[s, x:x + 1, :]), roll_y(f, 1)))
+        v = drift[2, x]
+        carried = v + roll_z(v, -1)
         for s in range(2):
-            tot[s] = tot[s] + (fz[s] - roll_z(fz[s], 1))
-        c0 = me[0] - tot[0]
-        c1 = me[1] - tot[1]
+            f = wz[s, x] * carried
+            tot[s] = tot[s] + (f - roll_z(f, 1))
+        c0 = base[0, x] - tot[0]
+        c1 = base[1, x] - tot[1]
         conc_out[0, x] = c0
         conc_out[1, x] = c1
-        cls = classes[x]
-        wall = jnp.zeros((N, Z), F32)
-        for q in range(4):
-            wall = wall + jnp.where(cls == q, charge[q], 0.0)
-        s_val = jnp.where(me[2] > 0.0, c0 - c1, wall)
+        s_val = jnp.where(cond[x] > 0.0, c0 - c1, wall[x])
         src[x] = s_val
         for r in range(RING - 1):
-            sy_lo[r, here, :] = row_of(s_val, r)
-            sy_hi[r, here, :] = row_of(s_val, N - 1 - r)
-        return tuple(fx)
-
-    carry = tuple(flux(x_face(fx_lo, xh_lo, xb_lo, -1.0), fields(0, 0)))
-    for x in range(N - 1):
-        carry = one(x, carry, fields(x + 1, 0))
-    one(N - 1, carry, x_face(fx_hi, xh_hi, xb_hi, 1.0))
-
-
-def sweep_kernel(pot, src, fy_lo, fy_hi, fx_lo, fx_hi, ys_lo, ys_hi, xs_lo, xs_hi, out, ext, even, odd, s_even, s_odd):
+            sy_lo[r, x:x + 1, :] = row_of(s_val, r)
+            sy_hi[r, x:x + 1, :] = row_of(s_val, N - 1 - r)
+
+
+def split(ext, a, b, pairs, shift):
+    shape = (N + 2 * OFF, Z)
+    mask = (lax.broadcasted_iota(jnp.int32, shape, 0) + lax.broadcasted_iota(jnp.int32, shape, 1)) % 2 == 0
+    for k in pairs:
+        p, q = ext[2 * k], ext[2 * k + 1]
+        a[k + shift] = jnp.where(mask, p, q)
+        b[k + shift] = jnp.where(mask, q, p)
+
+
+def prepare_kernel(pot, src, fy_lo, fy_hi, ys_lo, ys_hi, even, odd, s_even, s_odd, ext):
+    for centre, y_lo, y_hi, depth, a, b in ((pot, fy_lo, fy_hi, RING, even, odd), (src, ys_lo, ys_hi, RING - 1, s_even, s_odd)):
+        for x in range(N):
+            ext[x, OFF:OFF + N] = centre[x]
+            for r in range(depth):
+                ext[x, OFF - 1 - r:OFF - r, :] = y_lo[r, x:x + 1, :]
+                ext[x, OFF + N + r:OFF + N + r + 1, :] = y_hi[r, x:x + 1, :]
+        split(ext, a, b, range(N // 2), 0)
+
+
+def sweep_kernel(even_in, odd_in, s_even_in, s_odd_in, fx_lo, fx_hi, xs_lo, xs_hi, out, ext, even, odd, s_even, s_odd):
     mid = slice(OFF, OFF + N)
     top = RING + N
     half = (N + 2 * RING) // 2
     shape = (N + 2 * OFF, Z)
     mask = (lax.broadcasted_iota(jnp.int32, shape, 0) + lax.broadcasted_iota(jnp.int32, shape, 1)) % 2 == 0
-
-    def fill(centre, y_lo, y_hi, x_lo, x_hi, depth, listed):
-        def own(x, carry):
-            here = pl.ds(x, 1)
-            ext[RING + x, mid] = centre[x]
-            for r in range(depth):
-                ext[RING + x, OFF - 1 - r:OFF - r, :] = y_lo[r, here, :]
-                ext[RING + x, OFF + N + r:OFF + N + r + 1, :] = y_hi[r, here, :]
-            return carry
-
-        lax.fori_loop(0, N, own, 0, unroll=2)
-        for r in range(depth):
-            ext[RING - 1 - r, mid] = x_lo(r)
-            ext[top + r, mid] = x_hi(r)
-        for at, a, side, b in listed:
-            y = OFF + N + b - 1 if side else OFF - b
-            ext[RING - a, y:y + 1, :] = xs_lo[at:at + 1, :]
-            ext[top + a - 1, y:y + 1, :] = xs_hi[at:at + 1, :]
-
-    def split(a, b):
-        def pack(k, carry):
-            p, q = ext[2 * k], ext[2 * k + 1]
-            a[k + 1] = jnp.where(mask, p, q)
-            b[k + 1] = jnp.where(mask, q, p)
-            return carry
-
-        lax.fori_loop(0, half, pack, 0, unroll=2)
-
     zero = jnp.zeros(shape, F32)
     for ref in (even, odd):
         ref[0] = zero
         ref[half + 1] = zero
-    fill(pot, fy_lo, fy_hi, lambda r: fx_lo[r], lambda r: fx_hi[r], RING, POT_ROWS)
-    split(even, odd)
-    fill(src, ys_lo, ys_hi, lambda r: plane(xs_lo, r), lambda r: plane(xs_hi, r), RING - 1, SRC_ROWS)
-    split(s_even, s_odd)
+    for ref, given in ((even, even_in), (odd, odd_in), (s_even, s_even_in), (s_odd, s_odd_in)):
+        for k in range(N // 2):
+            ref[k + 1 + RING // 2] = given[k]
+    ends = list(range(RING // 2)) + list(range(RING // 2 + N // 2, half))
+    for x_lo, x_hi, depth, listed, a, b in (
+            (lambda r: fx_lo[r], lambda r: fx_hi[r], RING, POT_ROWS, even, odd),
+            (lambda r: plane(xs_lo, r), lambda r: plane(xs_hi, r), RING - 1, SRC_ROWS, s_even, s_odd)):
+        for r in range(depth):
+            ext[RING - 1 - r, mid] = x_lo(r)
+            ext[top + r, mid] = x_hi(r)
+        for at, a_ring, side, b_ring in listed:
+            y = OFF + N + b_ring - 1 if side else OFF - b_ring
+            ext[RING - a_ring, y:y + 1, :] = xs_lo[at:at + 1, :]
+            ext[top + a_ring - 1, y:y + 1, :] = xs_hi[at:at + 1, :]
+        split(ext, a, b, ends, 1)
+
     for h in range(6):
         this, other, s = (even, odd, s_even) if h % 2 == 0 else (odd, even, s_odd)
 
@@ -510,7 +494,8 @@
             return carry
 
         lo = (h + 1) // 2
-        lax.fori_loop(lo + 1, half - lo + 1, update, 0, unroll=2)
+        for k in range(lo + 1, half - lo + 1):
+            update(k, 0)
 
     def last(k, carry):
         p, q = even[k], odd[k]
@@ -562,13 +547,59 @@
 
 def flux(a, b):
     link = a[2] * b[2]
-    carried = 0.5 * (a[4] + b[4])
     drop = a[3] - b[3]
-    got = []
+    rest, weight = [], []
     for s in range(2):
-        mean = 0.5 * (a[s] + b[s])
-        got.append(link * (RATES[s] * ((a[s] - b[s]) + (VAL[s] * mean) * drop) + mean * carried))
-    return got
+        both = a[s] + b[s]
+        rest.append(link * (RATES[s] * ((a[s] - b[s]) + ((0.5 * VAL[s]) * both) * drop)))
+        weight.append((0.25 * link) * both)
+    return rest, weight
+
+
+def diffuse_kernel(charge, classes_h, cond, conc, pot, fx_lo, fx_hi, fy_lo, fy_hi, gy_lo,
+                   base, wx, wy, wy_low, wz, wall, low, classes, sem):
+    fetch = pltpu.make_async_copy(classes_h, classes, sem)
+    fetch.start()
+    row = rows()
+
+    def faces(ref):
+        return tuple(ref[RING + q] for q in range(3)) + (ref[0],)
+
+    rest, weight = flux(faces(fy_lo), faces(gy_lo))
+    for s in range(2):
+        low[s] = rest[s]
+        wy_low[s] = weight[s]
+    upper = faces(fy_hi)
+
+    def fields(x):
+        return (conc[0, x], conc[1, x], cond[x], pot[x])
+
+    behind, weight = flux(faces(fx_lo), fields(0))
+    for s in range(2):
+        wx[s, 0] = weight[s]
+    fetch.wait()
+    for x in range(N):
+        me = fields(x)
+        ahead, weight = flux(me, fields(x + 1) if x < N - 1 else faces(fx_hi))
+        tot = [ahead[s] - behind[s] for s in range(2)]
+        behind = ahead
+        for s in range(2):
+            wx[s, x + 1] = weight[s]
+        nxt = tuple(jnp.where(row == N - 1, spread(row_of(upper[q], x)), roll_y(me[q], -1)) for q in range(4))
+        rest, weight = flux(me, nxt)
+        for s in range(2):
+            wy[s, x] = weight[s]
+            tot[s] = tot[s] + (rest[s] - jnp.where(row == 0, spread(low[s, x:x + 1, :]), roll_y(rest[s], 1)))
+        rest, weight = flux(me, tuple(roll_z(v, -1) for v in me))
+        for s in range(2):
+            wz[s, x] = weight[s]
+            tot[s] = tot[s] + (rest[s] - roll_z(rest[s], 1))
+            base[s, x] = me[s] - tot[s]
+        cls = classes[x]
+        total = jnp.zeros((N, Z), F32)
+        for q in range(4):
+            total = total + jnp.where(cls == q, charge[q], 0.0)
+        wall[x] = total
 
 
 def ring_rows(depth, total):
@@ -632,20 +663,28 @@
     xb_lo, xb_hi = call(corner_kernel, [msg, msg], "corner", "v" * 7)(ex_lo, ex_hi, yh_lo, yh_hi, yb_lo, yb_hi, mom)
     xh_lo, xh_hi = swap("gx", xb_hi, xb_lo)
     face = VM((N, Z), F32)
+    fy_late, _ = lax.optimization_barrier((fy_lo, yh_lo))
+    pair = sds(2, N, N, Z)
+    base, wx, wy, wy_low, wz, wall = call(
+        diffuse_kernel, [pair, sds(2, N + 1, N, Z), pair, sds(2, N, Z), pair, cube], "diffuse", "sh" + "v" * 8,
+        scratch=[VM((2, N, Z), F32), VM((N, N, Z), jnp.int32), pltpu.SemaphoreType.DMA], flops=10000000, moved=6000000)(
+        charge, classes, cond, conc, pot, fx_lo, fx_hi, fy_late, fy_hi, gy_lo)
     conc_out, src, sy_lo, sy_hi = call(
-        transport_kernel, [sds(2, N, N, Z), cube, sds(RING - 1, N, Z), sds(RING - 1, N, Z)], "transport", "sh" + "v" * 17,
-        scratch=[VM((3, N, N, Z), F32), VM((8, N, Z), F32), VM((2, N, Z), F32), face, face, VM((N, N, Z), jnp.int32),
-                 pltpu.SemaphoreType.DMA], flops=10000000, moved=8000000)(
-        charge, classes, mom, cond, conc, pot, yh_lo, yh_hi, xh_lo, xh_hi, yb_lo, yb_hi, xb_lo, xb_hi,
-        fx_lo, fx_hi, fy_lo, fy_hi, gy_lo)
+        transport_kernel, [pair, cube, sds(RING - 1, N, Z), sds(RING - 1, N, Z)], "transport", "v" * 20,
+        scratch=[VM((3, N, N, Z), F32), VM((8, N, Z), F32), VM((2, N, Z), F32), face, face], flops=5000000, moved=4000000)(
+        mom, cond, base, wx, wy, wy_low, wz, wall, yh_lo, yh_hi, xh_lo, xh_hi, yb_lo, yb_hi, xb_lo, xb_hi,
+        fx_lo, fx_hi, fy_lo, fy_hi)
     ys_lo, ys_hi = swap("gy", sy_hi, sy_lo)
     bs_hi, bs_lo = call(pack_src_kernel, [sds(SRC_LEN, Z)] * 2, "pack_src", "v" * 5)(src, ys_lo, ys_hi, fy_lo, fy_hi)
     xs_lo, xs_hi = swap("gx", bs_hi, bs_lo)
     packed = VM(((N + 2 * RING) // 2 + 2, N + 2 * OFF, Z), F32)
+    prepared = call(
+        prepare_kernel, [sds(N // 2, N + 2 * OFF, Z)] * 4, "prepare", "v" * 6,
+        scratch=[VM((N, N + 2 * OFF, Z), F32)], flops=1000000, moved=4000000)(pot, src, fy_lo, fy_hi, ys_lo, ys_hi)
     potential_out = call(
-        sweep_kernel, [cube], "sweep", "v" * 10,
+        sweep_kernel, [cube], "sweep", "v" * 8,
         scratch=[VM((N + 2 * RING, N + 2 * OFF, Z), F32)] + [packed] * 4, flops=20000000, moved=4000000)(
-        pot, src, fy_lo, fy_hi, fx_lo, fx_hi, ys_lo, ys_hi, xs_lo, xs_hi)[0]
+        *prepared, fx_lo, fx_hi, xs_lo, xs_hi)[0]
     pop = call(
         patch_kernel, [sds(19, N, N, Z)], "patch", "v" * 9, out_specs="h",
         scratch=[VM((19, N, N, Z), F32), pltpu.SemaphoreType.DMA((19,))], mib=16, moved=10000000)(

time: 62 us -> 58 us (0.935)
  Pallas kernels: 17.7 us -> 15.5 us
  waiting for transfers between devices: 18.4 us -> 17.2 us
    pallas_call x2 -> x4, Pallas kernels: 8.04 us -> 6.11 us  [the longest x1 2.09 us: body(): call(sweep_kernel, [cube], 'sweep', 'v' * 8, scratch=[VM((N + 2 * RING, N...]
    ppermute x6, waiting for transfers between devices: 12.6 us -> 11.1 us  [swap(): lax.ppermute(jnp.where(even, lo, hi), axis, [(i, (i - 1 + 2 * (i % 2)) %...]
  transfers between devices with their start and end apart: 12 -> 12, of which waited for: 6 -> 6; matrix products, arithmetic and copies ran while one was open for 0% -> 0% of each run, Pallas kernels for 11% -> 16%
where the time goes in v2:
time: 58 us; the launch traced here: 57.8 us
  starting transfers between devices  22 us (38%)
  waiting for transfers between devices  17.2 us (30%)
  Pallas kernels  15.5 us (27%)
  local copies, waits for them, and re-layouts  2 us (3%)
  between operations  0.83 us (1%)
    ppermute x6, starting transfers between devices, swap(): lax.ppermute(jnp.where(even, lo, hi), axis, [(i, (i - 1 + 2 * (i % 2)) %...  22 us
    ppermute x6, waiting for transfers between devices, swap(): lax.ppermute(jnp.where(even, lo, hi), axis, [(i, (i - 1 + 2 * (i % 2)) %...  11.1 us
    ppermute x6, waiting for transfers between devices, swap(): lax.ppermute(jnp.where(even, hi, lo), axis, [(i, i + 1 - 2 * (i % 2)) for...  6.09 us
    pallas_call x1, Pallas kernels, body(): call(collide_kernel, [sds(19, N, N, Z), sds(4, N, N, Z)] + [sds(19, N, Z)...  4.29 us
    pallas_call x1, Pallas kernels, body(): call(patch_kernel, [sds(19, N, N, Z)], 'patch', 'v' * 9, out_specs='h', s...  2.46 us
    pallas_call x1, Pallas kernels, body(): call(sweep_kernel, [cube], 'sweep', 'v' * 8, scratch=[VM((N + 2 * RING, N...  2.09 us
    unnamed x8, local copies, waits for them, and re-layouts  2 us
    pallas_call x1, Pallas kernels, body(): call(diffuse_kernel, [pair, sds(2, N + 1, N, Z), pair, sds(2, N, Z), pair...  1.99 us
  transfers between devices with their start and end apart: 12, of which 6 were waited for; matrix products, arithmetic and copies ran while one was open for 0% of the time, Pallas kernels for 16%

profile of v2, /device:TPU:7, one launch (start us, length us, event | category | flops | bytes accessed | tf_op | source)
XLA Modules:
  0.0 57.8 jit_solution(12125322052991600326)
XLA Ops:
  0.6 1.6 %faces.1 = (f32[9,16,256]{2,1,0:T(8,128)S(1)}, f32[9,16,256]{2,1,0:T(8,128)S(1)}, f32[9,16,256]{2,1,0:T(8,128)S(1)}, f32[9,16,256]{2,1,0:T(8,128)S(1)}, f32[16,16,256]{2,1,0:T(8,128)S(1)}) custom-call(f32[16,16,256]{2,1,0:T(8,128)} %pot.3, f32[2,16,16,256]{3,2,1,0:T(8,128)} %conc.1, f32[16,16,256]{2,1,0:T(8,128)} %mob_h.1, s32[16,16,256]{2,1,0:T(8,128)} %solid_h.1), custom_call_target="tpu_custom_call" | custom-call | bytes 2600000 | tf_op jit(solution)/shard_map/faces/pallas_call | solution.py:646
  2.3 8.3 %collective-permute-start = (f32[9,16,256]{2,1,0:T(8,128)S(1)}, f32[9,16,256]{2,1,0:T(8,128)S(1)}, u32[]{:S(2)}, u32[]{:S(2)}) collective-permute-start(f32[9,16,256]{2,1,0:T(8,128)S(1)} %get-tuple-element.84), channel_id=1, source_target_pairs={{0,240},{16,32},{32,16},{48,64},{64,48},{80,96},{96,80},{112,128},... | collective-permute-start | bytes 442376 | tf_op jit(solution)/shard_map/ppermute | solution.py:639
  10.6 0.0 collective-permute-start.1
  10.6 1.2 %collective-permute-start.2 = (f32[9,16,256]{2,1,0:T(8,128)S(1)}, f32[9,16,256]{2,1,0:T(8,128)S(1)}, u32[]{:S(2)}, u32[]{:S(2)}) collective-permute-start(f32[9,16,256]{2,1,0:T(8,128)S(1)} %get-tuple-element.80), channel_id=1, source_target_pairs={{0,15},{1,2},{2,1},{3,4},{4,3},{5,6},{6,5},{7,8},{8,7},{9,10},{10,... | collective-permute-start | bytes 442376 | tf_op jit(solution)/shard_map/ppermute | solution.py:639
  11.8 0.0 collective-permute-start.3
  11.9 1.0 %copy-done = f32[2,16,16,256]{3,2,1,0:T(8,128)S(1)} copy-done((f32[2,16,16,256]{3,2,1,0:T(8,128)S(1)}, f32[2,16,16,256]{3,2,1,0:T(8,128)}, u32[]{:S(2)}) %copy-start) | copy-done | bytes 524312
  12.9 0.9 %copy-done.1 = f32[16,16,256]{2,1,0:T(8,128)S(1)} copy-done((f32[16,16,256]{2,1,0:T(8,128)S(1)}, f32[16,16,256]{2,1,0:T(8,128)}, u32[]{:S(2)}) %copy-start.1) | copy-done | bytes 262168
  13.8 4.3 %collide.1 = (f32[19,16,16,256]{3,2,1,0:T(8,128)S(1)}, f32[4,16,16,256]{3,2,1,0:T(8,128)S(1)}, f32[19,16,256]{2,1,0:T(8,128)S(1)}, f32[19,16,256]{2,1,0:T(8,128)...) custom-call(f32[19,16,16,256]{3,2,1,0:T(8,128)} %pops.1, f32[16,16,256]{2,1,0:T(8,128)S(1)} %copy-done.1, ...), custom_call_target="tpu_custom_call" | custom-call | flops 20000000 | bytes 14000000 | tf_op jit(solution)/shard_map/collide/pallas_call | solution.py:654
  18.1 0.0 copy-start.2
  18.2 0.0 copy-start.3
  18.2 0.0 collective-permute-done.1
  18.2 0.0 collective-permute-done.3
  18.3 1.0 %edge.1 = (f32[4,16,16,256]{3,2,1,0:T(8,128)S(1)}, f32[19,16,256]{2,1,0:T(8,128)S(1)}, f32[19,16,256]{2,1,0:T(8,128)S(1)}, f32[19,16,256]{2,1,0:T(8,128)S(1)}, f...) custom-call(f32[19,16,256]{2,1,0:T(8,128)S(1)} %get-tuple-element.42.px_lo, ...), custom_call_target="tpu_custom_call" | custom-call | bytes 3000000 | tf_op jit(solution)/shard_map/edge/pallas_call | solution.py:659
  19.3 2.8 %collective-permute-start.4 = (f32[120,256]{1,0:T(8,128)S(1)}, f32[120,256]{1,0:T(8,128)S(1)}, u32[]{:S(2)}, u32[]{:S(2)}) collective-permute-start(f32[120,256]{1,0:T(8,128)S(1)} %get-tuple-element.96), channel_id=1, source_target_pairs={{0,15},{1,2},{2,1},{3,4},{4,3},{5,6},{6,5},{7,8},{8,7},{9,10},{10,... | collective-permute-start | bytes 368648 | tf_op jit(solution)/shard_map/ppermute | solution.py:639
  22.1 0.0 collective-permute-start.5
  22.1 3.7 %collective-permute-done.4 = f32[120,256]{1,0:T(8,128)S(1)} collective-permute-done((f32[120,256]{1,0:T(8,128)S(1)}, f32[120,256]{1,0:T(8,128)S(1)}, u32[]{:S(2)}, u32[]{:S(2)}) %collective-permute-start.4) | collective-permute-done | bytes 122912 | tf_op jit(solution)/shard_map/ppermute | solution.py:639
  25.8 0.0 collective-permute-done.5
  25.9 4.4 %collective-permute-start.6 = (f32[120,256]{1,0:T(8,128)S(1)}, f32[120,256]{1,0:T(8,128)S(1)}, u32[]{:S(2)}, u32[]{:S(2)}) collective-permute-start(f32[120,256]{1,0:T(8,128)S(1)} %get-tuple-element.92), channel_id=1, source_target_pairs={{0,240},{16,32},{32,16},{48,64},{64,48},{80,96},{96,80},{112,128},... | collective-permute-start | bytes 368648 | tf_op jit(solution)/shard_map/ppermute | solution.py:639
  30.3 2.0 %diffuse.1 = (f32[2,16,16,256]{3,2,1,0:T(8,128)S(1)}, f32[2,17,16,256]{3,2,1,0:T(8,128)S(1)}, f32[2,16,16,256]{3,2,1,0:T(8,128)S(1)}, f32[2,16,256]{2,1,0:T(8,12...) custom-call(f32[4]{0:T(128)S(1)} %copy-done.3, s32[16,16,256]{2,1,0:T(8,128)S(1)} %copy-done.2, ...), custom_call_target="tpu_custom_call" | custom-call | flops 10000000 | bytes 6000000 | tf_op jit(solution)/shard_map/diffuse/pallas_call | solution.py:668
  32.3 1.2 %collective-permute-done.6 = f32[120,256]{1,0:T(8,128)S(1)} collective-permute-done((f32[120,256]{1,0:T(8,128)S(1)}, f32[120,256]{1,0:T(8,128)S(1)}, u32[]{:S(2)}, u32[]{:S(2)}) %collective-permute-start.6) | collective-permute-done | bytes 122912 | tf_op jit(solution)/shard_map/ppermute | solution.py:639
  33.5 3.0 %collective-permute-done.7 = f32[120,256]{1,0:T(8,128)S(1)} collective-permute-done((f32[120,256]{1,0:T(8,128)S(1)}, f32[120,256]{1,0:T(8,128)S(1)}, u32[]{:S(2)}, u32[]{:S(2)}) %collective-permute-start.7) | collective-permute-done | bytes 122912 | tf_op jit(solution)/shard_map/ppermute | solution.py:638
  36.5 1.8 %transport.1 = (f32[2,16,16,256]{3,2,1,0:T(8,128)}, f32[16,16,256]{2,1,0:T(8,128)S(1)}, f32[5,16,256]{2,1,0:T(8,128)S(1)}, f32[5,16,256]{2,1,0:T(8,128)S(1)}) custom-call(f32[4,16,16,256]{3,2,1,0:T(8,128)S(1)} %get-tuple-element.57.mom, f32[16,16,256]{2,1,0:T(8,128)S(1)} %get-tuple-element.40.cond, f32[2,16,16,256]{3,2,1,0:T(8,128)S(1)} %get-tuple-element.61.base, ...), custom_call_target="tpu_custom_call" | custom-call | flops 5000000 | bytes 4000000 | tf_op jit(solution)/shard_map/transport/pallas_call | solution.py:672
  38.3 2.1 %collective-permute-start.8 = (f32[5,16,256]{2,1,0:T(8,128)S(1)}, f32[5,16,256]{2,1,0:T(8,128)S(1)}, u32[]{:S(2)}, u32[]{:S(2)}) collective-permute-start(f32[5,16,256]{2,1,0:T(8,128)S(1)} %get-tuple-element.100), channel_id=1, source_target_pairs={{0,15},{1,2},{2,1},{3,4},{4,3},{5,6},{6,5},{7,8},{8,7},{9,10},{10,... | collective-permute-start | bytes 245768 | tf_op jit(solution)/shard_map/ppermute | solution.py:639
  40.4 3.9 %collective-permute-done.8 = f32[5,16,256]{2,1,0:T(8,128)S(1)} collective-permute-done((f32[5,16,256]{2,1,0:T(8,128)S(1)}, f32[5,16,256]{2,1,0:T(8,128)S(1)}, u32[]{:S(2)}, u32[]{:S(2)}) %collective-permute-start.8) | collective-permute-done | bytes 81952 | tf_op jit(solution)/shard_map/ppermute | solution.py:639
  44.4 0.1 pack_src.1
  44.5 3.1 %collective-permute-start.10 = (f32[136,256]{1,0:T(8,128)S(1)}, f32[136,256]{1,0:T(8,128)S(1)}, u32[]{:S(2)}, u32[]{:S(2)}) collective-permute-start(f32[136,256]{1,0:T(8,128)S(1)} %get-tuple-element.88), channel_id=1, source_target_pairs={{0,240},{16,32},{32,16},{48,64},{64,48},{80,96},{96,80},{112,128},... | collective-permute-start | bytes 417800 | tf_op jit(solution)/shard_map/ppermute | solution.py:639
  47.6 0.0 collective-permute-start.11
  47.6 2.5 %patch.1 = f32[19,16,16,256]{3,2,1,0:T(8,128)} custom-call(f32[19,16,16,256]{3,2,1,0:T(8,128)S(1)} %get-tuple-element.41.buf, f32[19,16,256]{2,1,0:T(8,128)S(1)} %get-tuple-element.51.ex_lo, f32[19,16,256]{2,1,0:T(8,128)S(1)} %get-tuple-element.52.ex_hi, f32[19,16,256]{2,1,0:T(8,128)S(1)} %get-tuple-element.53.ey_lo, ...), custom_call_target="tpu_custom_call" | custom-call | bytes 10000000 | tf_op jit(solution)/shard_map/patch/pallas_call | solution.py:688
  50.1 0.3 prepare.1
  50.4 2.2 %collective-permute-done.10 = f32[136,256]{1,0:T(8,128)S(1)} collective-permute-done((f32[136,256]{1,0:T(8,128)S(1)}, f32[136,256]{1,0:T(8,128)S(1)}, u32[]{:S(2)}, u32[]{:S(2)}) %collective-permute-start.10) | collective-permute-done | bytes 139296 | tf_op jit(solution)/shard_map/ppermute | solution.py:639
  52.6 3.1 %collective-permute-done.11 = f32[136,256]{1,0:T(8,128)S(1)} collective-permute-done((f32[136,256]{1,0:T(8,128)S(1)}, f32[136,256]{1,0:T(8,128)S(1)}, u32[]{:S(2)}, u32[]{:S(2)}) %collective-permute-start.11) | collective-permute-done | bytes 139296 | tf_op jit(solution)/shard_map/ppermute | solution.py:638
  55.7 2.1 %sweep.1 = f32[16,16,256]{2,1,0:T(8,128)} custom-call(f32[8,32,256]{2,1,0:T(8,128)S(1)} %get-tuple-element.71.even_in, f32[8,32,256]{2,1,0:T(8,128)S(1)} %get-tuple-element.72.odd_in, f32[8,32,256]{2,1,0:T(8,128)S(1)} %get-tuple-element.73.s_even_in, f32[8,32,256]{2,1,0:T(8,128)S(1)} %get-tuple-element.74.s_odd_in, ...), custom_call_target="tpu_custom_call" | custom-call | flops 20000000 | bytes 4000000 | tf_op jit(solution)/shard_map/sweep/pallas_call | solution.py:684
  (22 shorter events, 0.3 us)
Async XLA Ops:
  2.3 15.9 %collective-permute-start = (f32[9,16,256]{2,1,0:T(8,128)S(1)}, f32[9,16,256]{2,1,0:T(8,128)S(1)}, u32[]{:S(2)}, u32[]{:S(2)}) collective-permute-start(f32[9,16,256]{2,1,0:T(8,128)S(1)} %get-tuple-element.84), channel_id=1, source_target_pairs={{0,240},{16,32},{32,16},{48,64},{64,48},{80,96},{96,80},{112,128},... | collective-permute-start | bytes 442376 | tf_op jit(solution)/shard_map/ppermute | solution.py:639
  10.6 7.6 %collective-permute-start.1 = (f32[9,16,256]{2,1,0:T(8,128)S(1)}, f32[9,16,256]{2,1,0:T(8,128)S(1)}, u32[]{:S(2)}, u32[]{:S(2)}) collective-permute-start(f32[9,16,256]{2,1,0:T(8,128)S(1)} %get-tuple-element.83), channel_id=1, source_target_pairs={{0,16},{16,0},{32,48},{48,32},{64,80},{80,64},{96,112},{112,96},{1... | collective-permute-start | bytes 442376 | tf_op jit(solution)/shard_map/ppermute | solution.py:638
  10.6 7.6 %collective-permute-start.2 = (f32[9,16,256]{2,1,0:T(8,128)S(1)}, f32[9,16,256]{2,1,0:T(8,128)S(1)}, u32[]{:S(2)}, u32[]{:S(2)}) collective-permute-start(f32[9,16,256]{2,1,0:T(8,128)S(1)} %get-tuple-element.80), channel_id=1, source_target_pairs={{0,15},{1,2},{2,1},{3,4},{4,3},{5,6},{6,5},{7,8},{8,7},{9,10},{10,... | collective-permute-start | bytes 442376 | tf_op jit(solution)/shard_map/ppermute | solution.py:639
  11.8 6.4 %collective-permute-start.3 = (f32[9,16,256]{2,1,0:T(8,128)S(1)}, f32[9,16,256]{2,1,0:T(8,128)S(1)}, u32[]{:S(2)}, u32[]{:S(2)}) collective-permute-start(f32[9,16,256]{2,1,0:T(8,128)S(1)} %get-tuple-element.79), channel_id=1, source_target_pairs={{0,1},{1,0},{2,3},{3,2},{4,5},{5,4},{6,7},{7,6},{8,9},{9,8},{10,11... | collective-permute-start | bytes 442376 | tf_op jit(solution)/shard_map/ppermute | solution.py:638
  11.9 1.0 %copy-start = (f32[2,16,16,256]{3,2,1,0:T(8,128)S(1)}, f32[2,16,16,256]{3,2,1,0:T(8,128)}, u32[]{:S(2)}) copy-start(f32[2,16,16,256]{3,2,1,0:T(8,128)} %conc.1) | copy-start | bytes 1572868
  12.9 0.9 %copy-start.1 = (f32[16,16,256]{2,1,0:T(8,128)S(1)}, f32[16,16,256]{2,1,0:T(8,128)}, u32[]{:S(2)}) copy-start(f32[16,16,256]{2,1,0:T(8,128)} %pot.3) | copy-start | bytes 786436
  18.1 12.1 %copy-start.2 = (s32[16,16,256]{2,1,0:T(8,128)S(1)}, s32[16,16,256]{2,1,0:T(8,128)}, u32[]{:S(2)}) copy-start(s32[16,16,256]{2,1,0:T(8,128)} %classes_h.1) | copy-start | bytes 786436
  18.2 12.1 %copy-start.3 = (f32[4]{0:T(128)S(1)}, f32[4]{0:T(128)}, u32[]{:S(2)}) copy-start(f32[4]{0:T(128)} %charge.1) | copy-start | bytes 52
  19.3 6.5 %collective-permute-start.4 = (f32[120,256]{1,0:T(8,128)S(1)}, f32[120,256]{1,0:T(8,128)S(1)}, u32[]{:S(2)}, u32[]{:S(2)}) collective-permute-start(f32[120,256]{1,0:T(8,128)S(1)} %get-tuple-element.96), channel_id=1, source_target_pairs={{0,15},{1,2},{2,1},{3,4},{4,3},{5,6},{6,5},{7,8},{8,7},{9,10},{10,... | collective-permute-start | bytes 368648 | tf_op jit(solution)/shard_map/ppermute | solution.py:639
  22.1 3.7 %collective-permute-start.5 = (f32[120,256]{1,0:T(8,128)S(1)}, f32[120,256]{1,0:T(8,128)S(1)}, u32[]{:S(2)}, u32[]{:S(2)}) collective-permute-start(f32[120,256]{1,0:T(8,128)S(1)} %get-tuple-element.95), channel_id=1, source_target_pairs={{0,1},{1,0},{2,3},{3,2},{4,5},{5,4},{6,7},{7,6},{8,9},{9,8},{10,11... | collective-permute-start | bytes 368648 | tf_op jit(solution)/shard_map/ppermute | solution.py:638
  25.9 7.6 %collective-permute-start.6 = (f32[120,256]{1,0:T(8,128)S(1)}, f32[120,256]{1,0:T(8,128)S(1)}, u32[]{:S(2)}, u32[]{:S(2)}) collective-permute-start(f32[120,256]{1,0:T(8,128)S(1)} %get-tuple-element.92), channel_id=1, source_target_pairs={{0,240},{16,32},{32,16},{48,64},{64,48},{80,96},{96,80},{112,128},... | collective-permute-start | bytes 368648 | tf_op jit(solution)/shard_map/ppermute | solution.py:639
  30.3 6.2 %collective-permute-start.7 = (f32[120,256]{1,0:T(8,128)S(1)}, f32[120,256]{1,0:T(8,128)S(1)}, u32[]{:S(2)}, u32[]{:S(2)}) collective-permute-start(f32[120,256]{1,0:T(8,128)S(1)} %get-tuple-element.91), channel_id=1, source_target_pairs={{0,16},{16,0},{32,48},{48,32},{64,80},{80,64},{96,112},{112,96},{1... | collective-permute-start | bytes 368648 | tf_op jit(solution)/shard_map/ppermute | solution.py:638
  38.3 6.1 %collective-permute-start.8 = (f32[5,16,256]{2,1,0:T(8,128)S(1)}, f32[5,16,256]{2,1,0:T(8,128)S(1)}, u32[]{:S(2)}, u32[]{:S(2)}) collective-permute-start(f32[5,16,256]{2,1,0:T(8,128)S(1)} %get-tuple-element.100), channel_id=1, source_target_pairs={{0,15},{1,2},{2,1},{3,4},{4,3},{5,6},{6,5},{7,8},{8,7},{9,10},{10,... | collective-permute-start | bytes 245768 | tf_op jit(solution)/shard_map/ppermute | solution.py:639
  40.4 3.9 %collective-permute-start.9 = (f32[5,16,256]{2,1,0:T(8,128)S(1)}, f32[5,16,256]{2,1,0:T(8,128)S(1)}, u32[]{:S(2)}, u32[]{:S(2)}) collective-permute-start(f32[5,16,256]{2,1,0:T(8,128)S(1)} %get-tuple-element.99), channel_id=1, source_target_pairs={{0,1},{1,0},{2,3},{3,2},{4,5},{5,4},{6,7},{7,6},{8,9},{9,8},{10,11... | collective-permute-start | bytes 245768 | tf_op jit(solution)/shard_map/ppermute | solution.py:638
  44.5 8.1 %collective-permute-start.10 = (f32[136,256]{1,0:T(8,128)S(1)}, f32[136,256]{1,0:T(8,128)S(1)}, u32[]{:S(2)}, u32[]{:S(2)}) collective-permute-start(f32[136,256]{1,0:T(8,128)S(1)} %get-tuple-element.88), channel_id=1, source_target_pairs={{0,240},{16,32},{32,16},{48,64},{64,48},{80,96},{96,80},{112,128},... | collective-permute-start | bytes 417800 | tf_op jit(solution)/shard_map/ppermute | solution.py:639
  47.6 8.0 %collective-permute-start.11 = (f32[136,256]{1,0:T(8,128)S(1)}, f32[136,256]{1,0:T(8,128)S(1)}, u32[]{:S(2)}, u32[]{:S(2)}) collective-permute-start(f32[136,256]{1,0:T(8,128)S(1)} %get-tuple-element.87), channel_id=1, source_target_pairs={{0,16},{16,0},{32,48},{48,32},{64,80},{80,64},{96,112},{112,96},{1... | collective-permute-start | bytes 417800 | tf_op jit(solution)/shard_map/ppermute | solution.py:638

commit v3 on v2

--- a/solution.py
+++ b/solution.py
@@ -98,7 +98,7 @@
             gy_lo[RING + q, here, :] = v[x, 0:1, :]
         return carry
 
-    lax.fori_loop(0, N, step, 0, unroll=2)
+    lax.fori_loop(0, N, step, 0, unroll=True)
     for x, face in ((N - 1, gx_hi), (0, gx_lo)):
         for r in range(RING):
             face[r] = pot[abs(x - r)]
@@ -219,7 +219,7 @@
 
 
 def edge_kernel(px_lo, px_hi, pr_lo, pr_hi, gx_lo, gx_hi, gy_lo, gy_hi, fx_lo, fx_hi, fy_lo, fy_hi, mom0,
-                mom, ex_lo, ex_hi, ey_lo, ey_hi, yb_lo, yb_hi):
+                mom, ex_lo, ex_hi, ey_lo, ey_hi, yb_lo, yb_hi, xb_lo, xb_hi):
     row = rows()
     inner = (row >= 1) & (row <= N - 2)
     keep = {0: None, 1: row >= 1, -1: row <= N - 2}
@@ -297,6 +297,11 @@
         yb_hi[k + 1:k + 2, :] = row_of(g[2], N - 1)
         yb_lo[k:k + 1, :] = row_of(g[0], 0)
         yb_lo[k + 1:k + 2, :] = row_of(g[2], 0)
+    for ex, xb, slots, at in ((ex_hi, xb_hi, XPOS, N - 1), (ex_lo, xb_lo, XNEG, 0)):
+        for q, i in enumerate(slots):
+            xb[q * N:(q + 1) * N, :] = ex[i]
+        for q, m in ((5, 0), (6, 1)):
+            xb[q * N:(q + 1) * N, :] = mom[m, at]
     for x in range(N):
         for q, m in ((5, 0), (6, 2)):
             yb_lo[q * N + x:q * N + x + 1, :] = mom[m, x, 0:1, :]
@@ -324,33 +329,36 @@
     return below, (total, s9 - s8, -total, s18 - s16)
 
 
-def corner_kernel(ex_lo, ex_hi, yh_lo, yh_hi, yb_lo, yb_hi, mom, xb_lo, xb_hi):
-    row = rows()
+def corner_kernel(yh_lo, yh_hi, yb_lo, yb_hi, xl_lo, xl_hi):
     below, above = y_terms(yh_lo, yh_hi)
-    for ex, xb, slots, at in ((ex_hi, xb_hi, XPOS, N - 1), (ex_lo, xb_lo, XNEG, 0)):
-        for q, i in enumerate(slots):
-            v = ex[i]
-            if C[i][1] == 1:
-                v = jnp.where(row == 0, spread(line(yh_lo, YPOS.index(i), at)), v)
-            elif C[i][1] == -1:
-                v = jnp.where(row == N - 1, spread(line(yh_hi, YNEG.index(i), at)), v)
-            xb[q * N:(q + 1) * N, :] = v
-        for q, m in ((5, 0), (6, 1)):
-            v = mom[m, at] + jnp.where(row == 0, spread(row_of(below[m], at)), 0.0)
-            xb[q * N:(q + 1) * N, :] = v + jnp.where(row == N - 1, spread(row_of(above[m], at)), 0.0)
-        c = 1 if at else -1
+    for xl, at, up_slot, down_slot in ((xl_hi, N - 1, 7, 9), (xl_lo, 0, 10, 8)):
         k = LINE if at else LINE + 2
-        down = line(yb_lo, YNEG.index(9 if c == 1 else 8), at)
-        up = line(yb_hi, YPOS.index(7 if c == 1 else 10), at)
-        xb[LINE:LINE + 1, :] = yh_lo[k:k + 1, :] + down
-        xb[LINE + 1:LINE + 2, :] = yh_lo[k + 1:k + 2, :] - down
-        xb[LINE + 2:LINE + 3, :] = yh_hi[k:k + 1, :] + up
-        xb[LINE + 3:LINE + 4, :] = yh_hi[k + 1:k + 2, :] + up
-        xb[LINE + 4:, :] = jnp.zeros((4, Z), F32)
+        down = line(yb_lo, YNEG.index(down_slot), at)
+        up = line(yb_hi, YPOS.index(up_slot), at)
+        listed = (line(yh_lo, YPOS.index(up_slot), at), line(yh_hi, YNEG.index(down_slot), at),
+                  row_of(below[0], at), row_of(above[0], at), row_of(below[1], at), row_of(above[1], at),
+                  yh_lo[k:k + 1, :] + down, yh_lo[k + 1:k + 2, :] - down, yh_hi[k:k + 1, :] + up, yh_hi[k + 1:k + 2, :] + up)
+        for q, v in enumerate(listed):
+            xl[q:q + 1, :] = v
+        xl[len(listed):, :] = jnp.zeros((N - len(listed), Z), F32)
+
+
+def with_lines(v, xl, i):
+    if C[i][1] == 1:
+        return jnp.where(rows() == 0, spread(xl[0:1, :]), v)
+    if C[i][1] == -1:
+        return jnp.where(rows() == N - 1, spread(xl[1:2, :]), v)
+    return v
+
+
+def plus_lines(v, low, high):
+    v = v + jnp.where(rows() == 0, spread(low), 0.0)
+    return v + jnp.where(rows() == N - 1, spread(high), 0.0)
 
 
 def transport_kernel(mom, cond, base, wx, wy, wy_low, wz, wall, yh_lo, yh_hi, xh_lo, xh_hi, yb_lo, yb_hi, xb_lo, xb_hi,
-                     fx_lo, fx_hi, fy_lo, fy_hi, conc_out, src, sy_lo, sy_hi, drift, lines, low, dy_hi, own_dy):
+                     xl_lo, xl_hi, ol_lo, ol_hi, fx_lo, fx_hi, fy_lo, fy_hi,
+                     conc_out, src, sy_lo, sy_hi, sx_lo, sx_hi, drift, lines, low, dy_hi, own_dy):
     row = rows()
     below, above = y_terms(yh_lo, yh_hi)
     for m in range(4):
@@ -374,10 +382,10 @@
         drift[2, x] = full(3) * scale
         own_dy[here, :] = row_of(v, 0)
 
-    a = [plane(xh_lo, q) for q in range(5)]
+    a = [with_lines(plane(xh_lo, q), xl_lo, i) for q, i in enumerate(XPOS)]
     total = a[0] + a[1] + a[2] + a[3] + a[4]
     step(0, (total, total, a[1] - a[2], a[3] - a[4]))
-    b = [plane(xh_hi, q) for q in range(5)]
+    b = [with_lines(plane(xh_hi, q), xl_hi, i) for q, i in enumerate(XNEG)]
     total = b[0] + b[1] + b[2] + b[3] + b[4]
     step(N - 1, (total, -total, b[2] - b[1], b[4] - b[3]))
 
@@ -390,27 +398,30 @@
     def velocity(conductance, density, momentum):
         return jnp.where(conductance > 0.0, momentum / density, 0.0)
 
-    def x_face(fx, xh, xb, sign):
+    def x_face(fx, xh, xl, xb, ol, sign):
         out = plane(xb, 0) + plane(xb, 1) + plane(xb, 2) + plane(xb, 3) + plane(xb, 4)
-        return velocity(fx[RING + 2], plane(xh, 5) + out, plane(xh, 6) + sign * out)
+        out = plus_lines(out, ol[0:1, :], ol[1:2, :])
+        density = plus_lines(plane(xh, 5), xl[2:3, :], xl[3:4, :])
+        momentum = plus_lines(plane(xh, 6), xl[4:5, :], xl[5:6, :])
+        return velocity(fx[RING + 2], density + out, momentum + sign * out)
 
     from_hi, from_lo = y_terms(yb_hi, yb_lo)
 
     def y_face(fy, yh, terms, k):
         density = plane(yh, 5) + terms[0]
         momentum = plane(yh, 6) + terms[2]
-        for xh, x in ((xh_lo, 0), (xh_hi, N - 1)):
-            density = density + jnp.where(row == x, spread(xh[k:k + 1, :]), 0.0)
-            momentum = momentum + jnp.where(row == x, spread(xh[k + 1:k + 2, :]), 0.0)
+        for xl, x in ((xl_lo, 0), (xl_hi, N - 1)):
+            density = density + jnp.where(row == x, spread(xl[k:k + 1, :]), 0.0)
+            momentum = momentum + jnp.where(row == x, spread(xl[k + 1:k + 2, :]), 0.0)
         return velocity(fy[RING + 2], density, momentum)
 
-    carried = y_face(fy_lo, yh_lo, from_lo, LINE) + own_dy[...]
+    carried = y_face(fy_lo, yh_lo, from_lo, 6) + own_dy[...]
     for s in range(2):
         low[s] = wy_low[s] * carried
-    dy_hi[...] = y_face(fy_hi, yh_hi, from_hi, LINE + 2)
-    carried = x_face(fx_lo, xh_lo, xb_lo, -1.0) + drift[0, 0]
+    dy_hi[...] = y_face(fy_hi, yh_hi, from_hi, 8)
+    carried = x_face(fx_lo, xh_lo, xl_lo, xb_lo, ol_lo, -1.0) + drift[0, 0]
     behind = [wx[s, 0] * carried for s in range(2)]
-    last = x_face(fx_hi, xh_hi, xb_hi, 1.0)
+    last = x_face(fx_hi, xh_hi, xl_hi, xb_hi, ol_hi, 1.0)
     for x in range(N):
         carried = drift[0, x] + (drift[0, x + 1] if x < N - 1 else last)
         ahead = [wx[s, x + 1] * carried for s in range(2)]
@@ -435,6 +446,21 @@
         for r in range(RING - 1):
             sy_lo[r, x:x + 1, :] = row_of(s_val, r)
             sy_hi[r, x:x + 1, :] = row_of(s_val, N - 1 - r)
+        if x < RING - 1:
+            sx_lo[x * N:(x + 1) * N, :] = s_val
+        if N - 1 - x < RING - 1:
+            sx_hi[(N - 1 - x) * N:(N - x) * N, :] = s_val
+    corner_rows(POT_ROWS, fy_lo, fy_hi, sx_lo, sx_hi)
+
+
+def corner_rows(listed, lo, hi, o_lo, o_hi):
+    for at, a, side, b in listed:
+        halo = hi if side else lo
+        o_hi[at:at + 1, :] = halo[b - 1, N - a:N - a + 1, :]
+        o_lo[at:at + 1, :] = halo[b - 1, a - 1:a, :]
+    end = listed[-1][0] + 1
+    for ref in (o_lo, o_hi):
+        ref[end:, :] = jnp.zeros((ref.shape[0] - end, Z), F32)
 
 
 def split(ext, a, b, pairs, shift):
@@ -456,7 +482,7 @@
         split(ext, a, b, range(N // 2), 0)
 
 
-def sweep_kernel(even_in, odd_in, s_even_in, s_odd_in, fx_lo, fx_hi, xs_lo, xs_hi, out, ext, even, odd, s_even, s_odd):
+def sweep_kernel(even_in, odd_in, s_even_in, s_odd_in, fx_lo, fx_hi, xs_lo, xs_hi, xc_lo, xc_hi, out, ext, even, odd, s_even, s_odd):
     mid = slice(OFF, OFF + N)
     top = RING + N
     half = (N + 2 * RING) // 2
@@ -470,16 +496,16 @@
         for k in range(N // 2):
             ref[k + 1 + RING // 2] = given[k]
     ends = list(range(RING // 2)) + list(range(RING // 2 + N // 2, half))
-    for x_lo, x_hi, depth, listed, a, b in (
-            (lambda r: fx_lo[r], lambda r: fx_hi[r], RING, POT_ROWS, even, odd),
-            (lambda r: plane(xs_lo, r), lambda r: plane(xs_hi, r), RING - 1, SRC_ROWS, s_even, s_odd)):
+    for x_lo, x_hi, depth, listed, c_lo, c_hi, a, b in (
+            (lambda r: fx_lo[r], lambda r: fx_hi[r], RING, POT_ROWS, xs_lo, xs_hi, even, odd),
+            (lambda r: plane(xs_lo, r), lambda r: plane(xs_hi, r), RING - 1, SRC_ROWS, xc_lo, xc_hi, s_even, s_odd)):
         for r in range(depth):
             ext[RING - 1 - r, mid] = x_lo(r)
             ext[top + r, mid] = x_hi(r)
         for at, a_ring, side, b_ring in listed:
             y = OFF + N + b_ring - 1 if side else OFF - b_ring
-            ext[RING - a_ring, y:y + 1, :] = xs_lo[at:at + 1, :]
-            ext[top + a_ring - 1, y:y + 1, :] = xs_hi[at:at + 1, :]
+            ext[RING - a_ring, y:y + 1, :] = c_lo[at:at + 1, :]
+            ext[top + a_ring - 1, y:y + 1, :] = c_hi[at:at + 1, :]
         split(ext, a, b, ends, 1)
 
     for h in range(6):
@@ -506,7 +532,7 @@
     lax.fori_loop(RING // 2 + 1, RING // 2 + N // 2 + 1, last, 0)
 
 
-def patch_kernel(buf, ex_lo, ex_hi, ey_lo, ey_hi, yh_lo, yh_hi, xh_lo, xh_hi, out, done, sems):
+def patch_kernel(buf, ex_lo, ex_hi, ey_lo, ey_hi, yh_lo, yh_hi, xh_lo, xh_hi, xl_lo, xl_hi, out, done, sems):
     row = rows()
     copies = []
     for i in range(19):
@@ -529,15 +555,15 @@
             done[i, src + cx] = halo(v, src)
             return carry
 
-        lax.fori_loop(1, N - 1, inner, 0, unroll=2)
+        lax.fori_loop(1, N - 1, inner, 0, unroll=True)
         if cx != -1:
             done[i, cx] = halo(ex_lo[i], 0)
         if cx != 1:
             done[i, N - 1 + cx] = halo(ex_hi[i], N - 1)
         if cx == 1:
-            done[i, 0] = plane(xh_lo, XPOS.index(i))
+            done[i, 0] = with_lines(plane(xh_lo, XPOS.index(i)), xl_lo, i)
         if cx == -1:
-            done[i, N - 1] = plane(xh_hi, XNEG.index(i))
+            done[i, N - 1] = with_lines(plane(xh_hi, XNEG.index(i)), xl_hi, i)
         copy = pltpu.make_async_copy(done.at[i], out.at[i], sems.at[i])
         copy.start()
         copies.append(copy)
@@ -613,23 +639,13 @@
     return listed
 
 
-SRC_ROWS = ring_rows((RING - 1) * N, RING - 1)
-POT_ROWS = ring_rows(SRC_ROWS[-1][0] + 1, RING)
-SRC_LEN = 136
-
-
-def pack_src_kernel(src, ys_lo, ys_hi, fy_lo, fy_hi, o_hi, o_lo):
-    for k in range(RING - 1):
-        o_hi[k * N:(k + 1) * N, :] = src[N - 1 - k]
-        o_lo[k * N:(k + 1) * N, :] = src[k]
-    for listed, lo, hi in ((SRC_ROWS, ys_lo, ys_hi), (POT_ROWS, fy_lo, fy_hi)):
-        for at, a, side, b in listed:
-            halo = hi if side else lo
-            o_hi[at:at + 1, :] = halo[b - 1, N - a:N - a + 1, :]
-            o_lo[at:at + 1, :] = halo[b - 1, a - 1:a, :]
-    end = POT_ROWS[-1][0] + 1
-    o_hi[end:, :] = jnp.zeros((SRC_LEN - end, Z), F32)
-    o_lo[end:, :] = jnp.zeros((SRC_LEN - end, Z), F32)
+SRC_ROWS = ring_rows(0, RING - 1)
+POT_ROWS = ring_rows((RING - 1) * N, RING)
+SRC_LEN = 24
+
+
+def pack_src_kernel(ys_lo, ys_hi, o_lo, o_hi):
+    corner_rows(SRC_ROWS, ys_lo, ys_hi, o_lo, o_hi)
 
 
 def swap(axis, hi, lo):
@@ -656,12 +672,13 @@
         scratch=[VM((19, N, N, Z), F32), VM((N, N, Z), F32), VM((2, N, N, Z), F32),
                  pltpu.SemaphoreType.DMA((chunks,)), pltpu.SemaphoreType.DMA((4,))],
         mib=43, flops=20000000, moved=14000000)(pops, pot, conc, cond)
-    mom, ex_lo, ex_hi, ey_lo, ey_hi, yb_lo, yb_hi = call(
-        edge_kernel, [sds(4, N, N, Z)] + [sds(19, N, Z)] * 4 + [msg, msg], "edge", "v" * 13, moved=3000000)(
+    mom, ex_lo, ex_hi, ey_lo, ey_hi, yb_lo, yb_hi, xb_lo, xb_hi = call(
+        edge_kernel, [sds(4, N, N, Z)] + [sds(19, N, Z)] * 4 + [msg, msg, sds(LINE, Z), sds(LINE, Z)], "edge", "v" * 13, moved=3000000)(
         px_lo, px_hi, pr_lo, pr_hi, gx_lo, gx_hi, gy_lo, gy_hi, fx_lo, fx_hi, fy_lo, fy_hi, mom)
     yh_lo, yh_hi = swap("gy", yb_hi, yb_lo)
-    xb_lo, xb_hi = call(corner_kernel, [msg, msg], "corner", "v" * 7)(ex_lo, ex_hi, yh_lo, yh_hi, yb_lo, yb_hi, mom)
     xh_lo, xh_hi = swap("gx", xb_hi, xb_lo)
+    ol_lo, ol_hi = call(corner_kernel, [sds(N, Z)] * 2, "corner", "vvvv")(yh_lo, yh_hi, yb_lo, yb_hi)
+    xl_lo, xl_hi = swap("gx", ol_hi, ol_lo)
     face = VM((N, Z), F32)
     fy_late, _ = lax.optimization_barrier((fy_lo, yh_lo))
     pair = sds(2, N, N, Z)
@@ -669,26 +686,27 @@
         diffuse_kernel, [pair, sds(2, N + 1, N, Z), pair, sds(2, N, Z), pair, cube], "diffuse", "sh" + "v" * 8,
         scratch=[VM((2, N, Z), F32), VM((N, N, Z), jnp.int32), pltpu.SemaphoreType.DMA], flops=10000000, moved=6000000)(
         charge, classes, cond, conc, pot, fx_lo, fx_hi, fy_late, fy_hi, gy_lo)
-    conc_out, src, sy_lo, sy_hi = call(
-        transport_kernel, [pair, cube, sds(RING - 1, N, Z), sds(RING - 1, N, Z)], "transport", "v" * 20,
+    conc_out, src, sy_lo, sy_hi, sx_lo, sx_hi = call(
+        transport_kernel, [pair, cube, sds(RING - 1, N, Z), sds(RING - 1, N, Z), sds(LINE, Z), sds(LINE, Z)], "transport", "v" * 24,
         scratch=[VM((3, N, N, Z), F32), VM((8, N, Z), F32), VM((2, N, Z), F32), face, face], flops=5000000, moved=4000000)(
         mom, cond, base, wx, wy, wy_low, wz, wall, yh_lo, yh_hi, xh_lo, xh_hi, yb_lo, yb_hi, xb_lo, xb_hi,
-        fx_lo, fx_hi, fy_lo, fy_hi)
+        xl_lo, xl_hi, ol_lo, ol_hi, fx_lo, fx_hi, fy_lo, fy_hi)
     ys_lo, ys_hi = swap("gy", sy_hi, sy_lo)
-    bs_hi, bs_lo = call(pack_src_kernel, [sds(SRC_LEN, Z)] * 2, "pack_src", "v" * 5)(src, ys_lo, ys_hi, fy_lo, fy_hi)
-    xs_lo, xs_hi = swap("gx", bs_hi, bs_lo)
+    xs_lo, xs_hi = swap("gx", sx_hi, sx_lo)
+    oc_lo, oc_hi = call(pack_src_kernel, [sds(SRC_LEN, Z)] * 2, "pack_src", "vv")(ys_lo, ys_hi)
+    xc_lo, xc_hi = swap("gx", oc_hi, oc_lo)
     packed = VM(((N + 2 * RING) // 2 + 2, N + 2 * OFF, Z), F32)
     prepared = call(
         prepare_kernel, [sds(N // 2, N + 2 * OFF, Z)] * 4, "prepare", "v" * 6,
         scratch=[VM((N, N + 2 * OFF, Z), F32)], flops=1000000, moved=4000000)(pot, src, fy_lo, fy_hi, ys_lo, ys_hi)
     potential_out = call(
-        sweep_kernel, [cube], "sweep", "v" * 8,
+        sweep_kernel, [cube], "sweep", "v" * 10,
         scratch=[VM((N + 2 * RING, N + 2 * OFF, Z), F32)] + [packed] * 4, flops=20000000, moved=4000000)(
-        *prepared, fx_lo, fx_hi, xs_lo, xs_hi)[0]
+        *prepared, fx_lo, fx_hi, xs_lo, xs_hi, xc_lo, xc_hi)[0]
     pop = call(
-        patch_kernel, [sds(19, N, N, Z)], "patch", "v" * 9, out_specs="h",
+        patch_kernel, [sds(19, N, N, Z)], "patch", "v" * 11, out_specs="h",
         scratch=[VM((19, N, N, Z), F32), pltpu.SemaphoreType.DMA((19,))], mib=16, moved=10000000)(
-        buf, ex_lo, ex_hi, ey_lo, ey_hi, yh_lo, yh_hi, xh_lo, xh_hi)[0]
+        buf, ex_lo, ex_hi, ey_lo, ey_hi, yh_lo, yh_hi, xh_lo, xh_hi, xl_lo, xl_hi)[0]
     return (pop, conc_out, potential_out)
 
 

time: 58 us -> 59.9 us (1.033)
  starting transfers between devices: 22 us -> 28.3 us
  waiting for transfers between devices: 17.2 us -> 12.7 us
    ppermute x6 -> x8, starting transfers between devices: 22 us -> 28 us  [swap(): lax.ppermute(jnp.where(even, lo, hi), axis, [(i, (i - 1 + 2 * (i % 2)) %...]
    ppermute x6 -> x8, waiting for transfers between devices: 11.1 us -> 7.21 us  [swap(): lax.ppermute(jnp.where(even, lo, hi), axis, [(i, (i - 1 + 2 * (i % 2)) %...]
    ppermute x6 -> x8, waiting for transfers between devices: 6.09 us -> 5.45 us  [swap(): lax.ppermute(jnp.where(even, hi, lo), axis, [(i, i + 1 - 2 * (i % 2)) for...]
  transfers between devices with their start and end apart: 12 -> 16, of which waited for: 6 -> 5; matrix products, arithmetic and copies ran while one was open for 0% -> 0% of each run, Pallas kernels for 16% -> 15%
where the time goes in v3:
time: 59.9 us; the launch traced here: 59.5 us
  starting transfers between devices  28.3 us (47%)
  Pallas kernels  15.4 us (26%)
  waiting for transfers between devices  12.7 us (21%)
  local copies, waits for them, and re-layouts  2 us (3%)
  between operations  0.91 us (2%)
    ppermute x8, starting transfers between devices, swap(): lax.ppermute(jnp.where(even, lo, hi), axis, [(i, (i - 1 + 2 * (i % 2)) %...  28 us
    ppermute x8, waiting for transfers between devices, swap(): lax.ppermute(jnp.where(even, lo, hi), axis, [(i, (i - 1 + 2 * (i % 2)) %...  7.21 us
    ppermute x8, waiting for transfers between devices, swap(): lax.ppermute(jnp.where(even, hi, lo), axis, [(i, i + 1 - 2 * (i % 2)) for...  5.45 us
    pallas_call x1, Pallas kernels, body(): call(collide_kernel, [sds(19, N, N, Z), sds(4, N, N, Z)] + [sds(19, N, Z)...  4.29 us
    pallas_call x1, Pallas kernels, body(): call(patch_kernel, [sds(19, N, N, Z)], 'patch', 'v' * 11, out_specs='h',...  2.43 us
    pallas_call x1, Pallas kernels, body(): call(sweep_kernel, [cube], 'sweep', 'v' * 10, scratch=[VM((N + 2 * RING,...  2.09 us
    unnamed x8, local copies, waits for them, and re-layouts  2 us
    pallas_call x1, Pallas kernels, body(): call(diffuse_kernel, [pair, sds(2, N + 1, N, Z), pair, sds(2, N, Z), pair...  1.99 us
  transfers between devices with their start and end apart: 16, of which 5 were waited for; matrix products, arithmetic and copies ran while one was open for 0% of the time, Pallas kernels for 15%

profile of v3, /device:TPU:7, one launch (start us, length us, event | category | flops | bytes accessed | tf_op | source)
XLA Modules:
  0.0 59.5 jit_solution(9101533044395549079)
XLA Ops:
  0.6 1.5 %faces.1 = (f32[9,16,256]{2,1,0:T(8,128)S(1)}, f32[9,16,256]{2,1,0:T(8,128)S(1)}, f32[9,16,256]{2,1,0:T(8,128)S(1)}, f32[9,16,256]{2,1,0:T(8,128)S(1)}, f32[16,16,256]{2,1,0:T(8,128)S(1)}) custom-call(f32[16,16,256]{2,1,0:T(8,128)} %pot.3, f32[2,16,16,256]{3,2,1,0:T(8,128)} %conc.1, f32[16,16,256]{2,1,0:T(8,128)} %mob_h.1, s32[16,16,256]{2,1,0:T(8,128)} %solid_h.1), custom_call_target="tpu_custom_call" | custom-call | bytes 2600000 | tf_op jit(solution)/shard_map/faces/pallas_call | solution.py:662
  2.2 8.3 %collective-permute-start = (f32[9,16,256]{2,1,0:T(8,128)S(1)}, f32[9,16,256]{2,1,0:T(8,128)S(1)}, u32[]{:S(2)}, u32[]{:S(2)}) collective-permute-start(f32[9,16,256]{2,1,0:T(8,128)S(1)} %get-tuple-element.92), channel_id=1, source_target_pairs={{0,240},{16,32},{32,16},{48,64},{64,48},{80,96},{96,80},{112,128},... | collective-permute-start | bytes 442376 | tf_op jit(solution)/shard_map/ppermute | solution.py:655
  10.5 0.0 collective-permute-start.1
  10.5 1.2 %collective-permute-start.2 = (f32[9,16,256]{2,1,0:T(8,128)S(1)}, f32[9,16,256]{2,1,0:T(8,128)S(1)}, u32[]{:S(2)}, u32[]{:S(2)}) collective-permute-start(f32[9,16,256]{2,1,0:T(8,128)S(1)} %get-tuple-element.88), channel_id=1, source_target_pairs={{0,15},{1,2},{2,1},{3,4},{4,3},{5,6},{6,5},{7,8},{8,7},{9,10},{10,... | collective-permute-start | bytes 442376 | tf_op jit(solution)/shard_map/ppermute | solution.py:655
  11.8 0.0 collective-permute-start.3
  11.8 1.0 %copy-done = f32[2,16,16,256]{3,2,1,0:T(8,128)S(1)} copy-done((f32[2,16,16,256]{3,2,1,0:T(8,128)S(1)}, f32[2,16,16,256]{3,2,1,0:T(8,128)}, u32[]{:S(2)}) %copy-start) | copy-done | bytes 524312
  12.8 0.9 %copy-done.1 = f32[16,16,256]{2,1,0:T(8,128)S(1)} copy-done((f32[16,16,256]{2,1,0:T(8,128)S(1)}, f32[16,16,256]{2,1,0:T(8,128)}, u32[]{:S(2)}) %copy-start.1) | copy-done | bytes 262168
  13.8 4.3 %collide.1 = (f32[19,16,16,256]{3,2,1,0:T(8,128)S(1)}, f32[4,16,16,256]{3,2,1,0:T(8,128)S(1)}, f32[19,16,256]{2,1,0:T(8,128)S(1)}, f32[19,16,256]{2,1,0:T(8,128)...) custom-call(f32[19,16,16,256]{3,2,1,0:T(8,128)} %pops.1, f32[16,16,256]{2,1,0:T(8,128)S(1)} %copy-done.1, ...), custom_call_target="tpu_custom_call" | custom-call | flops 20000000 | bytes 14000000 | tf_op jit(solution)/shard_map/collide/pallas_call | solution.py:670
  18.1 0.0 copy-start.2
  18.1 0.0 copy-start.3
  18.1 0.0 collective-permute-done.1
  18.2 1.0 %edge.1 = (f32[4,16,16,256]{3,2,1,0:T(8,128)S(1)}, f32[19,16,256]{2,1,0:T(8,128)S(1)}, f32[19,16,256]{2,1,0:T(8,128)S(1)}, f32[19,16,256]{2,1,0:T(8,128)S(1)}, f...) custom-call(f32[19,16,256]{2,1,0:T(8,128)S(1)} %get-tuple-element.46, ...), custom_call_target="tpu_custom_call" | custom-call | bytes 3000000 | tf_op jit(solution)/shard_map/edge/pallas_call | solution.py:675
  19.2 2.8 %collective-permute-start.4 = (f32[120,256]{1,0:T(8,128)S(1)}, f32[120,256]{1,0:T(8,128)S(1)}, u32[]{:S(2)}, u32[]{:S(2)}) collective-permute-start(f32[120,256]{1,0:T(8,128)S(1)} %get-tuple-element.96), channel_id=1, source_target_pairs={{0,15},{1,2},{2,1},{3,4},{4,3},{5,6},{6,5},{7,8},{8,7},{9,10},{10,... | collective-permute-start | bytes 368648 | tf_op jit(solution)/shard_map/ppermute | solution.py:655
  22.0 3.5 %collective-permute-start.6 = (f32[112,256]{1,0:T(8,128)S(1)}, f32[112,256]{1,0:T(8,128)S(1)}, u32[]{:S(2)}, u32[]{:S(2)}) collective-permute-start(f32[112,256]{1,0:T(8,128)S(1)} %get-tuple-element.104), channel_id=1, source_target_pairs={{0,240},{16,32},{32,16},{48,64},{64,48},{80,96},{96,80},{112,128},... | collective-permute-start | bytes 344072 | tf_op jit(solution)/shard_map/ppermute | solution.py:655
  25.5 0.0 collective-permute-start.7
  25.5 0.2 collective-permute-done.4
  25.7 0.0 collective-permute-done.5
  25.8 5.3 %collective-permute-start.8 = (f32[16,256]{1,0:T(8,128)S(1)}, f32[16,256]{1,0:T(8,128)S(1)}, u32[]{:S(2)}, u32[]{:S(2)}) collective-permute-start(f32[16,256]{1,0:T(8,128)S(1)} %get-tuple-element.116), channel_id=1, source_target_pairs={{0,240},{16,32},{32,16},{48,64},{64,48},{80,96},{96,80},{112,128},... | collective-permute-start | bytes 49160 | tf_op jit(solution)/shard_map/ppermute | solution.py:655
  31.1 0.0 collective-permute-start.9
  31.1 2.9 %collective-permute-done.7 = f32[112,256]{1,0:T(8,128)S(1)} collective-permute-done((f32[112,256]{1,0:T(8,128)S(1)}, f32[112,256]{1,0:T(8,128)S(1)}, u32[]{:S(2)}, u32[]{:S(2)}) %collective-permute-start.7) | collective-permute-done | bytes 114720 | tf_op jit(solution)/shard_map/ppermute | solution.py:654
  34.1 2.0 %diffuse.1 = (f32[2,16,16,256]{3,2,1,0:T(8,128)S(1)}, f32[2,17,16,256]{3,2,1,0:T(8,128)S(1)}, f32[2,16,16,256]{3,2,1,0:T(8,128)S(1)}, f32[2,16,256]{2,1,0:T(8,12...) custom-call(f32[4]{0:T(128)S(1)} %copy-done.3, s32[16,16,256]{2,1,0:T(8,128)S(1)} %copy-done.2, ...), custom_call_target="tpu_custom_call" | custom-call | flops 10000000 | bytes 6000000 | tf_op jit(solution)/shard_map/diffuse/pallas_call | solution.py:685
  36.1 1.8 %transport.1 = (f32[2,16,16,256]{3,2,1,0:T(8,128)}, f32[16,16,256]{2,1,0:T(8,128)S(1)}, f32[5,16,256]{2,1,0:T(8,128)S(1)}, f32[5,16,256]{2,1,0:T(8,128)S(1)}, f3...) custom-call(f32[4,16,16,256]{3,2,1,0:T(8,128)S(1)} %get-tuple-element.65.mom, f32[16,16,256]{2,1,0:T(8,128)S(1)} %get-tuple-element.44.cond, ...), custom_call_target="tpu_custom_call" | custom-call | flops 5000000 | bytes 4000000 | tf_op jit(solution)/shard_map/transport/pallas_call | solution.py:689
  37.9 1.5 %collective-permute-start.10 = (f32[5,16,256]{2,1,0:T(8,128)S(1)}, f32[5,16,256]{2,1,0:T(8,128)S(1)}, u32[]{:S(2)}, u32[]{:S(2)}) collective-permute-start(f32[5,16,256]{2,1,0:T(8,128)S(1)} %get-tuple-element.108), channel_id=1, source_target_pairs={{0,15},{1,2},{2,1},{3,4},{4,3},{5,6},{6,5},{7,8},{8,7},{9,10},{10,... | collective-permute-start | bytes 245768 | tf_op jit(solution)/shard_map/ppermute | solution.py:655
  39.4 4.5 %collective-permute-done.10 = f32[5,16,256]{2,1,0:T(8,128)S(1)} collective-permute-done((f32[5,16,256]{2,1,0:T(8,128)S(1)}, f32[5,16,256]{2,1,0:T(8,128)S(1)}, u32[]{:S(2)}, u32[]{:S(2)}) %collective-permute-start.10) | collective-permute-done | bytes 81952 | tf_op jit(solution)/shard_map/ppermute | solution.py:655
  44.0 1.8 %collective-permute-start.14 = (f32[24,256]{1,0:T(8,128)S(1)}, f32[24,256]{1,0:T(8,128)S(1)}, u32[]{:S(2)}, u32[]{:S(2)}) collective-permute-start(f32[24,256]{1,0:T(8,128)S(1)} %get-tuple-element.112), channel_id=1, source_target_pairs={{0,240},{16,32},{32,16},{48,64},{64,48},{80,96},{96,80},{112,128},... | collective-permute-start | bytes 73736 | tf_op jit(solution)/shard_map/ppermute | solution.py:655
  45.8 0.3 collective-permute-start.15
  46.1 3.5 %collective-permute-start.12 = (f32[112,256]{1,0:T(8,128)S(1)}, f32[112,256]{1,0:T(8,128)S(1)}, u32[]{:S(2)}, u32[]{:S(2)}) collective-permute-start(f32[112,256]{1,0:T(8,128)S(1)} %get-tuple-element.100), channel_id=1, source_target_pairs={{0,240},{16,32},{32,16},{48,64},{64,48},{80,96},{96,80},{112,128},... | collective-permute-start | bytes 344072 | tf_op jit(solution)/shard_map/ppermute | solution.py:655
  49.6 2.4 %patch.1 = f32[19,16,16,256]{3,2,1,0:T(8,128)} custom-call(f32[19,16,16,256]{3,2,1,0:T(8,128)S(1)} %get-tuple-element.45.buf, f32[19,16,256]{2,1,0:T(8,128)S(1)} %get-tuple-element.55.ex_lo, f32[19,16,256]{2,1,0:T(8,128)S(1)} %get-tuple-element.56.ex_hi, f32[19,16,256]{2,1,0:T(8,128)S(1)} %get-tuple-element.57.ey_lo, ...), custom_call_target="tpu_custom_call" | custom-call | bytes 10000000 | tf_op jit(solution)/shard_map/patch/pallas_call | solution.py:706
  52.1 0.3 prepare.1
  52.4 2.5 %collective-permute-done.12 = f32[112,256]{1,0:T(8,128)S(1)} collective-permute-done((f32[112,256]{1,0:T(8,128)S(1)}, f32[112,256]{1,0:T(8,128)S(1)}, u32[]{:S(2)}, u32[]{:S(2)}) %collective-permute-start.12) | collective-permute-done | bytes 114720 | tf_op jit(solution)/shard_map/ppermute | solution.py:655
  54.9 2.5 %collective-permute-done.13 = f32[112,256]{1,0:T(8,128)S(1)} collective-permute-done((f32[112,256]{1,0:T(8,128)S(1)}, f32[112,256]{1,0:T(8,128)S(1)}, u32[]{:S(2)}, u32[]{:S(2)}) %collective-permute-start.13) | collective-permute-done | bytes 114720 | tf_op jit(solution)/shard_map/ppermute | solution.py:654
  57.4 2.1 %sweep.1 = f32[16,16,256]{2,1,0:T(8,128)} custom-call(f32[8,32,256]{2,1,0:T(8,128)S(1)} %get-tuple-element.77.even_in, f32[8,32,256]{2,1,0:T(8,128)S(1)} %get-tuple-element.78.odd_in, f32[8,32,256]{2,1,0:T(8,128)S(1)} %get-tuple-element.79.s_even_in, f32[8,32,256]{2,1,0:T(8,128)S(1)} %get-tuple-element.80.s_odd_in, ...), custom_call_target="tpu_custom_call" | custom-call | flops 20000000 | bytes 4000000 | tf_op jit(solution)/shard_map/sweep/pallas_call | solution.py:702
  (34 shorter events, 0.4 us)
Async XLA Ops:
  2.2 15.9 %collective-permute-start = (f32[9,16,256]{2,1,0:T(8,128)S(1)}, f32[9,16,256]{2,1,0:T(8,128)S(1)}, u32[]{:S(2)}, u32[]{:S(2)}) collective-permute-start(f32[9,16,256]{2,1,0:T(8,128)S(1)} %get-tuple-element.92), channel_id=1, source_target_pairs={{0,240},{16,32},{32,16},{48,64},{64,48},{80,96},{96,80},{112,128},... | collective-permute-start | bytes 442376 | tf_op jit(solution)/shard_map/ppermute | solution.py:655
  10.5 7.6 %collective-permute-start.1 = (f32[9,16,256]{2,1,0:T(8,128)S(1)}, f32[9,16,256]{2,1,0:T(8,128)S(1)}, u32[]{:S(2)}, u32[]{:S(2)}) collective-permute-start(f32[9,16,256]{2,1,0:T(8,128)S(1)} %get-tuple-element.91), channel_id=1, source_target_pairs={{0,16},{16,0},{32,48},{48,32},{64,80},{80,64},{96,112},{112,96},{1... | collective-permute-start | bytes 442376 | tf_op jit(solution)/shard_map/ppermute | solution.py:654
  10.5 7.6 %collective-permute-start.2 = (f32[9,16,256]{2,1,0:T(8,128)S(1)}, f32[9,16,256]{2,1,0:T(8,128)S(1)}, u32[]{:S(2)}, u32[]{:S(2)}) collective-permute-start(f32[9,16,256]{2,1,0:T(8,128)S(1)} %get-tuple-element.88), channel_id=1, source_target_pairs={{0,15},{1,2},{2,1},{3,4},{4,3},{5,6},{6,5},{7,8},{8,7},{9,10},{10,... | collective-permute-start | bytes 442376 | tf_op jit(solution)/shard_map/ppermute | solution.py:655
  11.8 6.4 %collective-permute-start.3 = (f32[9,16,256]{2,1,0:T(8,128)S(1)}, f32[9,16,256]{2,1,0:T(8,128)S(1)}, u32[]{:S(2)}, u32[]{:S(2)}) collective-permute-start(f32[9,16,256]{2,1,0:T(8,128)S(1)} %get-tuple-element.87), channel_id=1, source_target_pairs={{0,1},{1,0},{2,3},{3,2},{4,5},{5,4},{6,7},{7,6},{8,9},{9,8},{10,11... | collective-permute-start | bytes 442376 | tf_op jit(solution)/shard_map/ppermute | solution.py:654
  11.8 1.0 %copy-start = (f32[2,16,16,256]{3,2,1,0:T(8,128)S(1)}, f32[2,16,16,256]{3,2,1,0:T(8,128)}, u32[]{:S(2)}) copy-start(f32[2,16,16,256]{3,2,1,0:T(8,128)} %conc.1) | copy-start | bytes 1572868
  12.8 0.9 %copy-start.1 = (f32[16,16,256]{2,1,0:T(8,128)S(1)}, f32[16,16,256]{2,1,0:T(8,128)}, u32[]{:S(2)}) copy-start(f32[16,16,256]{2,1,0:T(8,128)} %pot.3) | copy-start | bytes 786436
  18.1 16.0 %copy-start.2 = (s32[16,16,256]{2,1,0:T(8,128)S(1)}, s32[16,16,256]{2,1,0:T(8,128)}, u32[]{:S(2)}) copy-start(s32[16,16,256]{2,1,0:T(8,128)} %classes_h.1) | copy-start | bytes 786436
  18.1 16.0 %copy-start.3 = (f32[4]{0:T(128)S(1)}, f32[4]{0:T(128)}, u32[]{:S(2)}) copy-start(f32[4]{0:T(128)} %charge.1) | copy-start | bytes 52
  19.2 6.5 %collective-permute-start.4 = (f32[120,256]{1,0:T(8,128)S(1)}, f32[120,256]{1,0:T(8,128)S(1)}, u32[]{:S(2)}, u32[]{:S(2)}) collective-permute-start(f32[120,256]{1,0:T(8,128)S(1)} %get-tuple-element.96), channel_id=1, source_target_pairs={{0,15},{1,2},{2,1},{3,4},{4,3},{5,6},{6,5},{7,8},{8,7},{9,10},{10,... | collective-permute-start | bytes 368648 | tf_op jit(solution)/shard_map/ppermute | solution.py:655
  22.0 3.7 %collective-permute-start.5 = (f32[120,256]{1,0:T(8,128)S(1)}, f32[120,256]{1,0:T(8,128)S(1)}, u32[]{:S(2)}, u32[]{:S(2)}) collective-permute-start(f32[120,256]{1,0:T(8,128)S(1)} %get-tuple-element.95), channel_id=1, source_target_pairs={{0,1},{1,0},{2,3},{3,2},{4,5},{5,4},{6,7},{7,6},{8,9},{9,8},{10,11... | collective-permute-start | bytes 368648 | tf_op jit(solution)/shard_map/ppermute | solution.py:654
  22.0 9.1 %collective-permute-start.6 = (f32[112,256]{1,0:T(8,128)S(1)}, f32[112,256]{1,0:T(8,128)S(1)}, u32[]{:S(2)}, u32[]{:S(2)}) collective-permute-start(f32[112,256]{1,0:T(8,128)S(1)} %get-tuple-element.104), channel_id=1, source_target_pairs={{0,240},{16,32},{32,16},{48,64},{64,48},{80,96},{96,80},{112,128},... | collective-permute-start | bytes 344072 | tf_op jit(solution)/shard_map/ppermute | solution.py:655
  25.5 8.5 %collective-permute-start.7 = (f32[112,256]{1,0:T(8,128)S(1)}, f32[112,256]{1,0:T(8,128)S(1)}, u32[]{:S(2)}, u32[]{:S(2)}) collective-permute-start(f32[112,256]{1,0:T(8,128)S(1)} %get-tuple-element.103), channel_id=1, source_target_pairs={{0,16},{16,0},{32,48},{48,32},{64,80},{80,64},{96,112},{112,96},{1... | collective-permute-start | bytes 344072 | tf_op jit(solution)/shard_map/ppermute | solution.py:654
  25.8 10.3 %collective-permute-start.8 = (f32[16,256]{1,0:T(8,128)S(1)}, f32[16,256]{1,0:T(8,128)S(1)}, u32[]{:S(2)}, u32[]{:S(2)}) collective-permute-start(f32[16,256]{1,0:T(8,128)S(1)} %get-tuple-element.116), channel_id=1, source_target_pairs={{0,240},{16,32},{32,16},{48,64},{64,48},{80,96},{96,80},{112,128},... | collective-permute-start | bytes 49160 | tf_op jit(solution)/shard_map/ppermute | solution.py:655
  31.1 5.0 %collective-permute-start.9 = (f32[16,256]{1,0:T(8,128)S(1)}, f32[16,256]{1,0:T(8,128)S(1)}, u32[]{:S(2)}, u32[]{:S(2)}) collective-permute-start(f32[16,256]{1,0:T(8,128)S(1)} %get-tuple-element.115), channel_id=1, source_target_pairs={{0,16},{16,0},{32,48},{48,32},{64,80},{80,64},{96,112},{112,96},{1... | collective-permute-start | bytes 49160 | tf_op jit(solution)/shard_map/ppermute | solution.py:654
  37.9 6.1 %collective-permute-start.10 = (f32[5,16,256]{2,1,0:T(8,128)S(1)}, f32[5,16,256]{2,1,0:T(8,128)S(1)}, u32[]{:S(2)}, u32[]{:S(2)}) collective-permute-start(f32[5,16,256]{2,1,0:T(8,128)S(1)} %get-tuple-element.108), channel_id=1, source_target_pairs={{0,15},{1,2},{2,1},{3,4},{4,3},{5,6},{6,5},{7,8},{8,7},{9,10},{10,... | collective-permute-start | bytes 245768 | tf_op jit(solution)/shard_map/ppermute | solution.py:655
  39.4 4.5 %collective-permute-start.11 = (f32[5,16,256]{2,1,0:T(8,128)S(1)}, f32[5,16,256]{2,1,0:T(8,128)S(1)}, u32[]{:S(2)}, u32[]{:S(2)}) collective-permute-start(f32[5,16,256]{2,1,0:T(8,128)S(1)} %get-tuple-element.107), channel_id=1, source_target_pairs={{0,1},{1,0},{2,3},{3,2},{4,5},{5,4},{6,7},{7,6},{8,9},{9,8},{10,11... | collective-permute-start | bytes 245768 | tf_op jit(solution)/shard_map/ppermute | solution.py:654
  44.0 8.3 %collective-permute-start.14 = (f32[24,256]{1,0:T(8,128)S(1)}, f32[24,256]{1,0:T(8,128)S(1)}, u32[]{:S(2)}, u32[]{:S(2)}) collective-permute-start(f32[24,256]{1,0:T(8,128)S(1)} %get-tuple-element.112), channel_id=1, source_target_pairs={{0,240},{16,32},{32,16},{48,64},{64,48},{80,96},{96,80},{112,128},... | collective-permute-start | bytes 73736 | tf_op jit(solution)/shard_map/ppermute | solution.py:655
  45.8 6.5 %collective-permute-start.15 = (f32[24,256]{1,0:T(8,128)S(1)}, f32[24,256]{1,0:T(8,128)S(1)}, u32[]{:S(2)}, u32[]{:S(2)}) collective-permute-start(f32[24,256]{1,0:T(8,128)S(1)} %get-tuple-element.111), channel_id=1, source_target_pairs={{0,16},{16,0},{32,48},{48,32},{64,80},{80,64},{96,112},{112,96},{1... | collective-permute-start | bytes 73736 | tf_op jit(solution)/shard_map/ppermute | solution.py:654
  46.1 8.8 %collective-permute-start.12 = (f32[112,256]{1,0:T(8,128)S(1)}, f32[112,256]{1,0:T(8,128)S(1)}, u32[]{:S(2)}, u32[]{:S(2)}) collective-permute-start(f32[112,256]{1,0:T(8,128)S(1)} %get-tuple-element.100), channel_id=1, source_target_pairs={{0,240},{16,32},{32,16},{48,64},{64,48},{80,96},{96,80},{112,128},... | collective-permute-start | bytes 344072 | tf_op jit(solution)/shard_map/ppermute | solution.py:655
  49.6 7.7 %collective-permute-start.13 = (f32[112,256]{1,0:T(8,128)S(1)}, f32[112,256]{1,0:T(8,128)S(1)}, u32[]{:S(2)}, u32[]{:S(2)}) collective-permute-start(f32[112,256]{1,0:T(8,128)S(1)} %get-tuple-element.99), channel_id=1, source_target_pairs={{0,16},{16,0},{32,48},{48,32},{64,80},{80,64},{96,112},{112,96},{1... | collective-permute-start | bytes 344072 | tf_op jit(solution)/shard_map/ppermute | solution.py:654

commit v4 on v2

--- a/solution.py
+++ b/solution.py
@@ -22,6 +22,7 @@
 OFF = 8
 ROWS = 7 * N + 8
 LINE = 7 * N
+SOLID = 1.0
 F32 = jnp.float32
 VM = pltpu.VMEM
 
@@ -79,7 +80,7 @@
     )
 
 
-def faces_kernel(pot_h, conc_h, mob_h, solid_h, gx_hi, gx_lo, gy_hi, gy_lo, cond, pot, conc, mob, solid, sems):
+def faces_kernel(pot_h, conc_h, mob_h, solid_h, gx_hi, gx_lo, gy_hi, gy_lo, pull, middle, pot, cond, conc, mob, solid, sems):
     pairs = ((pot_h, pot), (conc_h, conc), (mob_h, mob), (solid_h, solid))
     copies = [pltpu.make_async_copy(a, b, sems.at[q]) for q, (a, b) in enumerate(pairs)]
     for c in copies:
@@ -89,7 +90,9 @@
 
     def step(x, carry):
         here = pl.ds(x, 1)
-        cond[x] = jnp.where(solid[x] == 0, jnp.sqrt(mob[x]), 0.0)
+        is_fluid = solid[x] == 0
+        cond[x] = jnp.where(is_fluid, jnp.sqrt(mob[x]), 0.0)
+        pull[x] = jnp.where(is_fluid, (conc[0, x] - conc[1, x]) * (-0.001), SOLID)
         for r in range(RING):
             gy_hi[r, here, :] = pot[x, N - 1 - r:N - r, :]
             gy_lo[r, here, :] = pot[x, r:r + 1, :]
@@ -98,7 +101,9 @@
             gy_lo[RING + q, here, :] = v[x, 0:1, :]
         return carry
 
-    lax.fori_loop(0, N, step, 0, unroll=2)
+    lax.fori_loop(0, N, step, 0, unroll=True)
+    for x in range(RING, N - RING):
+        middle[x - RING] = pot[x]
     for x, face in ((N - 1, gx_hi), (0, gx_lo)):
         for r in range(RING):
             face[r] = pot[abs(x - r)]
@@ -108,7 +113,7 @@
 
 
 def post_of(p, fluid, q, slopes):
-    pull = jnp.where(fluid, q * (-0.001), 0.0)
+    pull = jnp.where(fluid, q, 0.0)
     force = [pull * d for d in slopes]
     density = p[0]
     for i in range(1, 19):
@@ -163,13 +168,12 @@
     return total
 
 
-def collide_kernel(pops, pot_h, conc_h, cond, buf, mom, px_lo, px_hi, pr_lo, pr_hi, held, pot, conc, sems, psems):
+def collide_kernel(pops, gx_hi, gx_lo, middle, pull, buf, mom, px_lo, px_hi, pr_lo, pr_hi, held, sems, psems):
     chunks = [pltpu.make_async_copy(pops.at[:, pl.ds(CHUNK * s, CHUNK)], held.at[:, pl.ds(CHUNK * s, CHUNK)], sems.at[s])
               for s in range(N // CHUNK)]
     ends = [pltpu.make_async_copy(pops.at[:, 0], px_lo, psems.at[0]),
             pltpu.make_async_copy(pops.at[:, N - 1], px_hi, psems.at[1])]
-    fields = [pltpu.make_async_copy(pot_h, pot, psems.at[2]), pltpu.make_async_copy(conc_h, conc, psems.at[3])]
-    for c in fields + chunks + ends:
+    for c in chunks + ends:
         c.start()
     row = rows()
     zero = jnp.zeros((N, Z), F32)
@@ -178,15 +182,18 @@
         mom[m, 0] = zero
         mom[m, 1] = zero
 
-    def step(x, carry):
+    def pot(x):
+        return gx_lo[x] if x < RING else gx_hi[N - 1 - x] if x >= N - RING else middle[x - RING]
+
+    def step(x):
         here = pl.ds(x, 1)
         p = [held[i, x] for i in range(19)]
         for i in range(19):
             pr_lo[i, here, :] = row_of(p[i], 0)
             pr_hi[i, here, :] = row_of(p[i], N - 1)
-        centre = pot[x]
-        slopes = (pot[x + 1] - pot[x - 1], roll_y(centre, -1) - roll_y(centre, 1), roll_z(centre, -1) - roll_z(centre, 1))
-        post, force = post_of(p, cond[x] > 0.0, conc[0, x] - conc[1, x], slopes)
+        centre = pot(x)
+        slopes = (pot(x + 1) - pot(x - 1), roll_y(centre, -1) - roll_y(centre, 1), roll_z(centre, -1) - roll_z(centre, 1))
+        post, force = post_of(p, pull[x] < 0.5 * SOLID, pull[x], slopes)
         moved = []
         for i in range(19):
             v = post[i]
@@ -207,13 +214,11 @@
         g = sums([(i, moved[i]) for i in XNEG], keep)
         for m in range(4):
             mom[m, x - 1] += g[m]
-        return carry
-
-    for c in fields:
-        c.wait()
+
     for s in range(N // CHUNK):
         chunks[s].wait()
-        lax.fori_loop(max(CHUNK * s, 1), min(CHUNK * s + CHUNK, N - 1), step, 0, unroll=True)
+        for x in range(max(CHUNK * s, 1), min(CHUNK * s + CHUNK, N - 1)):
+            step(x)
     for c in ends:
         c.wait()
 
@@ -228,7 +233,7 @@
         centre = gy[0]
         y_slope = gy[1] - fy[0] if low else fy[0] - gy[1]
         slopes = (roll_y(centre, -1) - roll_y(centre, 1), y_slope, roll_z(centre, -1) - roll_z(centre, 1))
-        post, force = post_of([pr[i] for i in range(19)], gy[RING + 2] > 0.0, gy[RING] - gy[RING + 1], slopes)
+        post, force = post_of([pr[i] for i in range(19)], gy[RING + 2] > 0.0, (gy[RING] - gy[RING + 1]) * (-0.001), slopes)
         for i in range(19):
             v = roll_z(post[i], C[i][2]) if C[i][2] else post[i]
             v = jnp.where(inner, v, 0.0)
@@ -267,7 +272,7 @@
         y_up = jnp.where(row == N - 1, spread(fy_hi[0, at:at + 1, :]), roll_y(centre, -1))
         y_dn = jnp.where(row == 0, spread(fy_lo[0, at:at + 1, :]), roll_y(centre, 1))
         slopes = (x_slope, y_up - y_dn, roll_z(centre, -1) - roll_z(centre, 1))
-        post, force = post_of([px[i] for i in range(19)], gx[RING + 2] > 0.0, gx[RING] - gx[RING + 1], slopes)
+        post, force = post_of([px[i] for i in range(19)], gx[RING + 2] > 0.0, (gx[RING] - gx[RING + 1]) * (-0.001), slopes)
         for i in range(19):
             v = roll_z(post[i], C[i][2]) if C[i][2] else post[i]
             if C[i][1] == 1:
@@ -529,7 +534,7 @@
             done[i, src + cx] = halo(v, src)
             return carry
 
-        lax.fori_loop(1, N - 1, inner, 0, unroll=2)
+        lax.fori_loop(1, N - 1, inner, 0, unroll=True)
         if cx != -1:
             done[i, cx] = halo(ex_lo[i], 0)
         if cx != 1:
@@ -556,8 +561,8 @@
     return rest, weight
 
 
-def diffuse_kernel(charge, classes_h, cond, conc, pot, fx_lo, fx_hi, fy_lo, fy_hi, gy_lo,
-                   base, wx, wy, wy_low, wz, wall, low, classes, sem):
+def diffuse_kernel(charge, classes_h, mob, solid, conc, pot, fx_lo, fx_hi, fy_lo, fy_hi, gy_lo,
+                   base, wx, wy, wy_low, wz, wall, cond, low, classes, sem):
     fetch = pltpu.make_async_copy(classes_h, classes, sem)
     fetch.start()
     row = rows()
@@ -570,6 +575,8 @@
         low[s] = rest[s]
         wy_low[s] = weight[s]
     upper = faces(fy_hi)
+    for x in range(N):
+        cond[x] = jnp.where(solid[x] == 0, jnp.sqrt(mob[x]), 0.0)
 
     def fields(x):
         return (conc[0, x], conc[1, x], cond[x], pot[x])
@@ -643,19 +650,19 @@
 def body(pops, conc, pot, mob, solid, classes, charge):
     cube = sds(N, N, Z)
     msg = sds(ROWS, Z)
-    gx_hi, gx_lo, gy_hi, gy_lo, cond = call(
-        faces_kernel, [sds(RING + 3, N, Z)] * 4 + [cube], "faces", "hhhh",
-        scratch=[VM((N, N, Z), F32), VM((2, N, N, Z), F32), VM((N, N, Z), F32), VM((N, N, Z), jnp.int32),
+    gx_hi, gx_lo, gy_hi, gy_lo, pull, middle = call(
+        faces_kernel, [sds(RING + 3, N, Z)] * 4 + [cube, sds(N - 2 * RING, N, Z)], "faces", "hhhh",
+        scratch=[VM((N, N, Z), F32), VM((N, N, Z), F32), VM((2, N, N, Z), F32), VM((N, N, Z), F32),
+                 VM((N, N, Z), jnp.int32),
                  pltpu.SemaphoreType.DMA((4,))], mib=53, moved=2600000)(
         pot, conc, mob, solid)
     fx_lo, fx_hi = swap("gx", gx_hi, gx_lo)
     fy_lo, fy_hi = swap("gy", gy_hi, gy_lo)
     chunks = N // CHUNK
     buf, mom, px_lo, px_hi, pr_lo, pr_hi = call(
-        collide_kernel, [sds(19, N, N, Z), sds(4, N, N, Z)] + [sds(19, N, Z)] * 4, "collide", "hhhv",
-        scratch=[VM((19, N, N, Z), F32), VM((N, N, Z), F32), VM((2, N, N, Z), F32),
-                 pltpu.SemaphoreType.DMA((chunks,)), pltpu.SemaphoreType.DMA((4,))],
-        mib=43, flops=20000000, moved=14000000)(pops, pot, conc, cond)
+        collide_kernel, [sds(19, N, N, Z), sds(4, N, N, Z)] + [sds(19, N, Z)] * 4, "collide", "hvvvv",
+        scratch=[VM((19, N, N, Z), F32), pltpu.SemaphoreType.DMA((chunks,)), pltpu.SemaphoreType.DMA((2,))],
+        mib=43, flops=20000000, moved=14000000)(pops, gx_hi, gx_lo, middle, pull)
     mom, ex_lo, ex_hi, ey_lo, ey_hi, yb_lo, yb_hi = call(
         edge_kernel, [sds(4, N, N, Z)] + [sds(19, N, Z)] * 4 + [msg, msg], "edge", "v" * 13, moved=3000000)(
         px_lo, px_hi, pr_lo, pr_hi, gx_lo, gx_hi, gy_lo, gy_hi, fx_lo, fx_hi, fy_lo, fy_hi, mom)
@@ -665,10 +672,10 @@
     face = VM((N, Z), F32)
     fy_late, _ = lax.optimization_barrier((fy_lo, yh_lo))
     pair = sds(2, N, N, Z)
-    base, wx, wy, wy_low, wz, wall = call(
-        diffuse_kernel, [pair, sds(2, N + 1, N, Z), pair, sds(2, N, Z), pair, cube], "diffuse", "sh" + "v" * 8,
+    base, wx, wy, wy_low, wz, wall, cond = call(
+        diffuse_kernel, [pair, sds(2, N + 1, N, Z), pair, sds(2, N, Z), pair, cube, cube], "diffuse", "sh" + "v" * 9,
         scratch=[VM((2, N, Z), F32), VM((N, N, Z), jnp.int32), pltpu.SemaphoreType.DMA], flops=10000000, moved=6000000)(
-        charge, classes, cond, conc, pot, fx_lo, fx_hi, fy_late, fy_hi, gy_lo)
+        charge, classes, mob, solid, conc, pot, fx_lo, fx_hi, fy_late, fy_hi, gy_lo)
     conc_out, src, sy_lo, sy_hi = call(
         transport_kernel, [pair, cube, sds(RING - 1, N, Z), sds(RING - 1, N, Z)], "transport", "v" * 20,
         scratch=[VM((3, N, N, Z), F32), VM((8, N, Z), F32), VM((2, N, Z), F32), face, face], flops=5000000, moved=4000000)(

time: 58 us -> 57.8 us (level)
  waiting for transfers between devices: 17.2 us -> 20.9 us
  local copies, waits for them, and re-layouts: 2 us -> 0.04 us
  starting transfers between devices: 22 us -> 20.2 us
    ppermute x6, waiting for transfers between devices: 11.1 us -> 14 us  [swap(): lax.ppermute(jnp.where(even, lo, hi), axis, [(i, (i - 1 + 2 * (i % 2)) %...]
    unnamed x8 -> x12, local copies, waits for them, and re-layouts: 2 us -> 0.04 us
    ppermute x6, starting transfers between devices: 22 us -> 20.2 us  [swap(): lax.ppermute(jnp.where(even, lo, hi), axis, [(i, (i - 1 + 2 * (i % 2)) %...]
    ppermute x6, waiting for transfers between devices: 6.09 us -> 6.89 us  [swap(): lax.ppermute(jnp.where(even, hi, lo), axis, [(i, i + 1 - 2 * (i % 2)) for...]
  transfers between devices with their start and end apart: 12 -> 12, of which waited for: 6 -> 8; matrix products, arithmetic and copies ran while one was open for 0% -> 0% of each run, Pallas kernels for 16% -> 16%
where the time goes in v4:
time: 57.8 us; the launch traced here: 57.7 us
  waiting for transfers between devices  20.9 us (36%)
  starting transfers between devices  20.2 us (35%)
  Pallas kernels  15.4 us (27%)
  between operations  0.87 us (2%)
    ppermute x6, starting transfers between devices, swap(): lax.ppermute(jnp.where(even, lo, hi), axis, [(i, (i - 1 + 2 * (i % 2)) %...  20.2 us
    ppermute x6, waiting for transfers between devices, swap(): lax.ppermute(jnp.where(even, lo, hi), axis, [(i, (i - 1 + 2 * (i % 2)) %...  14 us
    ppermute x6, waiting for transfers between devices, swap(): lax.ppermute(jnp.where(even, hi, lo), axis, [(i, i + 1 - 2 * (i % 2)) for...  6.89 us
    pallas_call x1, Pallas kernels, body(): call(collide_kernel, [sds(19, N, N, Z), sds(4, N, N, Z)] + [sds(19, N, Z)...  4.22 us
    pallas_call x1, Pallas kernels, body(): call(patch_kernel, [sds(19, N, N, Z)], 'patch', 'v' * 9, out_specs='h', s...  2.43 us
    pallas_call x1, Pallas kernels, body(): call(sweep_kernel, [cube], 'sweep', 'v' * 8, scratch=[VM((N + 2 * RING, N...  2.09 us
    pallas_call x1, Pallas kernels, body(): call(diffuse_kernel, [pair, sds(2, N + 1, N, Z), pair, sds(2, N, Z), pair...  2.07 us
    pallas_call x1, Pallas kernels, body(): call(transport_kernel, [pair, cube, sds(RING - 1, N, Z), sds(RING - 1, N,...  1.73 us
  transfers between devices with their start and end apart: 12, of which 8 were waited for; matrix products, arithmetic and copies ran while one was open for 0% of the time, Pallas kernels for 16%

profile of v4, /device:TPU:7, one launch (start us, length us, event | category | flops | bytes accessed | tf_op | source)
XLA Modules:
  0.0 57.7 jit_solution(2478946910419037138)
XLA Ops:
  0.6 1.6 %faces.1 = (f32[9,16,256]{2,1,0:T(8,128)S(1)}, f32[9,16,256]{2,1,0:T(8,128)S(1)}, f32[9,16,256]{2,1,0:T(8,128)S(1)}, f32[9,16,256]{2,1,0:T(8,128)S(1)}, f32[16,1...) custom-call(f32[16,16,256]{2,1,0:T(8,128)} %pot.3, f32[2,16,16,256]{3,2,1,0:T(8,128)} %conc.1, f32[16,16,256]{2,1,0:T(8,128)} %mob.1, ...), custom_call_target="tpu_custom_call" | custom-call | bytes 2600000 | tf_op jit(solution)/shard_map/faces/pallas_call | solution.py:653
  2.2 8.3 %collective-permute-start = (f32[9,16,256]{2,1,0:T(8,128)S(1)}, f32[9,16,256]{2,1,0:T(8,128)S(1)}, u32[]{:S(2)}, u32[]{:S(2)}) collective-permute-start(f32[9,16,256]{2,1,0:T(8,128)S(1)} %get-tuple-element.88), channel_id=1, source_target_pairs={{0,240},{16,32},{32,16},{48,64},{64,48},{80,96},{96,80},{112,128},... | collective-permute-start | bytes 442376 | tf_op jit(solution)/shard_map/ppermute | solution.py:646
  10.5 0.0 collective-permute-start.1
  10.6 1.2 %collective-permute-start.2 = (f32[9,16,256]{2,1,0:T(8,128)S(1)}, f32[9,16,256]{2,1,0:T(8,128)S(1)}, u32[]{:S(2)}, u32[]{:S(2)}) collective-permute-start(f32[9,16,256]{2,1,0:T(8,128)S(1)} %get-tuple-element.84), channel_id=1, source_target_pairs={{0,15},{1,2},{2,1},{3,4},{4,3},{5,6},{6,5},{7,8},{8,7},{9,10},{10,... | collective-permute-start | bytes 442376 | tf_op jit(solution)/shard_map/ppermute | solution.py:646
  11.8 0.0 collective-permute-start.3
  11.8 4.2 %collide.1 = (f32[19,16,16,256]{3,2,1,0:T(8,128)S(1)}, f32[4,16,16,256]{3,2,1,0:T(8,128)S(1)}, f32[19,16,256]{2,1,0:T(8,128)S(1)}, f32[19,16,256]{2,1,0:T(8,128)...) custom-call(f32[19,16,16,256]{3,2,1,0:T(8,128)} %pops.1, f32[9,16,256]{2,1,0:T(8,128)S(1)} %get-tuple-element.42.gx_hi, ...), custom_call_target="tpu_custom_call" | custom-call | flops 20000000 | bytes 14000000 | tf_op jit(solution)/shard_map/collide/pallas_call | solution.py:662
  16.0 0.0 copy-start
  16.1 0.0 copy-start.1
  16.1 0.0 copy-start.2
  16.1 0.0 copy-start.3
  16.1 0.0 copy-start.4
  16.1 0.0 copy-start.5
  16.1 0.7 %collective-permute-done.1 = f32[9,16,256]{2,1,0:T(8,128)S(1)} collective-permute-done((f32[9,16,256]{2,1,0:T(8,128)S(1)}, f32[9,16,256]{2,1,0:T(8,128)S(1)}, u32[]{:S(2)}, u32[]{:S(2)}) %collective-permute-start.1) | collective-permute-done | bytes 147488 | tf_op jit(solution)/shard_map/ppermute | solution.py:645
  16.9 0.8 %collective-permute-done.2 = f32[9,16,256]{2,1,0:T(8,128)S(1)} collective-permute-done((f32[9,16,256]{2,1,0:T(8,128)S(1)}, f32[9,16,256]{2,1,0:T(8,128)S(1)}, u32[]{:S(2)}, u32[]{:S(2)}) %collective-permute-start.2) | collective-permute-done | bytes 147488 | tf_op jit(solution)/shard_map/ppermute | solution.py:646
  17.7 1.0 %edge.1 = (f32[4,16,16,256]{3,2,1,0:T(8,128)S(1)}, f32[19,16,256]{2,1,0:T(8,128)S(1)}, f32[19,16,256]{2,1,0:T(8,128)S(1)}, f32[19,16,256]{2,1,0:T(8,128)S(1)}, f...) custom-call(f32[19,16,256]{2,1,0:T(8,128)S(1)} %get-tuple-element.47.px_lo, ...), custom_call_target="tpu_custom_call" | custom-call | bytes 3000000 | tf_op jit(solution)/shard_map/edge/pallas_call | solution.py:666
  18.7 1.3 %collective-permute-start.4 = (f32[120,256]{1,0:T(8,128)S(1)}, f32[120,256]{1,0:T(8,128)S(1)}, u32[]{:S(2)}, u32[]{:S(2)}) collective-permute-start(f32[120,256]{1,0:T(8,128)S(1)} %get-tuple-element.100), channel_id=1, source_target_pairs={{0,15},{1,2},{2,1},{3,4},{4,3},{5,6},{6,5},{7,8},{8,7},{9,10},{10,... | collective-permute-start | bytes 368648 | tf_op jit(solution)/shard_map/ppermute | solution.py:646
  20.0 5.2 %collective-permute-done.4 = f32[120,256]{1,0:T(8,128)S(1)} collective-permute-done((f32[120,256]{1,0:T(8,128)S(1)}, f32[120,256]{1,0:T(8,128)S(1)}, u32[]{:S(2)}, u32[]{:S(2)}) %collective-permute-start.4) | collective-permute-done | bytes 122912 | tf_op jit(solution)/shard_map/ppermute | solution.py:646
  25.3 4.5 %collective-permute-start.6 = (f32[120,256]{1,0:T(8,128)S(1)}, f32[120,256]{1,0:T(8,128)S(1)}, u32[]{:S(2)}, u32[]{:S(2)}) collective-permute-start(f32[120,256]{1,0:T(8,128)S(1)} %get-tuple-element.96), channel_id=1, source_target_pairs={{0,240},{16,32},{32,16},{48,64},{64,48},{80,96},{96,80},{112,128},... | collective-permute-start | bytes 368648 | tf_op jit(solution)/shard_map/ppermute | solution.py:646
  29.8 2.1 %diffuse.1 = (f32[2,16,16,256]{3,2,1,0:T(8,128)S(1)}, f32[2,17,16,256]{3,2,1,0:T(8,128)S(1)}, f32[2,16,16,256]{3,2,1,0:T(8,128)S(1)}, f32[2,16,256]{2,1,0:T(8,12...) custom-call(f32[4]{0:T(128)S(1)} %copy-done.5, ...), custom_call_target="tpu_custom_call" | custom-call | flops 10000000 | bytes 6000000 | tf_op jit(solution)/shard_map/diffuse/pallas_call | solution.py:675
  31.8 1.4 %collective-permute-done.6 = f32[120,256]{1,0:T(8,128)S(1)} collective-permute-done((f32[120,256]{1,0:T(8,128)S(1)}, f32[120,256]{1,0:T(8,128)S(1)}, u32[]{:S(2)}, u32[]{:S(2)}) %collective-permute-start.6) | collective-permute-done | bytes 122912 | tf_op jit(solution)/shard_map/ppermute | solution.py:646
  33.3 3.1 %collective-permute-done.7 = f32[120,256]{1,0:T(8,128)S(1)} collective-permute-done((f32[120,256]{1,0:T(8,128)S(1)}, f32[120,256]{1,0:T(8,128)S(1)}, u32[]{:S(2)}, u32[]{:S(2)}) %collective-permute-start.7) | collective-permute-done | bytes 122912 | tf_op jit(solution)/shard_map/ppermute | solution.py:645
  36.4 1.7 %transport.1 = (f32[2,16,16,256]{3,2,1,0:T(8,128)}, f32[16,16,256]{2,1,0:T(8,128)S(1)}, f32[5,16,256]{2,1,0:T(8,128)S(1)}, f32[5,16,256]{2,1,0:T(8,128)S(1)}) custom-call(f32[4,16,16,256]{3,2,1,0:T(8,128)S(1)} %get-tuple-element.60.mom, f32[16,16,256]{2,1,0:T(8,128)S(1)} %get-tuple-element.64.cond, f32[2,16,16,256]{3,2,1,0:T(8,128)S(1)} %get-tuple-element.65.base, ...), custom_call_target="tpu_custom_call" | custom-call | flops 5000000 | bytes 4000000 | tf_op jit(solution)/shard_map/transport/pallas_call | solution.py:679
  38.2 1.8 %collective-permute-start.8 = (f32[5,16,256]{2,1,0:T(8,128)S(1)}, f32[5,16,256]{2,1,0:T(8,128)S(1)}, u32[]{:S(2)}, u32[]{:S(2)}) collective-permute-start(f32[5,16,256]{2,1,0:T(8,128)S(1)} %get-tuple-element.104), channel_id=1, source_target_pairs={{0,15},{1,2},{2,1},{3,4},{4,3},{5,6},{6,5},{7,8},{8,7},{9,10},{10,... | collective-permute-start | bytes 245768 | tf_op jit(solution)/shard_map/ppermute | solution.py:646
  40.0 0.0 collective-permute-start.9
  40.0 4.2 %collective-permute-done.8 = f32[5,16,256]{2,1,0:T(8,128)S(1)} collective-permute-done((f32[5,16,256]{2,1,0:T(8,128)S(1)}, f32[5,16,256]{2,1,0:T(8,128)S(1)}, u32[]{:S(2)}, u32[]{:S(2)}) %collective-permute-start.8) | collective-permute-done | bytes 81952 | tf_op jit(solution)/shard_map/ppermute | solution.py:646
  44.2 0.1 pack_src.1
  44.4 3.0 %collective-permute-start.10 = (f32[136,256]{1,0:T(8,128)S(1)}, f32[136,256]{1,0:T(8,128)S(1)}, u32[]{:S(2)}, u32[]{:S(2)}) collective-permute-start(f32[136,256]{1,0:T(8,128)S(1)} %get-tuple-element.92), channel_id=1, source_target_pairs={{0,240},{16,32},{32,16},{48,64},{64,48},{80,96},{96,80},{112,128},... | collective-permute-start | bytes 417800 | tf_op jit(solution)/shard_map/ppermute | solution.py:646
  47.4 2.4 %patch.1 = f32[19,16,16,256]{3,2,1,0:T(8,128)} custom-call(f32[19,16,16,256]{3,2,1,0:T(8,128)S(1)} %get-tuple-element.46.buf, f32[19,16,256]{2,1,0:T(8,128)S(1)} %get-tuple-element.54.ex_lo, f32[19,16,256]{2,1,0:T(8,128)S(1)} %get-tuple-element.55.ex_hi, f32[19,16,256]{2,1,0:T(8,128)S(1)} %get-tuple-element.56.ey_lo, ...), custom_call_target="tpu_custom_call" | custom-call | bytes 10000000 | tf_op jit(solution)/shard_map/patch/pallas_call | solution.py:695
  49.8 0.3 prepare.1
  50.1 2.4 %collective-permute-done.10 = f32[136,256]{1,0:T(8,128)S(1)} collective-permute-done((f32[136,256]{1,0:T(8,128)S(1)}, f32[136,256]{1,0:T(8,128)S(1)}, u32[]{:S(2)}, u32[]{:S(2)}) %collective-permute-start.10) | collective-permute-done | bytes 139296 | tf_op jit(solution)/shard_map/ppermute | solution.py:646
  52.5 3.1 %collective-permute-done.11 = f32[136,256]{1,0:T(8,128)S(1)} collective-permute-done((f32[136,256]{1,0:T(8,128)S(1)}, f32[136,256]{1,0:T(8,128)S(1)}, u32[]{:S(2)}, u32[]{:S(2)}) %collective-permute-start.11) | collective-permute-done | bytes 139296 | tf_op jit(solution)/shard_map/ppermute | solution.py:645
  55.6 2.1 %sweep.1 = f32[16,16,256]{2,1,0:T(8,128)} custom-call(f32[8,32,256]{2,1,0:T(8,128)S(1)} %get-tuple-element.75.even_in, f32[8,32,256]{2,1,0:T(8,128)S(1)} %get-tuple-element.76.odd_in, f32[8,32,256]{2,1,0:T(8,128)S(1)} %get-tuple-element.77.s_even_in, f32[8,32,256]{2,1,0:T(8,128)S(1)} %get-tuple-element.78.s_odd_in, ...), custom_call_target="tpu_custom_call" | custom-call | flops 20000000 | bytes 4000000 | tf_op jit(solution)/shard_map/sweep/pallas_call | solution.py:691
  (26 shorter events, 0.3 us)
Async XLA Ops:
  2.2 13.9 %collective-permute-start = (f32[9,16,256]{2,1,0:T(8,128)S(1)}, f32[9,16,256]{2,1,0:T(8,128)S(1)}, u32[]{:S(2)}, u32[]{:S(2)}) collective-permute-start(f32[9,16,256]{2,1,0:T(8,128)S(1)} %get-tuple-element.88), channel_id=1, source_target_pairs={{0,240},{16,32},{32,16},{48,64},{64,48},{80,96},{96,80},{112,128},... | collective-permute-start | bytes 442376 | tf_op jit(solution)/shard_map/ppermute | solution.py:646
  10.5 6.3 %collective-permute-start.1 = (f32[9,16,256]{2,1,0:T(8,128)S(1)}, f32[9,16,256]{2,1,0:T(8,128)S(1)}, u32[]{:S(2)}, u32[]{:S(2)}) collective-permute-start(f32[9,16,256]{2,1,0:T(8,128)S(1)} %get-tuple-element.87), channel_id=1, source_target_pairs={{0,16},{16,0},{32,48},{48,32},{64,80},{80,64},{96,112},{112,96},{1... | collective-permute-start | bytes 442376 | tf_op jit(solution)/shard_map/ppermute | solution.py:645
  10.6 7.1 %collective-permute-start.2 = (f32[9,16,256]{2,1,0:T(8,128)S(1)}, f32[9,16,256]{2,1,0:T(8,128)S(1)}, u32[]{:S(2)}, u32[]{:S(2)}) collective-permute-start(f32[9,16,256]{2,1,0:T(8,128)S(1)} %get-tuple-element.84), channel_id=1, source_target_pairs={{0,15},{1,2},{2,1},{3,4},{4,3},{5,6},{6,5},{7,8},{8,7},{9,10},{10,... | collective-permute-start | bytes 442376 | tf_op jit(solution)/shard_map/ppermute | solution.py:646
  11.8 5.8 %collective-permute-start.3 = (f32[9,16,256]{2,1,0:T(8,128)S(1)}, f32[9,16,256]{2,1,0:T(8,128)S(1)}, u32[]{:S(2)}, u32[]{:S(2)}) collective-permute-start(f32[9,16,256]{2,1,0:T(8,128)S(1)} %get-tuple-element.83), channel_id=1, source_target_pairs={{0,1},{1,0},{2,3},{3,2},{4,5},{5,4},{6,7},{7,6},{8,9},{9,8},{10,11... | collective-permute-start | bytes 442376 | tf_op jit(solution)/shard_map/ppermute | solution.py:645
  16.0 13.7 %copy-start = (f32[16,16,256]{2,1,0:T(8,128)S(1)}, f32[16,16,256]{2,1,0:T(8,128)}, u32[]{:S(2)}) copy-start(f32[16,16,256]{2,1,0:T(8,128)} %pot.3) | copy-start | bytes 786436
  16.1 13.7 %copy-start.1 = (f32[2,16,16,256]{3,2,1,0:T(8,128)S(1)}, f32[2,16,16,256]{3,2,1,0:T(8,128)}, u32[]{:S(2)}) copy-start(f32[2,16,16,256]{3,2,1,0:T(8,128)} %conc.1) | copy-start | bytes 1572868
  16.1 13.7 %copy-start.2 = (f32[16,16,256]{2,1,0:T(8,128)S(1)}, f32[16,16,256]{2,1,0:T(8,128)}, u32[]{:S(2)}) copy-start(f32[16,16,256]{2,1,0:T(8,128)} %mob.1) | copy-start | bytes 786436
  16.1 13.7 %copy-start.3 = (s32[16,16,256]{2,1,0:T(8,128)S(1)}, s32[16,16,256]{2,1,0:T(8,128)}, u32[]{:S(2)}) copy-start(s32[16,16,256]{2,1,0:T(8,128)} %solid.1) | copy-start | bytes 786436
  16.1 13.7 %copy-start.4 = (s32[16,16,256]{2,1,0:T(8,128)S(1)}, s32[16,16,256]{2,1,0:T(8,128)}, u32[]{:S(2)}) copy-start(s32[16,16,256]{2,1,0:T(8,128)} %classes_h.1) | copy-start | bytes 786436
  16.1 13.7 %copy-start.5 = (f32[4]{0:T(128)S(1)}, f32[4]{0:T(128)}, u32[]{:S(2)}) copy-start(f32[4]{0:T(128)} %charge.1) | copy-start | bytes 52
  18.7 6.5 %collective-permute-start.4 = (f32[120,256]{1,0:T(8,128)S(1)}, f32[120,256]{1,0:T(8,128)S(1)}, u32[]{:S(2)}, u32[]{:S(2)}) collective-permute-start(f32[120,256]{1,0:T(8,128)S(1)} %get-tuple-element.100), channel_id=1, source_target_pairs={{0,15},{1,2},{2,1},{3,4},{4,3},{5,6},{6,5},{7,8},{8,7},{9,10},{10,... | collective-permute-start | bytes 368648 | tf_op jit(solution)/shard_map/ppermute | solution.py:646
  20.0 5.2 %collective-permute-start.5 = (f32[120,256]{1,0:T(8,128)S(1)}, f32[120,256]{1,0:T(8,128)S(1)}, u32[]{:S(2)}, u32[]{:S(2)}) collective-permute-start(f32[120,256]{1,0:T(8,128)S(1)} %get-tuple-element.99), channel_id=1, source_target_pairs={{0,1},{1,0},{2,3},{3,2},{4,5},{5,4},{6,7},{7,6},{8,9},{9,8},{10,11... | collective-permute-start | bytes 368648 | tf_op jit(solution)/shard_map/ppermute | solution.py:645
  25.3 8.0 %collective-permute-start.6 = (f32[120,256]{1,0:T(8,128)S(1)}, f32[120,256]{1,0:T(8,128)S(1)}, u32[]{:S(2)}, u32[]{:S(2)}) collective-permute-start(f32[120,256]{1,0:T(8,128)S(1)} %get-tuple-element.96), channel_id=1, source_target_pairs={{0,240},{16,32},{32,16},{48,64},{64,48},{80,96},{96,80},{112,128},... | collective-permute-start | bytes 368648 | tf_op jit(solution)/shard_map/ppermute | solution.py:646
  29.7 6.7 %collective-permute-start.7 = (f32[120,256]{1,0:T(8,128)S(1)}, f32[120,256]{1,0:T(8,128)S(1)}, u32[]{:S(2)}, u32[]{:S(2)}) collective-permute-start(f32[120,256]{1,0:T(8,128)S(1)} %get-tuple-element.95), channel_id=1, source_target_pairs={{0,16},{16,0},{32,48},{48,32},{64,80},{80,64},{96,112},{112,96},{1... | collective-permute-start | bytes 368648 | tf_op jit(solution)/shard_map/ppermute | solution.py:645
  38.2 6.1 %collective-permute-start.8 = (f32[5,16,256]{2,1,0:T(8,128)S(1)}, f32[5,16,256]{2,1,0:T(8,128)S(1)}, u32[]{:S(2)}, u32[]{:S(2)}) collective-permute-start(f32[5,16,256]{2,1,0:T(8,128)S(1)} %get-tuple-element.104), channel_id=1, source_target_pairs={{0,15},{1,2},{2,1},{3,4},{4,3},{5,6},{6,5},{7,8},{8,7},{9,10},{10,... | collective-permute-start | bytes 245768 | tf_op jit(solution)/shard_map/ppermute | solution.py:646
  40.0 4.2 %collective-permute-start.9 = (f32[5,16,256]{2,1,0:T(8,128)S(1)}, f32[5,16,256]{2,1,0:T(8,128)S(1)}, u32[]{:S(2)}, u32[]{:S(2)}) collective-permute-start(f32[5,16,256]{2,1,0:T(8,128)S(1)} %get-tuple-element.103), channel_id=1, source_target_pairs={{0,1},{1,0},{2,3},{3,2},{4,5},{5,4},{6,7},{7,6},{8,9},{9,8},{10,11... | collective-permute-start | bytes 245768 | tf_op jit(solution)/shard_map/ppermute | solution.py:645
  44.4 8.1 %collective-permute-start.10 = (f32[136,256]{1,0:T(8,128)S(1)}, f32[136,256]{1,0:T(8,128)S(1)}, u32[]{:S(2)}, u32[]{:S(2)}) collective-permute-start(f32[136,256]{1,0:T(8,128)S(1)} %get-tuple-element.92), channel_id=1, source_target_pairs={{0,240},{16,32},{32,16},{48,64},{64,48},{80,96},{96,80},{112,128},... | collective-permute-start | bytes 417800 | tf_op jit(solution)/shard_map/ppermute | solution.py:646
  47.4 8.2 %collective-permute-start.11 = (f32[136,256]{1,0:T(8,128)S(1)}, f32[136,256]{1,0:T(8,128)S(1)}, u32[]{:S(2)}, u32[]{:S(2)}) collective-permute-start(f32[136,256]{1,0:T(8,128)S(1)} %get-tuple-element.91), channel_id=1, source_target_pairs={{0,16},{16,0},{32,48},{48,32},{64,80},{80,64},{96,112},{112,96},{1... | collective-permute-start | bytes 417800 | tf_op jit(solution)/shard_map/ppermute | solution.py:645

commit v5 on v4

--- a/solution.py
+++ b/solution.py
@@ -354,92 +354,154 @@
         xb[LINE + 4:, :] = jnp.zeros((4, Z), F32)
 
 
-def transport_kernel(mom, cond, base, wx, wy, wy_low, wz, wall, yh_lo, yh_hi, xh_lo, xh_hi, yb_lo, yb_hi, xb_lo, xb_hi,
-                     fx_lo, fx_hi, fy_lo, fy_hi, conc_out, src, sy_lo, sy_hi, drift, lines, low, dy_hi, own_dy):
+def velocity(conductance, density, momentum):
+    return jnp.where(conductance > 0.0, momentum / density, 0.0)
+
+
+def full_moment(mom, m, x, below, above):
+    v = mom[m, x] + jnp.where(rows() == 0, spread(row_of(below[m], x)), 0.0)
+    return v + jnp.where(rows() == N - 1, spread(row_of(above[m], x)), 0.0)
+
+
+def inner_kernel(charge, classes_h, mob, solid, conc, pot, fx_lo, fx_hi, fy_lo, fy_hi, gy_lo, mom, yh_lo, yh_hi, yb_lo, yb_hi,
+                 base, wx, wy, wy_low, wz, wall, cond, drift, src, sy_lo, sy_hi, low, adv, classes, sem):
+    fetch = pltpu.make_async_copy(classes_h, classes, sem)
+    fetch.start()
+    row = rows()
+
+    def faces(ref):
+        return tuple(ref[RING + q] for q in range(3)) + (ref[0],)
+
+    rest, weight = flux(faces(fy_lo), faces(gy_lo))
+    for s in range(2):
+        low[s] = rest[s]
+        wy_low[s] = weight[s]
+    upper = faces(fy_hi)
+    for x in range(N):
+        cond[x] = jnp.where(solid[x] == 0, jnp.sqrt(mob[x]), 0.0)
+    below, above = y_terms(yh_lo, yh_hi)
+    for x in range(1, N - 1):
+        scale = jnp.where(cond[x] > 0.0, 1.0 / full_moment(mom, 0, x, below, above), 0.0)
+        for a in range(3):
+            drift[a, x] = full_moment(mom, a + 1, x, below, above) * scale
+    from_hi, from_lo = y_terms(yb_hi, yb_lo)
+    dy_lo = velocity(fy_lo[RING + 2], plane(yh_lo, 5) + from_lo[0], plane(yh_lo, 6) + from_lo[2])
+    dy_hi = velocity(fy_hi[RING + 2], plane(yh_hi, 5) + from_hi[0], plane(yh_hi, 6) + from_hi[2])
+    for x in range(1, N - 1):
+        carried = row_of(dy_lo, x) + drift[1, x, 0:1, :]
+        for s in range(2):
+            adv[s, x:x + 1, :] = wy_low[s, x:x + 1, :] * carried
+
+    def fields(x):
+        return (conc[0, x], conc[1, x], cond[x], pot[x])
+
+    behind, weight = flux(faces(fx_lo), fields(0))
+    for s in range(2):
+        wx[s, 0] = weight[s]
+    fetch.wait()
+    for x in range(N):
+        known = 1 <= x <= N - 2
+        me = fields(x)
+        ahead, weight = flux(me, fields(x + 1) if x < N - 1 else faces(fx_hi))
+        if 1 <= x <= N - 3:
+            carried = drift[0, x] + drift[0, x + 1]
+            ahead = [ahead[s] + weight[s] * carried for s in range(2)]
+        elif x in (0, N - 2):
+            for s in range(2):
+                wx[s, 1 if x == 0 else 2] = weight[s]
+        else:
+            for s in range(2):
+                wx[s, 3] = weight[s]
+        tot = [ahead[s] - behind[s] for s in range(2)]
+        behind = ahead
+        nxt = tuple(jnp.where(row == N - 1, spread(row_of(upper[q], x)), roll_y(me[q], -1)) for q in range(4))
+        rest, weight = flux(me, nxt)
+        first = [low[s, x:x + 1, :] for s in range(2)]
+        if known:
+            v = drift[1, x]
+            carried = v + jnp.where(row == N - 1, spread(row_of(dy_hi, x)), roll_y(v, -1))
+            rest = [rest[s] + weight[s] * carried for s in range(2)]
+            first = [first[s] + adv[s, x:x + 1, :] for s in range(2)]
+        else:
+            for s in range(2):
+                wy[s, x // (N - 1)] = weight[s]
+        for s in range(2):
+            tot[s] = tot[s] + (rest[s] - jnp.where(row == 0, spread(first[s]), roll_y(rest[s], 1)))
+        rest, weight = flux(me, tuple(roll_z(v, -1) for v in me))
+        if known:
+            v = drift[2, x]
+            carried = v + roll_z(v, -1)
+            rest = [rest[s] + weight[s] * carried for s in range(2)]
+        else:
+            for s in range(2):
+                wz[s, x // (N - 1)] = weight[s]
+        for s in range(2):
+            tot[s] = tot[s] + (rest[s] - roll_z(rest[s], 1))
+            base[s, x] = me[s] - tot[s]
+        cls = classes[x]
+        total = jnp.zeros((N, Z), F32)
+        for q in range(4):
+            total = total + jnp.where(cls == q, charge[q], 0.0)
+        if 2 <= x <= N - 3:
+            source_plane(x, jnp.where(cond[x] > 0.0, me[0] - tot[0] - (me[1] - tot[1]), total), src, sy_lo, sy_hi)
+        else:
+            wall[x] = total
+
+
+def source_plane(x, v, src, sy_lo, sy_hi):
+    src[x] = v
+    for r in range(RING - 1):
+        sy_lo[r, x:x + 1, :] = row_of(v, r)
+        sy_hi[r, x:x + 1, :] = row_of(v, N - 1 - r)
+
+
+def transport_kernel(mom, cond, base, wx, wy, wy_low, wz, wall, drift, src0, sy_lo0, sy_hi0,
+                     yh_lo, yh_hi, xh_lo, xh_hi, yb_lo, yb_hi, xb_lo, xb_hi,
+                     fx_lo, fx_hi, fy_lo, fy_hi, conc_out, src, sy_lo, sy_hi):
     row = rows()
     below, above = y_terms(yh_lo, yh_hi)
-    for m in range(4):
-        lines[m] = below[m]
-        lines[4 + m] = above[m]
-
-    def step(x, extra):
-        here = pl.ds(x, 1)
-
-        def full(m):
-            v = mom[m, x]
-            if extra is not None:
-                v = v + extra[m]
-            v = v + jnp.where(row == 0, spread(lines[m, here, :]), 0.0)
-            return v + jnp.where(row == N - 1, spread(lines[4 + m, here, :]), 0.0)
-
-        scale = jnp.where(cond[x] > 0.0, 1.0 / full(0), 0.0)
-        drift[0, x] = full(1) * scale
-        v = full(2) * scale
-        drift[1, x] = v
-        drift[2, x] = full(3) * scale
-        own_dy[here, :] = row_of(v, 0)
-
-    a = [plane(xh_lo, q) for q in range(5)]
-    total = a[0] + a[1] + a[2] + a[3] + a[4]
-    step(0, (total, total, a[1] - a[2], a[3] - a[4]))
-    b = [plane(xh_hi, q) for q in range(5)]
-    total = b[0] + b[1] + b[2] + b[3] + b[4]
-    step(N - 1, (total, -total, b[2] - b[1], b[4] - b[3]))
-
-    def loop(x, carry):
-        step(x, None)
-        return carry
-
-    lax.fori_loop(1, N - 1, loop, 0, unroll=2)
-
-    def velocity(conductance, density, momentum):
-        return jnp.where(conductance > 0.0, momentum / density, 0.0)
-
-    def x_face(fx, xh, xb, sign):
+    sy_lo[...] = sy_lo0[...]
+    sy_hi[...] = sy_hi0[...]
+    for x in range(2, N - 2):
+        src[x] = src0[x]
+        for s in range(2):
+            conc_out[s, x] = base[s, x]
+    from_hi, from_lo = y_terms(yb_hi, yb_lo)
+
+    def y_line(fy, yh, terms, k, xh, x):
+        density = line(yh, 5, x) + row_of(terms[0], x) + xh[k:k + 1, :]
+        momentum = line(yh, 6, x) + row_of(terms[2], x) + xh[k + 1:k + 2, :]
+        return velocity(fy[RING + 2, x:x + 1, :], density, momentum)
+
+    for x, near, xh, xb, fx, sign in ((0, 1, xh_lo, xb_lo, fx_lo, 1.0), (N - 1, N - 2, xh_hi, xb_hi, fx_hi, -1.0)):
+        a = [plane(xh, q) for q in range(5)]
+        total = a[0] + a[1] + a[2] + a[3] + a[4]
+        extra = (total, sign * total, sign * (a[1] - a[2]), sign * (a[3] - a[4]))
+        full = [full_moment(mom, m, x, below, above) + extra[m] for m in range(4)]
+        scale = jnp.where(cond[x] > 0.0, 1.0 / full[0], 0.0)
+        d = [full[m] * scale for m in (1, 2, 3)]
         out = plane(xb, 0) + plane(xb, 1) + plane(xb, 2) + plane(xb, 3) + plane(xb, 4)
-        return velocity(fx[RING + 2], plane(xh, 5) + out, plane(xh, 6) + sign * out)
-
-    from_hi, from_lo = y_terms(yb_hi, yb_lo)
-
-    def y_face(fy, yh, terms, k):
-        density = plane(yh, 5) + terms[0]
-        momentum = plane(yh, 6) + terms[2]
-        for xh, x in ((xh_lo, 0), (xh_hi, N - 1)):
-            density = density + jnp.where(row == x, spread(xh[k:k + 1, :]), 0.0)
-            momentum = momentum + jnp.where(row == x, spread(xh[k + 1:k + 2, :]), 0.0)
-        return velocity(fy[RING + 2], density, momentum)
-
-    carried = y_face(fy_lo, yh_lo, from_lo, LINE) + own_dy[...]
-    for s in range(2):
-        low[s] = wy_low[s] * carried
-    dy_hi[...] = y_face(fy_hi, yh_hi, from_hi, LINE + 2)
-    carried = x_face(fx_lo, xh_lo, xb_lo, -1.0) + drift[0, 0]
-    behind = [wx[s, 0] * carried for s in range(2)]
-    last = x_face(fx_hi, xh_hi, xb_hi, 1.0)
-    for x in range(N):
-        carried = drift[0, x] + (drift[0, x + 1] if x < N - 1 else last)
-        ahead = [wx[s, x + 1] * carried for s in range(2)]
-        tot = [ahead[s] - behind[s] for s in range(2)]
-        behind = ahead
-        v = drift[1, x]
-        carried = v + jnp.where(row == N - 1, spread(dy_hi[x:x + 1, :]), roll_y(v, -1))
+        beyond = velocity(fx[RING + 2], plane(xh, 5) + out, plane(xh, 6) - sign * out)
+        e = x // (N - 1)
+        outer = 3 * e
+        dy_lo = y_line(fy_lo, yh_lo, from_lo, LINE, xh, x)
+        dy_hi = y_line(fy_hi, yh_hi, from_hi, LINE + 2, xh, x)
+        c, c_near = [], []
+        up = d[1] + jnp.where(row == N - 1, spread(dy_hi), roll_y(d[1], -1))
+        turn = d[2] + roll_z(d[2], -1)
         for s in range(2):
-            f = wy[s, x] * carried
-            tot[s] = tot[s] + (f - jnp.where(row == 0, spread(low[s, x:x + 1, :]), roll_y(f, 1)))
-        v = drift[2, x]
-        carried = v + roll_z(v, -1)
-        for s in range(2):
-            f = wz[s, x] * carried
-            tot[s] = tot[s] + (f - roll_z(f, 1))
-        c0 = base[0, x] - tot[0]
-        c1 = base[1, x] - tot[1]
-        conc_out[0, x] = c0
-        conc_out[1, x] = c1
-        s_val = jnp.where(cond[x] > 0.0, c0 - c1, wall[x])
-        src[x] = s_val
-        for r in range(RING - 1):
-            sy_lo[r, x:x + 1, :] = row_of(s_val, r)
-            sy_hi[r, x:x + 1, :] = row_of(s_val, N - 1 - r)
+            far = wx[s, outer] * (beyond + d[0])
+            close = wx[s, 1 + e] * (d[0] + drift[0, near])
+            f = wy[s, e] * up
+            first = wy_low[s, x:x + 1, :] * (dy_lo + row_of(d[1], 0))
+            g = wz[s, e] * turn
+            tot = sign * (close - far) + (f - jnp.where(row == 0, spread(first), roll_y(f, 1))) + (g - roll_z(g, 1))
+            c.append(base[s, x] - tot)
+            c_near.append(base[s, near] + sign * close)
+            conc_out[s, x] = c[s]
+            conc_out[s, near] = c_near[s]
+        source_plane(x, jnp.where(cond[x] > 0.0, c[0] - c[1], wall[x]), src, sy_lo, sy_hi)
+        source_plane(near, jnp.where(cond[near] > 0.0, c_near[0] - c_near[1], wall[near]), src, sy_lo, sy_hi)
 
 
 def split(ext, a, b, pairs, shift):
@@ -511,9 +573,10 @@
     lax.fori_loop(RING // 2 + 1, RING // 2 + N // 2 + 1, last, 0)
 
 
-def patch_kernel(buf, ex_lo, ex_hi, ey_lo, ey_hi, yh_lo, yh_hi, xh_lo, xh_hi, out, done, sems):
+def patch_kernel(buf, ex_lo, ex_hi, ey_lo, ey_hi, yh_lo, yh_hi, xh_lo, xh_hi, conc, out, conc_out, done, sems):
     row = rows()
-    copies = []
+    copies = [pltpu.make_async_copy(conc, conc_out, sems.at[19])]
+    copies[0].start()
     for i in range(19):
         cx, cy, _ = C[i]
 
@@ -559,54 +622,6 @@
         rest.append(link * (RATES[s] * ((a[s] - b[s]) + ((0.5 * VAL[s]) * both) * drop)))
         weight.append((0.25 * link) * both)
     return rest, weight
-
-
-def diffuse_kernel(charge, classes_h, mob, solid, conc, pot, fx_lo, fx_hi, fy_lo, fy_hi, gy_lo,
-                   base, wx, wy, wy_low, wz, wall, cond, low, classes, sem):
-    fetch = pltpu.make_async_copy(classes_h, classes, sem)
-    fetch.start()
-    row = rows()
-
-    def faces(ref):
-        return tuple(ref[RING + q] for q in range(3)) + (ref[0],)
-
-    rest, weight = flux(faces(fy_lo), faces(gy_lo))
-    for s in range(2):
-        low[s] = rest[s]
-        wy_low[s] = weight[s]
-    upper = faces(fy_hi)
-    for x in range(N):
-        cond[x] = jnp.where(solid[x] == 0, jnp.sqrt(mob[x]), 0.0)
-
-    def fields(x):
-        return (conc[0, x], conc[1, x], cond[x], pot[x])
-
-    behind, weight = flux(faces(fx_lo), fields(0))
-    for s in range(2):
-        wx[s, 0] = weight[s]
-    fetch.wait()
-    for x in range(N):
-        me = fields(x)
-        ahead, weight = flux(me, fields(x + 1) if x < N - 1 else faces(fx_hi))
-        tot = [ahead[s] - behind[s] for s in range(2)]
-        behind = ahead
-        for s in range(2):
-            wx[s, x + 1] = weight[s]
-        nxt = tuple(jnp.where(row == N - 1, spread(row_of(upper[q], x)), roll_y(me[q], -1)) for q in range(4))
-        rest, weight = flux(me, nxt)
-        for s in range(2):
-            wy[s, x] = weight[s]
-            tot[s] = tot[s] + (rest[s] - jnp.where(row == 0, spread(low[s, x:x + 1, :]), roll_y(rest[s], 1)))
-        rest, weight = flux(me, tuple(roll_z(v, -1) for v in me))
-        for s in range(2):
-            wz[s, x] = weight[s]
-            tot[s] = tot[s] + (rest[s] - roll_z(rest[s], 1))
-            base[s, x] = me[s] - tot[s]
-        cls = classes[x]
-        total = jnp.zeros((N, Z), F32)
-        for q in range(4):
-            total = total + jnp.where(cls == q, charge[q], 0.0)
-        wall[x] = total
 
 
 def ring_rows(depth, total):
@@ -669,18 +684,19 @@
     yh_lo, yh_hi = swap("gy", yb_hi, yb_lo)
     xb_lo, xb_hi = call(corner_kernel, [msg, msg], "corner", "v" * 7)(ex_lo, ex_hi, yh_lo, yh_hi, yb_lo, yb_hi, mom)
     xh_lo, xh_hi = swap("gx", xb_hi, xb_lo)
-    face = VM((N, Z), F32)
     fy_late, _ = lax.optimization_barrier((fy_lo, yh_lo))
     pair = sds(2, N, N, Z)
-    base, wx, wy, wy_low, wz, wall, cond = call(
-        diffuse_kernel, [pair, sds(2, N + 1, N, Z), pair, sds(2, N, Z), pair, cube, cube], "diffuse", "sh" + "v" * 9,
-        scratch=[VM((2, N, Z), F32), VM((N, N, Z), jnp.int32), pltpu.SemaphoreType.DMA], flops=10000000, moved=6000000)(
-        charge, classes, mob, solid, conc, pot, fx_lo, fx_hi, fy_late, fy_hi, gy_lo)
-    conc_out, src, sy_lo, sy_hi = call(
-        transport_kernel, [pair, cube, sds(RING - 1, N, Z), sds(RING - 1, N, Z)], "transport", "v" * 20,
-        scratch=[VM((3, N, N, Z), F32), VM((8, N, Z), F32), VM((2, N, Z), F32), face, face], flops=5000000, moved=4000000)(
-        mom, cond, base, wx, wy, wy_low, wz, wall, yh_lo, yh_hi, xh_lo, xh_hi, yb_lo, yb_hi, xb_lo, xb_hi,
-        fx_lo, fx_hi, fy_lo, fy_hi)
+    ring = sds(RING - 1, N, Z)
+    base, wx, wy, wy_low, wz, wall, cond, drift, src, sy_lo, sy_hi = call(
+        inner_kernel, [pair, sds(2, 4, N, Z), sds(2, 2, N, Z), sds(2, N, Z), sds(2, 2, N, Z), cube, cube, sds(3, N, N, Z), cube, ring, ring],
+        "inner", "sh" + "v" * 14,
+        scratch=[VM((2, N, Z), F32), VM((2, N, Z), F32), VM((N, N, Z), jnp.int32), pltpu.SemaphoreType.DMA],
+        flops=10000000, moved=6000000)(
+        charge, classes, mob, solid, conc, pot, fx_lo, fx_hi, fy_late, fy_hi, gy_lo, mom, yh_lo, yh_hi, yb_lo, yb_hi)
+    conc_new, src, sy_lo, sy_hi = call(
+        transport_kernel, [pair, cube, ring, ring], "transport", "v" * 24, flops=3000000, moved=4000000)(
+        mom, cond, base, wx, wy, wy_low, wz, wall, drift, src, sy_lo, sy_hi,
+        yh_lo, yh_hi, xh_lo, xh_hi, yb_lo, yb_hi, xb_lo, xb_hi, fx_lo, fx_hi, fy_lo, fy_hi)
     ys_lo, ys_hi = swap("gy", sy_hi, sy_lo)
     bs_hi, bs_lo = call(pack_src_kernel, [sds(SRC_LEN, Z)] * 2, "pack_src", "v" * 5)(src, ys_lo, ys_hi, fy_lo, fy_hi)
     xs_lo, xs_hi = swap("gx", bs_hi, bs_lo)
@@ -692,10 +708,10 @@
         sweep_kernel, [cube], "sweep", "v" * 8,
         scratch=[VM((N + 2 * RING, N + 2 * OFF, Z), F32)] + [packed] * 4, flops=20000000, moved=4000000)(
         *prepared, fx_lo, fx_hi, xs_lo, xs_hi)[0]
-    pop = call(
-        patch_kernel, [sds(19, N, N, Z)], "patch", "v" * 9, out_specs="h",
-        scratch=[VM((19, N, N, Z), F32), pltpu.SemaphoreType.DMA((19,))], mib=16, moved=10000000)(
-        buf, ex_lo, ex_hi, ey_lo, ey_hi, yh_lo, yh_hi, xh_lo, xh_hi)[0]
+    pop, conc_out = call(
+        patch_kernel, [sds(19, N, N, Z), pair], "patch", "v" * 10, out_specs="hh",
+        scratch=[VM((19, N, N, Z), F32), pltpu.SemaphoreType.DMA((20,))], mib=16, moved=10000000)(
+        buf, ex_lo, ex_hi, ey_lo, ey_hi, yh_lo, yh_hi, xh_lo, xh_hi, conc_new)
     return (pop, conc_out, potential_out)
 
 

time: 57.8 us -> 56.4 us (0.976)
  Pallas kernels: 15.4 us -> 14.4 us
    pallas_call x3, Pallas kernels: 6.23 us -> 5.18 us  [the longest x1 2.57 us: body(): call(patch_kernel, [sds(19, N, N, Z), pair], 'patch', 'v' * 10, out_specs...]
  transfers between devices with their start and end apart: 12 -> 12, of which waited for: 8 -> 8; matrix products, arithmetic and copies ran while one was open for 0% -> 0% of each run, Pallas kernels for 16% -> 17%
where the time goes in v5:
time: 56.4 us; the launch traced here: 56.3 us
  waiting for transfers between devices  20.5 us (36%)
  starting transfers between devices  20.2 us (36%)
  Pallas kernels  14.4 us (26%)
  between operations  0.86 us (2%)
    ppermute x6, starting transfers between devices, swap(): lax.ppermute(jnp.where(even, lo, hi), axis, [(i, (i - 1 + 2 * (i % 2)) %...  20.2 us
    ppermute x6, waiting for transfers between devices, swap(): lax.ppermute(jnp.where(even, lo, hi), axis, [(i, (i - 1 + 2 * (i % 2)) %...  13.6 us
    ppermute x6, waiting for transfers between devices, swap(): lax.ppermute(jnp.where(even, hi, lo), axis, [(i, i + 1 - 2 * (i % 2)) for...  6.89 us
    pallas_call x1, Pallas kernels, body(): call(collide_kernel, [sds(19, N, N, Z), sds(4, N, N, Z)] + [sds(19, N, Z)...  4.22 us
    pallas_call x1, Pallas kernels, body(): call(patch_kernel, [sds(19, N, N, Z), pair], 'patch', 'v' * 10, out_specs...  2.57 us
    pallas_call x1, Pallas kernels, body(): call(inner_kernel, [pair, sds(2, 4, N, Z), sds(2, 2, N, Z), sds(2, N, Z),...  2.34 us
    pallas_call x1, Pallas kernels, body(): call(sweep_kernel, [cube], 'sweep', 'v' * 8, scratch=[VM((N + 2 * RING, N...  2.11 us
    pallas_call x1, Pallas kernels, body(): call(faces_kernel, [sds(RING + 3, N, Z)] * 4 + [cube, sds(N - 2 * RING, N...  1.56 us
  transfers between devices with their start and end apart: 12, of which 8 were waited for; matrix products, arithmetic and copies ran while one was open for 0% of the time, Pallas kernels for 17%

profile of v5, /device:TPU:7, one launch (start us, length us, event | category | flops | bytes accessed | tf_op | source)
XLA Modules:
  0.0 56.3 jit_solution(1024495957865701206)
XLA Ops:
  0.6 1.6 %faces.1 = (f32[9,16,256]{2,1,0:T(8,128)S(1)}, f32[9,16,256]{2,1,0:T(8,128)S(1)}, f32[9,16,256]{2,1,0:T(8,128)S(1)}, f32[9,16,256]{2,1,0:T(8,128)S(1)}, f32[16,1...) custom-call(f32[16,16,256]{2,1,0:T(8,128)} %pot.3, f32[2,16,16,256]{3,2,1,0:T(8,128)} %conc.1, f32[16,16,256]{2,1,0:T(8,128)} %mob.1, ...), custom_call_target="tpu_custom_call" | custom-call | bytes 2600000 | tf_op jit(solution)/shard_map/faces/pallas_call | solution.py:668
  2.2 8.3 %collective-permute-start = (f32[9,16,256]{2,1,0:T(8,128)S(1)}, f32[9,16,256]{2,1,0:T(8,128)S(1)}, u32[]{:S(2)}, u32[]{:S(2)}) collective-permute-start(f32[9,16,256]{2,1,0:T(8,128)S(1)} %get-tuple-element.100), channel_id=1, source_target_pairs={{0,240},{16,32},{32,16},{48,64},{64,48},{80,96},{96,80},{112,128},... | collective-permute-start | bytes 442376 | tf_op jit(solution)/shard_map/ppermute | solution.py:661
  10.5 0.0 collective-permute-start.1
  10.6 1.2 %collective-permute-start.2 = (f32[9,16,256]{2,1,0:T(8,128)S(1)}, f32[9,16,256]{2,1,0:T(8,128)S(1)}, u32[]{:S(2)}, u32[]{:S(2)}) collective-permute-start(f32[9,16,256]{2,1,0:T(8,128)S(1)} %get-tuple-element.96), channel_id=1, source_target_pairs={{0,15},{1,2},{2,1},{3,4},{4,3},{5,6},{6,5},{7,8},{8,7},{9,10},{10,... | collective-permute-start | bytes 442376 | tf_op jit(solution)/shard_map/ppermute | solution.py:661
  11.8 0.0 collective-permute-start.3
  11.8 4.2 %collide.1 = (f32[19,16,16,256]{3,2,1,0:T(8,128)S(1)}, f32[4,16,16,256]{3,2,1,0:T(8,128)S(1)}, f32[19,16,256]{2,1,0:T(8,128)S(1)}, f32[19,16,256]{2,1,0:T(8,128)...) custom-call(f32[19,16,16,256]{3,2,1,0:T(8,128)} %pops.1, f32[9,16,256]{2,1,0:T(8,128)S(1)} %get-tuple-element.48.gx_hi, ...), custom_call_target="tpu_custom_call" | custom-call | flops 20000000 | bytes 14000000 | tf_op jit(solution)/shard_map/collide/pallas_call | solution.py:677
  16.0 0.0 copy-start
  16.1 0.0 copy-start.1
  16.1 0.0 copy-start.2
  16.1 0.0 copy-start.3
  16.1 0.0 copy-start.4
  16.1 0.0 copy-start.5
  16.1 0.7 %collective-permute-done.1 = f32[9,16,256]{2,1,0:T(8,128)S(1)} collective-permute-done((f32[9,16,256]{2,1,0:T(8,128)S(1)}, f32[9,16,256]{2,1,0:T(8,128)S(1)}, u32[]{:S(2)}, u32[]{:S(2)}) %collective-permute-start.1) | collective-permute-done | bytes 147488 | tf_op jit(solution)/shard_map/ppermute | solution.py:660
  16.9 0.8 %collective-permute-done.2 = f32[9,16,256]{2,1,0:T(8,128)S(1)} collective-permute-done((f32[9,16,256]{2,1,0:T(8,128)S(1)}, f32[9,16,256]{2,1,0:T(8,128)S(1)}, u32[]{:S(2)}, u32[]{:S(2)}) %collective-permute-start.2) | collective-permute-done | bytes 147488 | tf_op jit(solution)/shard_map/ppermute | solution.py:661
  17.7 1.0 %edge.1 = (f32[4,16,16,256]{3,2,1,0:T(8,128)S(1)}, f32[19,16,256]{2,1,0:T(8,128)S(1)}, f32[19,16,256]{2,1,0:T(8,128)S(1)}, f32[19,16,256]{2,1,0:T(8,128)S(1)}, f...) custom-call(f32[19,16,256]{2,1,0:T(8,128)S(1)} %get-tuple-element.53.px_lo, ...), custom_call_target="tpu_custom_call" | custom-call | bytes 3000000 | tf_op jit(solution)/shard_map/edge/pallas_call | solution.py:681
  18.7 1.3 %collective-permute-start.4 = (f32[120,256]{1,0:T(8,128)S(1)}, f32[120,256]{1,0:T(8,128)S(1)}, u32[]{:S(2)}, u32[]{:S(2)}) collective-permute-start(f32[120,256]{1,0:T(8,128)S(1)} %get-tuple-element.112), channel_id=1, source_target_pairs={{0,15},{1,2},{2,1},{3,4},{4,3},{5,6},{6,5},{7,8},{8,7},{9,10},{10,... | collective-permute-start | bytes 368648 | tf_op jit(solution)/shard_map/ppermute | solution.py:661
  20.0 5.2 %collective-permute-done.4 = f32[120,256]{1,0:T(8,128)S(1)} collective-permute-done((f32[120,256]{1,0:T(8,128)S(1)}, f32[120,256]{1,0:T(8,128)S(1)}, u32[]{:S(2)}, u32[]{:S(2)}) %collective-permute-start.4) | collective-permute-done | bytes 122912 | tf_op jit(solution)/shard_map/ppermute | solution.py:661
  25.3 4.5 %collective-permute-start.6 = (f32[120,256]{1,0:T(8,128)S(1)}, f32[120,256]{1,0:T(8,128)S(1)}, u32[]{:S(2)}, u32[]{:S(2)}) collective-permute-start(f32[120,256]{1,0:T(8,128)S(1)} %get-tuple-element.108), channel_id=1, source_target_pairs={{0,240},{16,32},{32,16},{48,64},{64,48},{80,96},{96,80},{112,128},... | collective-permute-start | bytes 368648 | tf_op jit(solution)/shard_map/ppermute | solution.py:661
  29.8 2.3 %inner.1 = (f32[2,16,16,256]{3,2,1,0:T(8,128)S(1)}, f32[2,4,16,256]{3,2,1,0:T(8,128)S(1)}, f32[2,2,16,256]{3,2,1,0:T(8,128)S(1)}, f32[2,16,256]{2,1,0:T(8,128)S(...) custom-call(f32[4]{0:T(128)S(1)} %copy-done.5, ...), custom_call_target="tpu_custom_call" | custom-call | flops 10000000 | bytes 6000000 | tf_op jit(solution)/shard_map/inner/pallas_call | solution.py:690
  32.1 1.2 %collective-permute-done.6 = f32[120,256]{1,0:T(8,128)S(1)} collective-permute-done((f32[120,256]{1,0:T(8,128)S(1)}, f32[120,256]{1,0:T(8,128)S(1)}, u32[]{:S(2)}, u32[]{:S(2)}) %collective-permute-start.6) | collective-permute-done | bytes 122912 | tf_op jit(solution)/shard_map/ppermute | solution.py:661
  33.3 3.1 %collective-permute-done.7 = f32[120,256]{1,0:T(8,128)S(1)} collective-permute-done((f32[120,256]{1,0:T(8,128)S(1)}, f32[120,256]{1,0:T(8,128)S(1)}, u32[]{:S(2)}, u32[]{:S(2)}) %collective-permute-start.7) | collective-permute-done | bytes 122912 | tf_op jit(solution)/shard_map/ppermute | solution.py:660
  36.4 0.3 transport.1
  36.7 1.8 %collective-permute-start.8 = (f32[5,16,256]{2,1,0:T(8,128)S(1)}, f32[5,16,256]{2,1,0:T(8,128)S(1)}, u32[]{:S(2)}, u32[]{:S(2)}) collective-permute-start(f32[5,16,256]{2,1,0:T(8,128)S(1)} %get-tuple-element.116), channel_id=1, source_target_pairs={{0,15},{1,2},{2,1},{3,4},{4,3},{5,6},{6,5},{7,8},{8,7},{9,10},{10,... | collective-permute-start | bytes 245768 | tf_op jit(solution)/shard_map/ppermute | solution.py:661
  38.5 0.0 collective-permute-start.9
  38.5 4.2 %collective-permute-done.8 = f32[5,16,256]{2,1,0:T(8,128)S(1)} collective-permute-done((f32[5,16,256]{2,1,0:T(8,128)S(1)}, f32[5,16,256]{2,1,0:T(8,128)S(1)}, u32[]{:S(2)}, u32[]{:S(2)}) %collective-permute-start.8) | collective-permute-done | bytes 81952 | tf_op jit(solution)/shard_map/ppermute | solution.py:661
  42.8 0.1 pack_src.1
  42.9 3.0 %collective-permute-start.10 = (f32[136,256]{1,0:T(8,128)S(1)}, f32[136,256]{1,0:T(8,128)S(1)}, u32[]{:S(2)}, u32[]{:S(2)}) collective-permute-start(f32[136,256]{1,0:T(8,128)S(1)} %get-tuple-element.104), channel_id=1, source_target_pairs={{0,240},{16,32},{32,16},{48,64},{64,48},{80,96},{96,80},{112,128},... | collective-permute-start | bytes 417800 | tf_op jit(solution)/shard_map/ppermute | solution.py:661
  45.9 2.6 %patch.1 = (f32[19,16,16,256]{3,2,1,0:T(8,128)}, f32[2,16,16,256]{3,2,1,0:T(8,128)}) custom-call(f32[19,16,16,256]{3,2,1,0:T(8,128)S(1)} %get-tuple-element.52.buf, f32[19,16,256]{2,1,0:T(8,128)S(1)} %get-tuple-element.60.ex_lo, f32[19,16,256]{2,1,0:T(8,128)S(1)} %get-tuple-element.61.ex_hi, f32[19,16,256]{2,1,0:T(8,128)S(1)} %get-tuple-element.62.ey_lo, ...), custom_call_target="tpu_custom_call" | custom-call | bytes 10000000 | tf_op jit(solution)/shard_map/patch/pallas_call | solution.py:711
  48.5 0.3 prepare.1
  48.8 2.3 %collective-permute-done.10 = f32[136,256]{1,0:T(8,128)S(1)} collective-permute-done((f32[136,256]{1,0:T(8,128)S(1)}, f32[136,256]{1,0:T(8,128)S(1)}, u32[]{:S(2)}, u32[]{:S(2)}) %collective-permute-start.10) | collective-permute-done | bytes 139296 | tf_op jit(solution)/shard_map/ppermute | solution.py:661
  51.0 3.1 %collective-permute-done.11 = f32[136,256]{1,0:T(8,128)S(1)} collective-permute-done((f32[136,256]{1,0:T(8,128)S(1)}, f32[136,256]{1,0:T(8,128)S(1)}, u32[]{:S(2)}, u32[]{:S(2)}) %collective-permute-start.11) | collective-permute-done | bytes 139296 | tf_op jit(solution)/shard_map/ppermute | solution.py:660
  54.1 2.1 %sweep.1 = f32[16,16,256]{2,1,0:T(8,128)} custom-call(f32[8,32,256]{2,1,0:T(8,128)S(1)} %get-tuple-element.87.even_in, f32[8,32,256]{2,1,0:T(8,128)S(1)} %get-tuple-element.88.odd_in, f32[8,32,256]{2,1,0:T(8,128)S(1)} %get-tuple-element.89.s_even_in, f32[8,32,256]{2,1,0:T(8,128)S(1)} %get-tuple-element.90.s_odd_in, ...), custom_call_target="tpu_custom_call" | custom-call | flops 20000000 | bytes 4000000 | tf_op jit(solution)/shard_map/sweep/pallas_call | solution.py:707
  (26 shorter events, 0.3 us)
Async XLA Ops:
  2.2 13.9 %collective-permute-start = (f32[9,16,256]{2,1,0:T(8,128)S(1)}, f32[9,16,256]{2,1,0:T(8,128)S(1)}, u32[]{:S(2)}, u32[]{:S(2)}) collective-permute-start(f32[9,16,256]{2,1,0:T(8,128)S(1)} %get-tuple-element.100), channel_id=1, source_target_pairs={{0,240},{16,32},{32,16},{48,64},{64,48},{80,96},{96,80},{112,128},... | collective-permute-start | bytes 442376 | tf_op jit(solution)/shard_map/ppermute | solution.py:661
  10.5 6.3 %collective-permute-start.1 = (f32[9,16,256]{2,1,0:T(8,128)S(1)}, f32[9,16,256]{2,1,0:T(8,128)S(1)}, u32[]{:S(2)}, u32[]{:S(2)}) collective-permute-start(f32[9,16,256]{2,1,0:T(8,128)S(1)} %get-tuple-element.99), channel_id=1, source_target_pairs={{0,16},{16,0},{32,48},{48,32},{64,80},{80,64},{96,112},{112,96},{1... | collective-permute-start | bytes 442376 | tf_op jit(solution)/shard_map/ppermute | solution.py:660
  10.6 7.1 %collective-permute-start.2 = (f32[9,16,256]{2,1,0:T(8,128)S(1)}, f32[9,16,256]{2,1,0:T(8,128)S(1)}, u32[]{:S(2)}, u32[]{:S(2)}) collective-permute-start(f32[9,16,256]{2,1,0:T(8,128)S(1)} %get-tuple-element.96), channel_id=1, source_target_pairs={{0,15},{1,2},{2,1},{3,4},{4,3},{5,6},{6,5},{7,8},{8,7},{9,10},{10,... | collective-permute-start | bytes 442376 | tf_op jit(solution)/shard_map/ppermute | solution.py:661
  11.8 5.8 %collective-permute-start.3 = (f32[9,16,256]{2,1,0:T(8,128)S(1)}, f32[9,16,256]{2,1,0:T(8,128)S(1)}, u32[]{:S(2)}, u32[]{:S(2)}) collective-permute-start(f32[9,16,256]{2,1,0:T(8,128)S(1)} %get-tuple-element.95), channel_id=1, source_target_pairs={{0,1},{1,0},{2,3},{3,2},{4,5},{5,4},{6,7},{7,6},{8,9},{9,8},{10,11... | collective-permute-start | bytes 442376 | tf_op jit(solution)/shard_map/ppermute | solution.py:660
  16.0 13.7 %copy-start = (f32[16,16,256]{2,1,0:T(8,128)S(1)}, f32[16,16,256]{2,1,0:T(8,128)}, u32[]{:S(2)}) copy-start(f32[16,16,256]{2,1,0:T(8,128)} %pot.3) | copy-start | bytes 786436
  16.1 13.7 %copy-start.1 = (f32[2,16,16,256]{3,2,1,0:T(8,128)S(1)}, f32[2,16,16,256]{3,2,1,0:T(8,128)}, u32[]{:S(2)}) copy-start(f32[2,16,16,256]{3,2,1,0:T(8,128)} %conc.1) | copy-start | bytes 1572868
  16.1 13.7 %copy-start.2 = (f32[16,16,256]{2,1,0:T(8,128)S(1)}, f32[16,16,256]{2,1,0:T(8,128)}, u32[]{:S(2)}) copy-start(f32[16,16,256]{2,1,0:T(8,128)} %mob.1) | copy-start | bytes 786436
  16.1 13.7 %copy-start.3 = (s32[16,16,256]{2,1,0:T(8,128)S(1)}, s32[16,16,256]{2,1,0:T(8,128)}, u32[]{:S(2)}) copy-start(s32[16,16,256]{2,1,0:T(8,128)} %solid.1) | copy-start | bytes 786436
  16.1 13.7 %copy-start.4 = (s32[16,16,256]{2,1,0:T(8,128)S(1)}, s32[16,16,256]{2,1,0:T(8,128)}, u32[]{:S(2)}) copy-start(s32[16,16,256]{2,1,0:T(8,128)} %classes_h.1) | copy-start | bytes 786436
  16.1 13.7 %copy-start.5 = (f32[4]{0:T(128)S(1)}, f32[4]{0:T(128)}, u32[]{:S(2)}) copy-start(f32[4]{0:T(128)} %charge.1) | copy-start | bytes 52
  18.7 6.5 %collective-permute-start.4 = (f32[120,256]{1,0:T(8,128)S(1)}, f32[120,256]{1,0:T(8,128)S(1)}, u32[]{:S(2)}, u32[]{:S(2)}) collective-permute-start(f32[120,256]{1,0:T(8,128)S(1)} %get-tuple-element.112), channel_id=1, source_target_pairs={{0,15},{1,2},{2,1},{3,4},{4,3},{5,6},{6,5},{7,8},{8,7},{9,10},{10,... | collective-permute-start | bytes 368648 | tf_op jit(solution)/shard_map/ppermute | solution.py:661
  20.0 5.2 %collective-permute-start.5 = (f32[120,256]{1,0:T(8,128)S(1)}, f32[120,256]{1,0:T(8,128)S(1)}, u32[]{:S(2)}, u32[]{:S(2)}) collective-permute-start(f32[120,256]{1,0:T(8,128)S(1)} %get-tuple-element.111), channel_id=1, source_target_pairs={{0,1},{1,0},{2,3},{3,2},{4,5},{5,4},{6,7},{7,6},{8,9},{9,8},{10,11... | collective-permute-start | bytes 368648 | tf_op jit(solution)/shard_map/ppermute | solution.py:660
  25.3 8.0 %collective-permute-start.6 = (f32[120,256]{1,0:T(8,128)S(1)}, f32[120,256]{1,0:T(8,128)S(1)}, u32[]{:S(2)}, u32[]{:S(2)}) collective-permute-start(f32[120,256]{1,0:T(8,128)S(1)} %get-tuple-element.108), channel_id=1, source_target_pairs={{0,240},{16,32},{32,16},{48,64},{64,48},{80,96},{96,80},{112,128},... | collective-permute-start | bytes 368648 | tf_op jit(solution)/shard_map/ppermute | solution.py:661
  29.7 6.7 %collective-permute-start.7 = (f32[120,256]{1,0:T(8,128)S(1)}, f32[120,256]{1,0:T(8,128)S(1)}, u32[]{:S(2)}, u32[]{:S(2)}) collective-permute-start(f32[120,256]{1,0:T(8,128)S(1)} %get-tuple-element.107), channel_id=1, source_target_pairs={{0,16},{16,0},{32,48},{48,32},{64,80},{80,64},{96,112},{112,96},{1... | collective-permute-start | bytes 368648 | tf_op jit(solution)/shard_map/ppermute | solution.py:660
  36.7 6.1 %collective-permute-start.8 = (f32[5,16,256]{2,1,0:T(8,128)S(1)}, f32[5,16,256]{2,1,0:T(8,128)S(1)}, u32[]{:S(2)}, u32[]{:S(2)}) collective-permute-start(f32[5,16,256]{2,1,0:T(8,128)S(1)} %get-tuple-element.116), channel_id=1, source_target_pairs={{0,15},{1,2},{2,1},{3,4},{4,3},{5,6},{6,5},{7,8},{8,7},{9,10},{10,... | collective-permute-start | bytes 245768 | tf_op jit(solution)/shard_map/ppermute | solution.py:661
  38.5 4.2 %collective-permute-start.9 = (f32[5,16,256]{2,1,0:T(8,128)S(1)}, f32[5,16,256]{2,1,0:T(8,128)S(1)}, u32[]{:S(2)}, u32[]{:S(2)}) collective-permute-start(f32[5,16,256]{2,1,0:T(8,128)S(1)} %get-tuple-element.115), channel_id=1, source_target_pairs={{0,1},{1,0},{2,3},{3,2},{4,5},{5,4},{6,7},{7,6},{8,9},{9,8},{10,11... | collective-permute-start | bytes 245768 | tf_op jit(solution)/shard_map/ppermute | solution.py:660
  42.9 8.1 %collective-permute-start.10 = (f32[136,256]{1,0:T(8,128)S(1)}, f32[136,256]{1,0:T(8,128)S(1)}, u32[]{:S(2)}, u32[]{:S(2)}) collective-permute-start(f32[136,256]{1,0:T(8,128)S(1)} %get-tuple-element.104), channel_id=1, source_target_pairs={{0,240},{16,32},{32,16},{48,64},{64,48},{80,96},{96,80},{112,128},... | collective-permute-start | bytes 417800 | tf_op jit(solution)/shard_map/ppermute | solution.py:661
  45.9 8.2 %collective-permute-start.11 = (f32[136,256]{1,0:T(8,128)S(1)}, f32[136,256]{1,0:T(8,128)S(1)}, u32[]{:S(2)}, u32[]{:S(2)}) collective-permute-start(f32[136,256]{1,0:T(8,128)S(1)} %get-tuple-element.103), channel_id=1, source_target_pairs={{0,16},{16,0},{32,48},{48,32},{64,80},{80,64},{96,112},{112,96},{1... | collective-permute-start | bytes 417800 | tf_op jit(solution)/shard_map/ppermute | solution.py:660

commit v6 on v5

--- a/solution.py
+++ b/solution.py
@@ -537,13 +537,18 @@
         for k in range(N // 2):
             ref[k + 1 + RING // 2] = given[k]
     ends = list(range(RING // 2)) + list(range(RING // 2 + N // 2, half))
-    for x_lo, x_hi, depth, listed, a, b in (
-            (lambda r: fx_lo[r], lambda r: fx_hi[r], RING, POT_ROWS, even, odd),
-            (lambda r: plane(xs_lo, r), lambda r: plane(xs_hi, r), RING - 1, SRC_ROWS, s_even, s_odd)):
+    def far(ref):
+        v = ref[FAR:FAR + N // 2, :]
+        return jnp.concatenate([v, roll_z(v, -1)], axis=0)
+
+    for x_lo, x_hi, depth, single, shared, a, b in (
+            (lambda r: fx_lo[r], lambda r: fx_hi[r], RING, POT_ROWS, POT_SHARED, even, odd),
+            (lambda r: plane(xs_lo, r) if r < RING - 2 else far(xs_lo), lambda r: plane(xs_hi, r) if r < RING - 2 else far(xs_hi),
+             RING - 1, SRC_ROWS, SRC_SHARED, s_even, s_odd)):
         for r in range(depth):
             ext[RING - 1 - r, mid] = x_lo(r)
             ext[top + r, mid] = x_hi(r)
-        for at, a_ring, side, b_ring in listed:
+        for at, a_ring, side, b_ring in single + [(at, p, side, q) for at, p, q in shared for side in (0, 1)]:
             y = OFF + N + b_ring - 1 if side else OFF - b_ring
             ext[RING - a_ring, y:y + 1, :] = xs_lo[at:at + 1, :]
             ext[top + a_ring - 1, y:y + 1, :] = xs_hi[at:at + 1, :]
@@ -624,34 +629,46 @@
     return rest, weight
 
 
-def ring_rows(depth, total):
-    listed = []
-    at = depth
+def ring_rows(at, total):
+    single, shared = [], []
     for a in range(1, total):
-        for side in (0, 1):
-            for b in range(1, total - a + 1):
-                listed.append((at, a, side, b))
+        for b in range(1, total - a):
+            for side in (0, 1):
+                single.append((at, a, side, b))
                 at += 1
-    return listed
-
-
-SRC_ROWS = ring_rows((RING - 1) * N, RING - 1)
-POT_ROWS = ring_rows(SRC_ROWS[-1][0] + 1, RING)
-SRC_LEN = 136
+    for a in range(1, total):
+        shared.append((at, a, total - a))
+        at += 1
+    return single, shared, at
+
+
+FAR = (RING - 2) * N
+SRC_ROWS, SRC_SHARED, POT_START = ring_rows(FAR + N // 2, RING - 1)
+POT_ROWS, POT_SHARED, SRC_END = ring_rows(POT_START, RING)
+SRC_LEN = -(-SRC_END // 8) * 8
 
 
 def pack_src_kernel(src, ys_lo, ys_hi, fy_lo, fy_hi, o_hi, o_lo):
-    for k in range(RING - 1):
-        o_hi[k * N:(k + 1) * N, :] = src[N - 1 - k]
-        o_lo[k * N:(k + 1) * N, :] = src[k]
-    for listed, lo, hi in ((SRC_ROWS, ys_lo, ys_hi), (POT_ROWS, fy_lo, fy_hi)):
-        for at, a, side, b in listed:
-            halo = hi if side else lo
-            o_hi[at:at + 1, :] = halo[b - 1, N - a:N - a + 1, :]
-            o_lo[at:at + 1, :] = halo[b - 1, a - 1:a, :]
-    end = POT_ROWS[-1][0] + 1
-    o_hi[end:, :] = jnp.zeros((SRC_LEN - end, Z), F32)
-    o_lo[end:, :] = jnp.zeros((SRC_LEN - end, Z), F32)
+    lane = lax.broadcasted_iota(jnp.int32, (1, Z), 1) % 2
+    half = (N // 2, Z)
+    shade = (lax.broadcasted_iota(jnp.int32, half, 0) + lax.broadcasted_iota(jnp.int32, half, 1)) % 2
+    for o, high in ((o_hi, True), (o_lo, False)):
+        def at_x(a, high=high):
+            return N - a if high else a - 1
+
+        for k in range(RING - 2):
+            o[k * N:(k + 1) * N, :] = src[at_x(k + 1)]
+        x = at_x(RING - 1)
+        v = src[x]
+        o[FAR:FAR + N // 2, :] = jnp.where(shade == x % 2, v[:N // 2], roll_z(v[N // 2:], 1))
+        for single, shared, lo, hi, odd in ((SRC_ROWS, SRC_SHARED, ys_lo, ys_hi, 0), (POT_ROWS, POT_SHARED, fy_lo, fy_hi, 1)):
+            for at, a, side, b in single:
+                halo = hi if side else lo
+                o[at:at + 1, :] = halo[b - 1, at_x(a):at_x(a) + 1, :]
+            for at, a, b in shared:
+                x = at_x(a)
+                o[at:at + 1, :] = jnp.where(lane == (x + b + odd) % 2, lo[b - 1, x:x + 1, :], hi[b - 1, x:x + 1, :])
+        o[SRC_END:, :] = jnp.zeros((SRC_LEN - SRC_END, Z), F32)
 
 
 def swap(axis, hi, lo):

time: 56.4 us -> 55.6 us (0.986)
  waiting for transfers between devices: 20.5 us -> 19.8 us
where the time goes in v6:
time: 55.6 us; the launch traced here: 55.5 us
  starting transfers between devices  20.2 us (36%)
  waiting for transfers between devices  19.8 us (36%)
  Pallas kernels  14.4 us (26%)
  between operations  0.87 us (2%)
    ppermute x6, starting transfers between devices, swap(): lax.ppermute(jnp.where(even, lo, hi), axis, [(i, (i - 1 + 2 * (i % 2)) %...  20.2 us
    ppermute x6, waiting for transfers between devices, swap(): lax.ppermute(jnp.where(even, lo, hi), axis, [(i, (i - 1 + 2 * (i % 2)) %...  13.2 us
    ppermute x6, waiting for transfers between devices, swap(): lax.ppermute(jnp.where(even, hi, lo), axis, [(i, i + 1 - 2 * (i % 2)) for...  6.54 us
    pallas_call x1, Pallas kernels, body(): call(collide_kernel, [sds(19, N, N, Z), sds(4, N, N, Z)] + [sds(19, N, Z)...  4.22 us
    pallas_call x1, Pallas kernels, body(): call(patch_kernel, [sds(19, N, N, Z), pair], 'patch', 'v' * 10, out_specs...  2.57 us
    pallas_call x1, Pallas kernels, body(): call(inner_kernel, [pair, sds(2, 4, N, Z), sds(2, 2, N, Z), sds(2, N, Z),...  2.34 us
    pallas_call x1, Pallas kernels, body(): call(sweep_kernel, [cube], 'sweep', 'v' * 8, scratch=[VM((N + 2 * RING, N...  2.08 us
    pallas_call x1, Pallas kernels, body(): call(faces_kernel, [sds(RING + 3, N, Z)] * 4 + [cube, sds(N - 2 * RING, N...  1.56 us
  transfers between devices with their start and end apart: 12, of which 8 were waited for; matrix products, arithmetic and copies ran while one was open for 0% of the time, Pallas kernels for 17%

profile of v6, /device:TPU:7, one launch (start us, length us, event | category | flops | bytes accessed | tf_op | source)
XLA Modules:
  0.0 55.5 jit_solution(3963791025895753798)
XLA Ops:
  0.6 1.6 %faces.1 = (f32[9,16,256]{2,1,0:T(8,128)S(1)}, f32[9,16,256]{2,1,0:T(8,128)S(1)}, f32[9,16,256]{2,1,0:T(8,128)S(1)}, f32[9,16,256]{2,1,0:T(8,128)S(1)}, f32[16,1...) custom-call(f32[16,16,256]{2,1,0:T(8,128)} %pot.3, f32[2,16,16,256]{3,2,1,0:T(8,128)} %conc.1, f32[16,16,256]{2,1,0:T(8,128)} %mob.1, ...), custom_call_target="tpu_custom_call" | custom-call | bytes 2600000 | tf_op jit(solution)/shard_map/faces/pallas_call | solution.py:685
  2.2 8.3 %collective-permute-start = (f32[9,16,256]{2,1,0:T(8,128)S(1)}, f32[9,16,256]{2,1,0:T(8,128)S(1)}, u32[]{:S(2)}, u32[]{:S(2)}) collective-permute-start(f32[9,16,256]{2,1,0:T(8,128)S(1)} %get-tuple-element.100), channel_id=1, source_target_pairs={{0,240},{16,32},{32,16},{48,64},{64,48},{80,96},{96,80},{112,128},... | collective-permute-start | bytes 442376 | tf_op jit(solution)/shard_map/ppermute | solution.py:678
  10.6 1.2 %collective-permute-start.2 = (f32[9,16,256]{2,1,0:T(8,128)S(1)}, f32[9,16,256]{2,1,0:T(8,128)S(1)}, u32[]{:S(2)}, u32[]{:S(2)}) collective-permute-start(f32[9,16,256]{2,1,0:T(8,128)S(1)} %get-tuple-element.96), channel_id=1, source_target_pairs={{0,15},{1,2},{2,1},{3,4},{4,3},{5,6},{6,5},{7,8},{8,7},{9,10},{10,... | collective-permute-start | bytes 442376 | tf_op jit(solution)/shard_map/ppermute | solution.py:678
  11.8 0.0 collective-permute-start.3
  11.8 4.2 %collide.1 = (f32[19,16,16,256]{3,2,1,0:T(8,128)S(1)}, f32[4,16,16,256]{3,2,1,0:T(8,128)S(1)}, f32[19,16,256]{2,1,0:T(8,128)S(1)}, f32[19,16,256]{2,1,0:T(8,128)...) custom-call(f32[19,16,16,256]{3,2,1,0:T(8,128)} %pops.1, f32[9,16,256]{2,1,0:T(8,128)S(1)} %get-tuple-element.48.gx_hi, ...), custom_call_target="tpu_custom_call" | custom-call | flops 20000000 | bytes 14000000 | tf_op jit(solution)/shard_map/collide/pallas_call | solution.py:694
  16.0 0.0 copy-start
  16.1 0.0 copy-start.1
  16.1 0.0 copy-start.2
  16.1 0.0 copy-start.3
  16.1 0.0 copy-start.4
  16.1 0.0 copy-start.5
  16.1 0.0 collective-permute-done
  16.1 0.7 %collective-permute-done.1 = f32[9,16,256]{2,1,0:T(8,128)S(1)} collective-permute-done((f32[9,16,256]{2,1,0:T(8,128)S(1)}, f32[9,16,256]{2,1,0:T(8,128)S(1)}, u32[]{:S(2)}, u32[]{:S(2)}) %collective-permute-start.1) | collective-permute-done | bytes 147488 | tf_op jit(solution)/shard_map/ppermute | solution.py:677
  16.9 0.8 %collective-permute-done.2 = f32[9,16,256]{2,1,0:T(8,128)S(1)} collective-permute-done((f32[9,16,256]{2,1,0:T(8,128)S(1)}, f32[9,16,256]{2,1,0:T(8,128)S(1)}, u32[]{:S(2)}, u32[]{:S(2)}) %collective-permute-start.2) | collective-permute-done | bytes 147488 | tf_op jit(solution)/shard_map/ppermute | solution.py:678
  17.7 1.0 %edge.1 = (f32[4,16,16,256]{3,2,1,0:T(8,128)S(1)}, f32[19,16,256]{2,1,0:T(8,128)S(1)}, f32[19,16,256]{2,1,0:T(8,128)S(1)}, f32[19,16,256]{2,1,0:T(8,128)S(1)}, f...) custom-call(f32[19,16,256]{2,1,0:T(8,128)S(1)} %get-tuple-element.53.px_lo, ...), custom_call_target="tpu_custom_call" | custom-call | bytes 3000000 | tf_op jit(solution)/shard_map/edge/pallas_call | solution.py:698
  18.7 1.3 %collective-permute-start.4 = (f32[120,256]{1,0:T(8,128)S(1)}, f32[120,256]{1,0:T(8,128)S(1)}, u32[]{:S(2)}, u32[]{:S(2)}) collective-permute-start(f32[120,256]{1,0:T(8,128)S(1)} %get-tuple-element.112), channel_id=1, source_target_pairs={{0,15},{1,2},{2,1},{3,4},{4,3},{5,6},{6,5},{7,8},{8,7},{9,10},{10,... | collective-permute-start | bytes 368648 | tf_op jit(solution)/shard_map/ppermute | solution.py:678
  20.0 5.2 %collective-permute-done.4 = f32[120,256]{1,0:T(8,128)S(1)} collective-permute-done((f32[120,256]{1,0:T(8,128)S(1)}, f32[120,256]{1,0:T(8,128)S(1)}, u32[]{:S(2)}, u32[]{:S(2)}) %collective-permute-start.4) | collective-permute-done | bytes 122912 | tf_op jit(solution)/shard_map/ppermute | solution.py:678
  25.3 4.5 %collective-permute-start.6 = (f32[120,256]{1,0:T(8,128)S(1)}, f32[120,256]{1,0:T(8,128)S(1)}, u32[]{:S(2)}, u32[]{:S(2)}) collective-permute-start(f32[120,256]{1,0:T(8,128)S(1)} %get-tuple-element.108), channel_id=1, source_target_pairs={{0,240},{16,32},{32,16},{48,64},{64,48},{80,96},{96,80},{112,128},... | collective-permute-start | bytes 368648 | tf_op jit(solution)/shard_map/ppermute | solution.py:678
  29.8 2.3 %inner.1 = (f32[2,16,16,256]{3,2,1,0:T(8,128)S(1)}, f32[2,4,16,256]{3,2,1,0:T(8,128)S(1)}, f32[2,2,16,256]{3,2,1,0:T(8,128)S(1)}, f32[2,16,256]{2,1,0:T(8,128)S(...) custom-call(f32[4]{0:T(128)S(1)} %copy-done.5, ...), custom_call_target="tpu_custom_call" | custom-call | flops 10000000 | bytes 6000000 | tf_op jit(solution)/shard_map/inner/pallas_call | solution.py:707
  32.1 1.2 %collective-permute-done.6 = f32[120,256]{1,0:T(8,128)S(1)} collective-permute-done((f32[120,256]{1,0:T(8,128)S(1)}, f32[120,256]{1,0:T(8,128)S(1)}, u32[]{:S(2)}, u32[]{:S(2)}) %collective-permute-start.6) | collective-permute-done | bytes 122912 | tf_op jit(solution)/shard_map/ppermute | solution.py:678
  33.3 3.1 %collective-permute-done.7 = f32[120,256]{1,0:T(8,128)S(1)} collective-permute-done((f32[120,256]{1,0:T(8,128)S(1)}, f32[120,256]{1,0:T(8,128)S(1)}, u32[]{:S(2)}, u32[]{:S(2)}) %collective-permute-start.7) | collective-permute-done | bytes 122912 | tf_op jit(solution)/shard_map/ppermute | solution.py:677
  36.4 0.3 transport.1
  36.7 1.8 %collective-permute-start.8 = (f32[5,16,256]{2,1,0:T(8,128)S(1)}, f32[5,16,256]{2,1,0:T(8,128)S(1)}, u32[]{:S(2)}, u32[]{:S(2)}) collective-permute-start(f32[5,16,256]{2,1,0:T(8,128)S(1)} %get-tuple-element.116), channel_id=1, source_target_pairs={{0,15},{1,2},{2,1},{3,4},{4,3},{5,6},{6,5},{7,8},{8,7},{9,10},{10,... | collective-permute-start | bytes 245768 | tf_op jit(solution)/shard_map/ppermute | solution.py:678
  38.5 0.0 collective-permute-start.9
  38.5 4.2 %collective-permute-done.8 = f32[5,16,256]{2,1,0:T(8,128)S(1)} collective-permute-done((f32[5,16,256]{2,1,0:T(8,128)S(1)}, f32[5,16,256]{2,1,0:T(8,128)S(1)}, u32[]{:S(2)}, u32[]{:S(2)}) %collective-permute-start.8) | collective-permute-done | bytes 81952 | tf_op jit(solution)/shard_map/ppermute | solution.py:678
  42.8 0.1 pack_src.1
  42.9 3.0 %collective-permute-start.10 = (f32[120,256]{1,0:T(8,128)S(1)}, f32[120,256]{1,0:T(8,128)S(1)}, u32[]{:S(2)}, u32[]{:S(2)}) collective-permute-start(f32[120,256]{1,0:T(8,128)S(1)} %get-tuple-element.104), channel_id=1, source_target_pairs={{0,240},{16,32},{32,16},{48,64},{64,48},{80,96},{96,80},{112,128},... | collective-permute-start | bytes 368648 | tf_op jit(solution)/shard_map/ppermute | solution.py:678
  45.9 2.6 %patch.1 = (f32[19,16,16,256]{3,2,1,0:T(8,128)}, f32[2,16,16,256]{3,2,1,0:T(8,128)}) custom-call(f32[19,16,16,256]{3,2,1,0:T(8,128)S(1)} %get-tuple-element.52.buf, f32[19,16,256]{2,1,0:T(8,128)S(1)} %get-tuple-element.60.ex_lo, f32[19,16,256]{2,1,0:T(8,128)S(1)} %get-tuple-element.61.ex_hi, f32[19,16,256]{2,1,0:T(8,128)S(1)} %get-tuple-element.62.ey_lo, ...), custom_call_target="tpu_custom_call" | custom-call | bytes 10000000 | tf_op jit(solution)/shard_map/patch/pallas_call | solution.py:728
  48.5 0.3 prepare.1
  48.8 1.9 %collective-permute-done.10 = f32[120,256]{1,0:T(8,128)S(1)} collective-permute-done((f32[120,256]{1,0:T(8,128)S(1)}, f32[120,256]{1,0:T(8,128)S(1)}, u32[]{:S(2)}, u32[]{:S(2)}) %collective-permute-start.10) | collective-permute-done | bytes 122912 | tf_op jit(solution)/shard_map/ppermute | solution.py:678
  50.7 2.7 %collective-permute-done.11 = f32[120,256]{1,0:T(8,128)S(1)} collective-permute-done((f32[120,256]{1,0:T(8,128)S(1)}, f32[120,256]{1,0:T(8,128)S(1)}, u32[]{:S(2)}, u32[]{:S(2)}) %collective-permute-start.11) | collective-permute-done | bytes 122912 | tf_op jit(solution)/shard_map/ppermute | solution.py:677
  53.4 2.1 %sweep.1 = f32[16,16,256]{2,1,0:T(8,128)} custom-call(f32[8,32,256]{2,1,0:T(8,128)S(1)} %get-tuple-element.87.even_in, f32[8,32,256]{2,1,0:T(8,128)S(1)} %get-tuple-element.88.odd_in, f32[8,32,256]{2,1,0:T(8,128)S(1)} %get-tuple-element.89.s_even_in, f32[8,32,256]{2,1,0:T(8,128)S(1)} %get-tuple-element.90.s_odd_in, ...), custom_call_target="tpu_custom_call" | custom-call | flops 20000000 | bytes 4000000 | tf_op jit(solution)/shard_map/sweep/pallas_call | solution.py:724
  (26 shorter events, 0.3 us)
Async XLA Ops:
  2.2 13.9 %collective-permute-start = (f32[9,16,256]{2,1,0:T(8,128)S(1)}, f32[9,16,256]{2,1,0:T(8,128)S(1)}, u32[]{:S(2)}, u32[]{:S(2)}) collective-permute-start(f32[9,16,256]{2,1,0:T(8,128)S(1)} %get-tuple-element.100), channel_id=1, source_target_pairs={{0,240},{16,32},{32,16},{48,64},{64,48},{80,96},{96,80},{112,128},... | collective-permute-start | bytes 442376 | tf_op jit(solution)/shard_map/ppermute | solution.py:678
  10.5 6.3 %collective-permute-start.1 = (f32[9,16,256]{2,1,0:T(8,128)S(1)}, f32[9,16,256]{2,1,0:T(8,128)S(1)}, u32[]{:S(2)}, u32[]{:S(2)}) collective-permute-start(f32[9,16,256]{2,1,0:T(8,128)S(1)} %get-tuple-element.99), channel_id=1, source_target_pairs={{0,16},{16,0},{32,48},{48,32},{64,80},{80,64},{96,112},{112,96},{1... | collective-permute-start | bytes 442376 | tf_op jit(solution)/shard_map/ppermute | solution.py:677
  10.6 7.1 %collective-permute-start.2 = (f32[9,16,256]{2,1,0:T(8,128)S(1)}, f32[9,16,256]{2,1,0:T(8,128)S(1)}, u32[]{:S(2)}, u32[]{:S(2)}) collective-permute-start(f32[9,16,256]{2,1,0:T(8,128)S(1)} %get-tuple-element.96), channel_id=1, source_target_pairs={{0,15},{1,2},{2,1},{3,4},{4,3},{5,6},{6,5},{7,8},{8,7},{9,10},{10,... | collective-permute-start | bytes 442376 | tf_op jit(solution)/shard_map/ppermute | solution.py:678
  11.8 5.8 %collective-permute-start.3 = (f32[9,16,256]{2,1,0:T(8,128)S(1)}, f32[9,16,256]{2,1,0:T(8,128)S(1)}, u32[]{:S(2)}, u32[]{:S(2)}) collective-permute-start(f32[9,16,256]{2,1,0:T(8,128)S(1)} %get-tuple-element.95), channel_id=1, source_target_pairs={{0,1},{1,0},{2,3},{3,2},{4,5},{5,4},{6,7},{7,6},{8,9},{9,8},{10,11... | collective-permute-start | bytes 442376 | tf_op jit(solution)/shard_map/ppermute | solution.py:677
  16.0 13.7 %copy-start = (f32[16,16,256]{2,1,0:T(8,128)S(1)}, f32[16,16,256]{2,1,0:T(8,128)}, u32[]{:S(2)}) copy-start(f32[16,16,256]{2,1,0:T(8,128)} %pot.3) | copy-start | bytes 786436
  16.1 13.7 %copy-start.1 = (f32[2,16,16,256]{3,2,1,0:T(8,128)S(1)}, f32[2,16,16,256]{3,2,1,0:T(8,128)}, u32[]{:S(2)}) copy-start(f32[2,16,16,256]{3,2,1,0:T(8,128)} %conc.1) | copy-start | bytes 1572868
  16.1 13.7 %copy-start.2 = (f32[16,16,256]{2,1,0:T(8,128)S(1)}, f32[16,16,256]{2,1,0:T(8,128)}, u32[]{:S(2)}) copy-start(f32[16,16,256]{2,1,0:T(8,128)} %mob.1) | copy-start | bytes 786436
  16.1 13.7 %copy-start.3 = (s32[16,16,256]{2,1,0:T(8,128)S(1)}, s32[16,16,256]{2,1,0:T(8,128)}, u32[]{:S(2)}) copy-start(s32[16,16,256]{2,1,0:T(8,128)} %solid.1) | copy-start | bytes 786436
  16.1 13.7 %copy-start.4 = (s32[16,16,256]{2,1,0:T(8,128)S(1)}, s32[16,16,256]{2,1,0:T(8,128)}, u32[]{:S(2)}) copy-start(s32[16,16,256]{2,1,0:T(8,128)} %classes_h.1) | copy-start | bytes 786436
  16.1 13.7 %copy-start.5 = (f32[4]{0:T(128)S(1)}, f32[4]{0:T(128)}, u32[]{:S(2)}) copy-start(f32[4]{0:T(128)} %charge.1) | copy-start | bytes 52
  18.7 6.5 %collective-permute-start.4 = (f32[120,256]{1,0:T(8,128)S(1)}, f32[120,256]{1,0:T(8,128)S(1)}, u32[]{:S(2)}, u32[]{:S(2)}) collective-permute-start(f32[120,256]{1,0:T(8,128)S(1)} %get-tuple-element.112), channel_id=1, source_target_pairs={{0,15},{1,2},{2,1},{3,4},{4,3},{5,6},{6,5},{7,8},{8,7},{9,10},{10,... | collective-permute-start | bytes 368648 | tf_op jit(solution)/shard_map/ppermute | solution.py:678
  20.0 5.2 %collective-permute-start.5 = (f32[120,256]{1,0:T(8,128)S(1)}, f32[120,256]{1,0:T(8,128)S(1)}, u32[]{:S(2)}, u32[]{:S(2)}) collective-permute-start(f32[120,256]{1,0:T(8,128)S(1)} %get-tuple-element.111), channel_id=1, source_target_pairs={{0,1},{1,0},{2,3},{3,2},{4,5},{5,4},{6,7},{7,6},{8,9},{9,8},{10,11... | collective-permute-start | bytes 368648 | tf_op jit(solution)/shard_map/ppermute | solution.py:677
  25.3 8.0 %collective-permute-start.6 = (f32[120,256]{1,0:T(8,128)S(1)}, f32[120,256]{1,0:T(8,128)S(1)}, u32[]{:S(2)}, u32[]{:S(2)}) collective-permute-start(f32[120,256]{1,0:T(8,128)S(1)} %get-tuple-element.108), channel_id=1, source_target_pairs={{0,240},{16,32},{32,16},{48,64},{64,48},{80,96},{96,80},{112,128},... | collective-permute-start | bytes 368648 | tf_op jit(solution)/shard_map/ppermute | solution.py:678
  29.7 6.7 %collective-permute-start.7 = (f32[120,256]{1,0:T(8,128)S(1)}, f32[120,256]{1,0:T(8,128)S(1)}, u32[]{:S(2)}, u32[]{:S(2)}) collective-permute-start(f32[120,256]{1,0:T(8,128)S(1)} %get-tuple-element.107), channel_id=1, source_target_pairs={{0,16},{16,0},{32,48},{48,32},{64,80},{80,64},{96,112},{112,96},{1... | collective-permute-start | bytes 368648 | tf_op jit(solution)/shard_map/ppermute | solution.py:677
  36.7 6.1 %collective-permute-start.8 = (f32[5,16,256]{2,1,0:T(8,128)S(1)}, f32[5,16,256]{2,1,0:T(8,128)S(1)}, u32[]{:S(2)}, u32[]{:S(2)}) collective-permute-start(f32[5,16,256]{2,1,0:T(8,128)S(1)} %get-tuple-element.116), channel_id=1, source_target_pairs={{0,15},{1,2},{2,1},{3,4},{4,3},{5,6},{6,5},{7,8},{8,7},{9,10},{10,... | collective-permute-start | bytes 245768 | tf_op jit(solution)/shard_map/ppermute | solution.py:678
  38.5 4.2 %collective-permute-start.9 = (f32[5,16,256]{2,1,0:T(8,128)S(1)}, f32[5,16,256]{2,1,0:T(8,128)S(1)}, u32[]{:S(2)}, u32[]{:S(2)}) collective-permute-start(f32[5,16,256]{2,1,0:T(8,128)S(1)} %get-tuple-element.115), channel_id=1, source_target_pairs={{0,1},{1,0},{2,3},{3,2},{4,5},{5,4},{6,7},{7,6},{8,9},{9,8},{10,11... | collective-permute-start | bytes 245768 | tf_op jit(solution)/shard_map/ppermute | solution.py:677
  42.9 7.8 %collective-permute-start.10 = (f32[120,256]{1,0:T(8,128)S(1)}, f32[120,256]{1,0:T(8,128)S(1)}, u32[]{:S(2)}, u32[]{:S(2)}) collective-permute-start(f32[120,256]{1,0:T(8,128)S(1)} %get-tuple-element.104), channel_id=1, source_target_pairs={{0,240},{16,32},{32,16},{48,64},{64,48},{80,96},{96,80},{112,128},... | collective-permute-start | bytes 368648 | tf_op jit(solution)/shard_map/ppermute | solution.py:678
  45.9 7.5 %collective-permute-start.11 = (f32[120,256]{1,0:T(8,128)S(1)}, f32[120,256]{1,0:T(8,128)S(1)}, u32[]{:S(2)}, u32[]{:S(2)}) collective-permute-start(f32[120,256]{1,0:T(8,128)S(1)} %get-tuple-element.103), channel_id=1, source_target_pairs={{0,16},{16,0},{32,48},{48,32},{64,80},{80,64},{96,112},{112,96},{1... | collective-permute-start | bytes 368648 | tf_op jit(solution)/shard_map/ppermute | solution.py:677

commit v7 on v6

--- a/solution.py
+++ b/solution.py
@@ -80,36 +80,40 @@
     )
 
 
-def faces_kernel(pot_h, conc_h, mob_h, solid_h, gx_hi, gx_lo, gy_hi, gy_lo, pull, middle, pot, cond, conc, mob, solid, sems):
+def faces_kernel(pot_h, conc_h, mob_h, solid_h, gx_hi, gx_lo, gy_hi, gy_lo, pull, middle, pot, conc, mob, solid, sems):
     pairs = ((pot_h, pot), (conc_h, conc), (mob_h, mob), (solid_h, solid))
     copies = [pltpu.make_async_copy(a, b, sems.at[q]) for q, (a, b) in enumerate(pairs)]
     for c in copies:
         c.start()
-    for c in copies:
-        c.wait()
-
-    def step(x, carry):
-        here = pl.ds(x, 1)
-        is_fluid = solid[x] == 0
-        cond[x] = jnp.where(is_fluid, jnp.sqrt(mob[x]), 0.0)
-        pull[x] = jnp.where(is_fluid, (conc[0, x] - conc[1, x]) * (-0.001), SOLID)
+    copies[0].wait()
+    for x in range(N):
         for r in range(RING):
-            gy_hi[r, here, :] = pot[x, N - 1 - r:N - r, :]
-            gy_lo[r, here, :] = pot[x, r:r + 1, :]
-        for q, v in ((0, conc.at[0]), (1, conc.at[1]), (2, cond)):
-            gy_hi[RING + q, here, :] = v[x, N - 1:N, :]
-            gy_lo[RING + q, here, :] = v[x, 0:1, :]
-        return carry
-
-    lax.fori_loop(0, N, step, 0, unroll=True)
+            gy_hi[r, x:x + 1, :] = pot[x, N - 1 - r:N - r, :]
+            gy_lo[r, x:x + 1, :] = pot[x, r:r + 1, :]
+    for r in range(RING):
+        gx_hi[r] = pot[N - 1 - r]
+        gx_lo[r] = pot[r]
     for x in range(RING, N - RING):
         middle[x - RING] = pot[x]
-    for x, face in ((N - 1, gx_hi), (0, gx_lo)):
-        for r in range(RING):
-            face[r] = pot[abs(x - r)]
-        face[RING] = conc[0, x]
-        face[RING + 1] = conc[1, x]
-        face[RING + 2] = cond[x]
+    copies[1].wait()
+    for s in range(2):
+        for x in range(N):
+            gy_hi[RING + s, x:x + 1, :] = conc[s, x, N - 1:N, :]
+            gy_lo[RING + s, x:x + 1, :] = conc[s, x, 0:1, :]
+        gx_hi[RING + s] = conc[s, N - 1]
+        gx_lo[RING + s] = conc[s, 0]
+    copies[2].wait()
+    copies[3].wait()
+    for x in range(N):
+        is_fluid = solid[x] == 0
+        v = jnp.where(is_fluid, jnp.sqrt(mob[x]), 0.0)
+        pull[x] = jnp.where(is_fluid, (conc[0, x] - conc[1, x]) * (-0.001), SOLID)
+        gy_hi[RING + 2, x:x + 1, :] = row_of(v, N - 1)
+        gy_lo[RING + 2, x:x + 1, :] = row_of(v, 0)
+        if x == 0:
+            gx_lo[RING + 2] = v
+        if x == N - 1:
+            gx_hi[RING + 2] = v
 
 
 def post_of(p, fluid, q, slopes):
@@ -684,7 +688,7 @@
     msg = sds(ROWS, Z)
     gx_hi, gx_lo, gy_hi, gy_lo, pull, middle = call(
         faces_kernel, [sds(RING + 3, N, Z)] * 4 + [cube, sds(N - 2 * RING, N, Z)], "faces", "hhhh",
-        scratch=[VM((N, N, Z), F32), VM((N, N, Z), F32), VM((2, N, N, Z), F32), VM((N, N, Z), F32),
+        scratch=[VM((N, N, Z), F32), VM((2, N, N, Z), F32), VM((N, N, Z), F32),
                  VM((N, N, Z), jnp.int32),
                  pltpu.SemaphoreType.DMA((4,))], mib=53, moved=2600000)(
         pot, conc, mob, solid)

time: 55.6 us -> 55.5 us (level)
  no operation moved by 1% of the time
where the time goes in v7:
time: 55.5 us; the launch traced here: 55.4 us
  starting transfers between devices  20.2 us (36%)
  waiting for transfers between devices  19.8 us (36%)
  Pallas kernels  14.3 us (26%)
  between operations  0.87 us (2%)
    ppermute x6, starting transfers between devices, swap(): lax.ppermute(jnp.where(even, lo, hi), axis, [(i, (i - 1 + 2 * (i % 2)) %...  20.2 us
    ppermute x6, waiting for transfers between devices, swap(): lax.ppermute(jnp.where(even, lo, hi), axis, [(i, (i - 1 + 2 * (i % 2)) %...  13.2 us
    ppermute x6, waiting for transfers between devices, swap(): lax.ppermute(jnp.where(even, hi, lo), axis, [(i, i + 1 - 2 * (i % 2)) for...  6.54 us
    pallas_call x1, Pallas kernels, body(): call(collide_kernel, [sds(19, N, N, Z), sds(4, N, N, Z)] + [sds(19, N, Z)...  4.22 us
    pallas_call x1, Pallas kernels, body(): call(patch_kernel, [sds(19, N, N, Z), pair], 'patch', 'v' * 10, out_specs...  2.57 us
    pallas_call x1, Pallas kernels, body(): call(inner_kernel, [pair, sds(2, 4, N, Z), sds(2, 2, N, Z), sds(2, N, Z),...  2.34 us
    pallas_call x1, Pallas kernels, body(): call(sweep_kernel, [cube], 'sweep', 'v' * 8, scratch=[VM((N + 2 * RING, N...  2.08 us
    pallas_call x1, Pallas kernels, body(): call(faces_kernel, [sds(RING + 3, N, Z)] * 4 + [cube, sds(N - 2 * RING, N...  1.43 us
  transfers between devices with their start and end apart: 12, of which 8 were waited for; matrix products, arithmetic and copies ran while one was open for 0% of the time, Pallas kernels for 17%

profile of v7, /device:TPU:7, one launch (start us, length us, event | category | flops | bytes accessed | tf_op | source)
XLA Modules:
  0.0 55.4 jit_solution(4217646162421817750)
XLA Ops:
  0.6 1.4 %faces.1 = (f32[9,16,256]{2,1,0:T(8,128)S(1)}, f32[9,16,256]{2,1,0:T(8,128)S(1)}, f32[9,16,256]{2,1,0:T(8,128)S(1)}, f32[9,16,256]{2,1,0:T(8,128)S(1)}, f32[16,1...) custom-call(f32[16,16,256]{2,1,0:T(8,128)} %pot.3, f32[2,16,16,256]{3,2,1,0:T(8,128)} %conc.1, f32[16,16,256]{2,1,0:T(8,128)} %mob.1, ...), custom_call_target="tpu_custom_call" | custom-call | bytes 2600000 | tf_op jit(solution)/shard_map/faces/pallas_call | solution.py:689
  2.1 8.3 %collective-permute-start = (f32[9,16,256]{2,1,0:T(8,128)S(1)}, f32[9,16,256]{2,1,0:T(8,128)S(1)}, u32[]{:S(2)}, u32[]{:S(2)}) collective-permute-start(f32[9,16,256]{2,1,0:T(8,128)S(1)} %get-tuple-element.100), channel_id=1, source_target_pairs={{0,240},{16,32},{32,16},{48,64},{64,48},{80,96},{96,80},{112,128},... | collective-permute-start | bytes 442376 | tf_op jit(solution)/shard_map/ppermute | solution.py:682
  10.4 0.0 collective-permute-start.1
  10.4 1.2 %collective-permute-start.2 = (f32[9,16,256]{2,1,0:T(8,128)S(1)}, f32[9,16,256]{2,1,0:T(8,128)S(1)}, u32[]{:S(2)}, u32[]{:S(2)}) collective-permute-start(f32[9,16,256]{2,1,0:T(8,128)S(1)} %get-tuple-element.96), channel_id=1, source_target_pairs={{0,15},{1,2},{2,1},{3,4},{4,3},{5,6},{6,5},{7,8},{8,7},{9,10},{10,... | collective-permute-start | bytes 442376 | tf_op jit(solution)/shard_map/ppermute | solution.py:682
  11.7 4.2 %collide.1 = (f32[19,16,16,256]{3,2,1,0:T(8,128)S(1)}, f32[4,16,16,256]{3,2,1,0:T(8,128)S(1)}, f32[19,16,256]{2,1,0:T(8,128)S(1)}, f32[19,16,256]{2,1,0:T(8,128)...) custom-call(f32[19,16,16,256]{3,2,1,0:T(8,128)} %pops.1, f32[9,16,256]{2,1,0:T(8,128)S(1)} %get-tuple-element.48.gx_hi, ...), custom_call_target="tpu_custom_call" | custom-call | flops 20000000 | bytes 14000000 | tf_op jit(solution)/shard_map/collide/pallas_call | solution.py:698
  15.9 0.0 copy-start
  15.9 0.0 copy-start.1
  15.9 0.0 copy-start.2
  15.9 0.0 copy-start.3
  16.0 0.0 copy-start.4
  16.0 0.0 copy-start.5
  16.0 0.7 %collective-permute-done.1 = f32[9,16,256]{2,1,0:T(8,128)S(1)} collective-permute-done((f32[9,16,256]{2,1,0:T(8,128)S(1)}, f32[9,16,256]{2,1,0:T(8,128)S(1)}, u32[]{:S(2)}, u32[]{:S(2)}) %collective-permute-start.1) | collective-permute-done | bytes 147488 | tf_op jit(solution)/shard_map/ppermute | solution.py:681
  16.7 0.8 %collective-permute-done.2 = f32[9,16,256]{2,1,0:T(8,128)S(1)} collective-permute-done((f32[9,16,256]{2,1,0:T(8,128)S(1)}, f32[9,16,256]{2,1,0:T(8,128)S(1)}, u32[]{:S(2)}, u32[]{:S(2)}) %collective-permute-start.2) | collective-permute-done | bytes 147488 | tf_op jit(solution)/shard_map/ppermute | solution.py:682
  17.5 1.0 %edge.1 = (f32[4,16,16,256]{3,2,1,0:T(8,128)S(1)}, f32[19,16,256]{2,1,0:T(8,128)S(1)}, f32[19,16,256]{2,1,0:T(8,128)S(1)}, f32[19,16,256]{2,1,0:T(8,128)S(1)}, f...) custom-call(f32[19,16,256]{2,1,0:T(8,128)S(1)} %get-tuple-element.53.px_lo, ...), custom_call_target="tpu_custom_call" | custom-call | bytes 3000000 | tf_op jit(solution)/shard_map/edge/pallas_call | solution.py:702
  18.5 1.3 %collective-permute-start.4 = (f32[120,256]{1,0:T(8,128)S(1)}, f32[120,256]{1,0:T(8,128)S(1)}, u32[]{:S(2)}, u32[]{:S(2)}) collective-permute-start(f32[120,256]{1,0:T(8,128)S(1)} %get-tuple-element.112), channel_id=1, source_target_pairs={{0,15},{1,2},{2,1},{3,4},{4,3},{5,6},{6,5},{7,8},{8,7},{9,10},{10,... | collective-permute-start | bytes 368648 | tf_op jit(solution)/shard_map/ppermute | solution.py:682
  19.9 0.0 collective-permute-start.5
  19.9 5.2 %collective-permute-done.4 = f32[120,256]{1,0:T(8,128)S(1)} collective-permute-done((f32[120,256]{1,0:T(8,128)S(1)}, f32[120,256]{1,0:T(8,128)S(1)}, u32[]{:S(2)}, u32[]{:S(2)}) %collective-permute-start.4) | collective-permute-done | bytes 122912 | tf_op jit(solution)/shard_map/ppermute | solution.py:682
  25.1 4.5 %collective-permute-start.6 = (f32[120,256]{1,0:T(8,128)S(1)}, f32[120,256]{1,0:T(8,128)S(1)}, u32[]{:S(2)}, u32[]{:S(2)}) collective-permute-start(f32[120,256]{1,0:T(8,128)S(1)} %get-tuple-element.108), channel_id=1, source_target_pairs={{0,240},{16,32},{32,16},{48,64},{64,48},{80,96},{96,80},{112,128},... | collective-permute-start | bytes 368648 | tf_op jit(solution)/shard_map/ppermute | solution.py:682
  29.6 2.3 %inner.1 = (f32[2,16,16,256]{3,2,1,0:T(8,128)S(1)}, f32[2,4,16,256]{3,2,1,0:T(8,128)S(1)}, f32[2,2,16,256]{3,2,1,0:T(8,128)S(1)}, f32[2,16,256]{2,1,0:T(8,128)S(...) custom-call(f32[4]{0:T(128)S(1)} %copy-done.5, ...), custom_call_target="tpu_custom_call" | custom-call | flops 10000000 | bytes 6000000 | tf_op jit(solution)/shard_map/inner/pallas_call | solution.py:711
  32.0 1.2 %collective-permute-done.6 = f32[120,256]{1,0:T(8,128)S(1)} collective-permute-done((f32[120,256]{1,0:T(8,128)S(1)}, f32[120,256]{1,0:T(8,128)S(1)}, u32[]{:S(2)}, u32[]{:S(2)}) %collective-permute-start.6) | collective-permute-done | bytes 122912 | tf_op jit(solution)/shard_map/ppermute | solution.py:682
  33.2 3.1 %collective-permute-done.7 = f32[120,256]{1,0:T(8,128)S(1)} collective-permute-done((f32[120,256]{1,0:T(8,128)S(1)}, f32[120,256]{1,0:T(8,128)S(1)}, u32[]{:S(2)}, u32[]{:S(2)}) %collective-permute-start.7) | collective-permute-done | bytes 122912 | tf_op jit(solution)/shard_map/ppermute | solution.py:681
  36.3 0.3 transport.1
  36.6 1.8 %collective-permute-start.8 = (f32[5,16,256]{2,1,0:T(8,128)S(1)}, f32[5,16,256]{2,1,0:T(8,128)S(1)}, u32[]{:S(2)}, u32[]{:S(2)}) collective-permute-start(f32[5,16,256]{2,1,0:T(8,128)S(1)} %get-tuple-element.116), channel_id=1, source_target_pairs={{0,15},{1,2},{2,1},{3,4},{4,3},{5,6},{6,5},{7,8},{8,7},{9,10},{10,... | collective-permute-start | bytes 245768 | tf_op jit(solution)/shard_map/ppermute | solution.py:682
  38.4 0.0 collective-permute-start.9
  38.4 4.2 %collective-permute-done.8 = f32[5,16,256]{2,1,0:T(8,128)S(1)} collective-permute-done((f32[5,16,256]{2,1,0:T(8,128)S(1)}, f32[5,16,256]{2,1,0:T(8,128)S(1)}, u32[]{:S(2)}, u32[]{:S(2)}) %collective-permute-start.8) | collective-permute-done | bytes 81952 | tf_op jit(solution)/shard_map/ppermute | solution.py:682
  42.7 0.1 pack_src.1
  42.8 3.0 %collective-permute-start.10 = (f32[120,256]{1,0:T(8,128)S(1)}, f32[120,256]{1,0:T(8,128)S(1)}, u32[]{:S(2)}, u32[]{:S(2)}) collective-permute-start(f32[120,256]{1,0:T(8,128)S(1)} %get-tuple-element.104), channel_id=1, source_target_pairs={{0,240},{16,32},{32,16},{48,64},{64,48},{80,96},{96,80},{112,128},... | collective-permute-start | bytes 368648 | tf_op jit(solution)/shard_map/ppermute | solution.py:682
  45.8 2.6 %patch.1 = (f32[19,16,16,256]{3,2,1,0:T(8,128)}, f32[2,16,16,256]{3,2,1,0:T(8,128)}) custom-call(f32[19,16,16,256]{3,2,1,0:T(8,128)S(1)} %get-tuple-element.52.buf, f32[19,16,256]{2,1,0:T(8,128)S(1)} %get-tuple-element.60.ex_lo, f32[19,16,256]{2,1,0:T(8,128)S(1)} %get-tuple-element.61.ex_hi, f32[19,16,256]{2,1,0:T(8,128)S(1)} %get-tuple-element.62.ey_lo, ...), custom_call_target="tpu_custom_call" | custom-call | bytes 10000000 | tf_op jit(solution)/shard_map/patch/pallas_call | solution.py:732
  48.4 0.3 prepare.1
  48.6 1.9 %collective-permute-done.10 = f32[120,256]{1,0:T(8,128)S(1)} collective-permute-done((f32[120,256]{1,0:T(8,128)S(1)}, f32[120,256]{1,0:T(8,128)S(1)}, u32[]{:S(2)}, u32[]{:S(2)}) %collective-permute-start.10) | collective-permute-done | bytes 122912 | tf_op jit(solution)/shard_map/ppermute | solution.py:682
  50.6 2.7 %collective-permute-done.11 = f32[120,256]{1,0:T(8,128)S(1)} collective-permute-done((f32[120,256]{1,0:T(8,128)S(1)}, f32[120,256]{1,0:T(8,128)S(1)}, u32[]{:S(2)}, u32[]{:S(2)}) %collective-permute-start.11) | collective-permute-done | bytes 122912 | tf_op jit(solution)/shard_map/ppermute | solution.py:681
  53.3 2.1 %sweep.1 = f32[16,16,256]{2,1,0:T(8,128)} custom-call(f32[8,32,256]{2,1,0:T(8,128)S(1)} %get-tuple-element.87.even_in, f32[8,32,256]{2,1,0:T(8,128)S(1)} %get-tuple-element.88.odd_in, f32[8,32,256]{2,1,0:T(8,128)S(1)} %get-tuple-element.89.s_even_in, f32[8,32,256]{2,1,0:T(8,128)S(1)} %get-tuple-element.90.s_odd_in, ...), custom_call_target="tpu_custom_call" | custom-call | flops 20000000 | bytes 4000000 | tf_op jit(solution)/shard_map/sweep/pallas_call | solution.py:728
  (26 shorter events, 0.3 us)
Async XLA Ops:
  2.1 13.9 %collective-permute-start = (f32[9,16,256]{2,1,0:T(8,128)S(1)}, f32[9,16,256]{2,1,0:T(8,128)S(1)}, u32[]{:S(2)}, u32[]{:S(2)}) collective-permute-start(f32[9,16,256]{2,1,0:T(8,128)S(1)} %get-tuple-element.100), channel_id=1, source_target_pairs={{0,240},{16,32},{32,16},{48,64},{64,48},{80,96},{96,80},{112,128},... | collective-permute-start | bytes 442376 | tf_op jit(solution)/shard_map/ppermute | solution.py:682
  10.4 6.3 %collective-permute-start.1 = (f32[9,16,256]{2,1,0:T(8,128)S(1)}, f32[9,16,256]{2,1,0:T(8,128)S(1)}, u32[]{:S(2)}, u32[]{:S(2)}) collective-permute-start(f32[9,16,256]{2,1,0:T(8,128)S(1)} %get-tuple-element.99), channel_id=1, source_target_pairs={{0,16},{16,0},{32,48},{48,32},{64,80},{80,64},{96,112},{112,96},{1... | collective-permute-start | bytes 442376 | tf_op jit(solution)/shard_map/ppermute | solution.py:681
  10.4 7.1 %collective-permute-start.2 = (f32[9,16,256]{2,1,0:T(8,128)S(1)}, f32[9,16,256]{2,1,0:T(8,128)S(1)}, u32[]{:S(2)}, u32[]{:S(2)}) collective-permute-start(f32[9,16,256]{2,1,0:T(8,128)S(1)} %get-tuple-element.96), channel_id=1, source_target_pairs={{0,15},{1,2},{2,1},{3,4},{4,3},{5,6},{6,5},{7,8},{8,7},{9,10},{10,... | collective-permute-start | bytes 442376 | tf_op jit(solution)/shard_map/ppermute | solution.py:682
  11.7 5.8 %collective-permute-start.3 = (f32[9,16,256]{2,1,0:T(8,128)S(1)}, f32[9,16,256]{2,1,0:T(8,128)S(1)}, u32[]{:S(2)}, u32[]{:S(2)}) collective-permute-start(f32[9,16,256]{2,1,0:T(8,128)S(1)} %get-tuple-element.95), channel_id=1, source_target_pairs={{0,1},{1,0},{2,3},{3,2},{4,5},{5,4},{6,7},{7,6},{8,9},{9,8},{10,11... | collective-permute-start | bytes 442376 | tf_op jit(solution)/shard_map/ppermute | solution.py:681
  15.9 13.7 %copy-start = (f32[16,16,256]{2,1,0:T(8,128)S(1)}, f32[16,16,256]{2,1,0:T(8,128)}, u32[]{:S(2)}) copy-start(f32[16,16,256]{2,1,0:T(8,128)} %pot.3) | copy-start | bytes 786436
  15.9 13.7 %copy-start.1 = (f32[2,16,16,256]{3,2,1,0:T(8,128)S(1)}, f32[2,16,16,256]{3,2,1,0:T(8,128)}, u32[]{:S(2)}) copy-start(f32[2,16,16,256]{3,2,1,0:T(8,128)} %conc.1) | copy-start | bytes 1572868
  15.9 13.7 %copy-start.2 = (f32[16,16,256]{2,1,0:T(8,128)S(1)}, f32[16,16,256]{2,1,0:T(8,128)}, u32[]{:S(2)}) copy-start(f32[16,16,256]{2,1,0:T(8,128)} %mob.1) | copy-start | bytes 786436
  15.9 13.7 %copy-start.3 = (s32[16,16,256]{2,1,0:T(8,128)S(1)}, s32[16,16,256]{2,1,0:T(8,128)}, u32[]{:S(2)}) copy-start(s32[16,16,256]{2,1,0:T(8,128)} %solid.1) | copy-start | bytes 786436
  16.0 13.7 %copy-start.4 = (s32[16,16,256]{2,1,0:T(8,128)S(1)}, s32[16,16,256]{2,1,0:T(8,128)}, u32[]{:S(2)}) copy-start(s32[16,16,256]{2,1,0:T(8,128)} %classes_h.1) | copy-start | bytes 786436
  16.0 13.7 %copy-start.5 = (f32[4]{0:T(128)S(1)}, f32[4]{0:T(128)}, u32[]{:S(2)}) copy-start(f32[4]{0:T(128)} %charge.1) | copy-start | bytes 52
  18.5 6.5 %collective-permute-start.4 = (f32[120,256]{1,0:T(8,128)S(1)}, f32[120,256]{1,0:T(8,128)S(1)}, u32[]{:S(2)}, u32[]{:S(2)}) collective-permute-start(f32[120,256]{1,0:T(8,128)S(1)} %get-tuple-element.112), channel_id=1, source_target_pairs={{0,15},{1,2},{2,1},{3,4},{4,3},{5,6},{6,5},{7,8},{8,7},{9,10},{10,... | collective-permute-start | bytes 368648 | tf_op jit(solution)/shard_map/ppermute | solution.py:682
  19.9 5.2 %collective-permute-start.5 = (f32[120,256]{1,0:T(8,128)S(1)}, f32[120,256]{1,0:T(8,128)S(1)}, u32[]{:S(2)}, u32[]{:S(2)}) collective-permute-start(f32[120,256]{1,0:T(8,128)S(1)} %get-tuple-element.111), channel_id=1, source_target_pairs={{0,1},{1,0},{2,3},{3,2},{4,5},{5,4},{6,7},{7,6},{8,9},{9,8},{10,11... | collective-permute-start | bytes 368648 | tf_op jit(solution)/shard_map/ppermute | solution.py:681
  25.1 8.0 %collective-permute-start.6 = (f32[120,256]{1,0:T(8,128)S(1)}, f32[120,256]{1,0:T(8,128)S(1)}, u32[]{:S(2)}, u32[]{:S(2)}) collective-permute-start(f32[120,256]{1,0:T(8,128)S(1)} %get-tuple-element.108), channel_id=1, source_target_pairs={{0,240},{16,32},{32,16},{48,64},{64,48},{80,96},{96,80},{112,128},... | collective-permute-start | bytes 368648 | tf_op jit(solution)/shard_map/ppermute | solution.py:682
  29.6 6.7 %collective-permute-start.7 = (f32[120,256]{1,0:T(8,128)S(1)}, f32[120,256]{1,0:T(8,128)S(1)}, u32[]{:S(2)}, u32[]{:S(2)}) collective-permute-start(f32[120,256]{1,0:T(8,128)S(1)} %get-tuple-element.107), channel_id=1, source_target_pairs={{0,16},{16,0},{32,48},{48,32},{64,80},{80,64},{96,112},{112,96},{1... | collective-permute-start | bytes 368648 | tf_op jit(solution)/shard_map/ppermute | solution.py:681
  36.6 6.1 %collective-permute-start.8 = (f32[5,16,256]{2,1,0:T(8,128)S(1)}, f32[5,16,256]{2,1,0:T(8,128)S(1)}, u32[]{:S(2)}, u32[]{:S(2)}) collective-permute-start(f32[5,16,256]{2,1,0:T(8,128)S(1)} %get-tuple-element.116), channel_id=1, source_target_pairs={{0,15},{1,2},{2,1},{3,4},{4,3},{5,6},{6,5},{7,8},{8,7},{9,10},{10,... | collective-permute-start | bytes 245768 | tf_op jit(solution)/shard_map/ppermute | solution.py:682
  38.4 4.2 %collective-permute-start.9 = (f32[5,16,256]{2,1,0:T(8,128)S(1)}, f32[5,16,256]{2,1,0:T(8,128)S(1)}, u32[]{:S(2)}, u32[]{:S(2)}) collective-permute-start(f32[5,16,256]{2,1,0:T(8,128)S(1)} %get-tuple-element.115), channel_id=1, source_target_pairs={{0,1},{1,0},{2,3},{3,2},{4,5},{5,4},{6,7},{7,6},{8,9},{9,8},{10,11... | collective-permute-start | bytes 245768 | tf_op jit(solution)/shard_map/ppermute | solution.py:681
  42.8 7.8 %collective-permute-start.10 = (f32[120,256]{1,0:T(8,128)S(1)}, f32[120,256]{1,0:T(8,128)S(1)}, u32[]{:S(2)}, u32[]{:S(2)}) collective-permute-start(f32[120,256]{1,0:T(8,128)S(1)} %get-tuple-element.104), channel_id=1, source_target_pairs={{0,240},{16,32},{32,16},{48,64},{64,48},{80,96},{96,80},{112,128},... | collective-permute-start | bytes 368648 | tf_op jit(solution)/shard_map/ppermute | solution.py:682
  45.8 7.5 %collective-permute-start.11 = (f32[120,256]{1,0:T(8,128)S(1)}, f32[120,256]{1,0:T(8,128)S(1)}, u32[]{:S(2)}, u32[]{:S(2)}) collective-permute-start(f32[120,256]{1,0:T(8,128)S(1)} %get-tuple-element.103), channel_id=1, source_target_pairs={{0,16},{16,0},{32,48},{48,32},{64,80},{80,64},{96,112},{112,96},{1... | collective-permute-start | bytes 368648 | tf_op jit(solution)/shard_map/ppermute | solution.py:681

commit v8 on v7

--- a/solution.py
+++ b/solution.py
@@ -527,7 +527,7 @@
         split(ext, a, b, range(N // 2), 0)
 
 
-def sweep_kernel(even_in, odd_in, s_even_in, s_odd_in, fx_lo, fx_hi, xs_lo, xs_hi, out, ext, even, odd, s_even, s_odd):
+def sweep_kernel(even_in, odd_in, s_even_in, s_odd_in, fx_lo, fx_hi, xs_lo, xs_hi, out, ext, even, odd, s_even, s_odd, done, sems):
     mid = slice(OFF, OFF + N)
     top = RING + N
     half = (N + 2 * RING) // 2
@@ -558,6 +558,7 @@
             ext[top + a_ring - 1, y:y + 1, :] = xs_hi[at:at + 1, :]
         split(ext, a, b, ends, 1)
 
+    copies = []
     for h in range(6):
         this, other, s = (even, odd, s_even) if h % 2 == 0 else (odd, even, s_odd)
 
@@ -572,14 +573,15 @@
         lo = (h + 1) // 2
         for k in range(lo + 1, half - lo + 1):
             update(k, 0)
-
-    def last(k, carry):
-        p, q = even[k], odd[k]
-        out[2 * (k - 1) - RING] = jnp.where(mask, p, q)[OFF:OFF + N]
-        out[2 * (k - 1) - RING + 1] = jnp.where(mask, q, p)[OFF:OFF + N]
-        return carry
-
-    lax.fori_loop(RING // 2 + 1, RING // 2 + N // 2 + 1, last, 0)
+            if h == 5:
+                p, q = even[k], odd[k]
+                x = 2 * (k - 1) - RING
+                done[x] = jnp.where(mask, p, q)[OFF:OFF + N]
+                done[x + 1] = jnp.where(mask, q, p)[OFF:OFF + N]
+                copies.append(pltpu.make_async_copy(done.at[x:x + 2], out.at[x:x + 2], sems.at[x // 2]))
+                copies[-1].start()
+    for c in copies:
+        c.wait()
 
 
 def patch_kernel(buf, ex_lo, ex_hi, ey_lo, ey_hi, yh_lo, yh_hi, xh_lo, xh_hi, conc, out, conc_out, done, sems):
@@ -727,7 +729,7 @@
         scratch=[VM((N, N + 2 * OFF, Z), F32)], flops=1000000, moved=4000000)(pot, src, fy_lo, fy_hi, ys_lo, ys_hi)
     potential_out = call(
         sweep_kernel, [cube], "sweep", "v" * 8,
-        scratch=[VM((N + 2 * RING, N + 2 * OFF, Z), F32)] + [packed] * 4, flops=20000000, moved=4000000)(
+        scratch=[VM((N + 2 * RING, N + 2 * OFF, Z), F32)] + [packed] * 4 + [VM((N, N, Z), F32), pltpu.SemaphoreType.DMA((N // 2,))], out_specs="h", flops=20000000, moved=4000000)(
         *prepared, fx_lo, fx_hi, xs_lo, xs_hi)[0]
     pop, conc_out = call(
         patch_kernel, [sds(19, N, N, Z), pair], "patch", "v" * 10, out_specs="hh",

time: 55.5 us -> 55.5 us (level)
  no operation moved by 1% of the time
where the time goes in v8:
time: 55.5 us; the launch traced here: 55.4 us
  starting transfers between devices  20.2 us (36%)
  waiting for transfers between devices  19.8 us (36%)
  Pallas kernels  14.2 us (26%)
  between operations  1.03 us (2%)
    ppermute x6, starting transfers between devices, swap(): lax.ppermute(jnp.where(even, lo, hi), axis, [(i, (i - 1 + 2 * (i % 2)) %...  20.2 us
    ppermute x6, waiting for transfers between devices, swap(): lax.ppermute(jnp.where(even, lo, hi), axis, [(i, (i - 1 + 2 * (i % 2)) %...  13.2 us
    ppermute x6, waiting for transfers between devices, swap(): lax.ppermute(jnp.where(even, hi, lo), axis, [(i, i + 1 - 2 * (i % 2)) for...  6.54 us
    pallas_call x1, Pallas kernels, body(): call(collide_kernel, [sds(19, N, N, Z), sds(4, N, N, Z)] + [sds(19, N, Z)...  4.22 us
    pallas_call x1, Pallas kernels, body(): call(patch_kernel, [sds(19, N, N, Z), pair], 'patch', 'v' * 10, out_specs...  2.57 us
    pallas_call x1, Pallas kernels, body(): call(inner_kernel, [pair, sds(2, 4, N, Z), sds(2, 2, N, Z), sds(2, N, Z),...  2.34 us
    pallas_call x1, Pallas kernels, body(): call(sweep_kernel, [cube], 'sweep', 'v' * 8, scratch=[VM((N + 2 * RING, N...  1.96 us
    pallas_call x1, Pallas kernels, body(): call(faces_kernel, [sds(RING + 3, N, Z)] * 4 + [cube, sds(N - 2 * RING, N...  1.43 us
  transfers between devices with their start and end apart: 12, of which 8 were waited for; matrix products, arithmetic and copies ran while one was open for 0% of the time, Pallas kernels for 17%

profile of v8, /device:TPU:7, one launch (start us, length us, event | category | flops | bytes accessed | tf_op | source)
XLA Modules:
  0.0 55.4 jit_solution(13002596210415727598)
XLA Ops:
  0.6 1.4 %faces.1 = (f32[9,16,256]{2,1,0:T(8,128)S(1)}, f32[9,16,256]{2,1,0:T(8,128)S(1)}, f32[9,16,256]{2,1,0:T(8,128)S(1)}, f32[9,16,256]{2,1,0:T(8,128)S(1)}, f32[16,1...) custom-call(f32[16,16,256]{2,1,0:T(8,128)} %pot.3, f32[2,16,16,256]{3,2,1,0:T(8,128)} %conc.1, f32[16,16,256]{2,1,0:T(8,128)} %mob.1, ...), custom_call_target="tpu_custom_call" | custom-call | bytes 2600000 | tf_op jit(solution)/shard_map/faces/pallas_call | solution.py:691
  2.1 8.3 %collective-permute-start = (f32[9,16,256]{2,1,0:T(8,128)S(1)}, f32[9,16,256]{2,1,0:T(8,128)S(1)}, u32[]{:S(2)}, u32[]{:S(2)}) collective-permute-start(f32[9,16,256]{2,1,0:T(8,128)S(1)} %get-tuple-element.100), channel_id=1, source_target_pairs={{0,240},{16,32},{32,16},{48,64},{64,48},{80,96},{96,80},{112,128},... | collective-permute-start | bytes 442376 | tf_op jit(solution)/shard_map/ppermute | solution.py:684
  10.4 1.2 %collective-permute-start.2 = (f32[9,16,256]{2,1,0:T(8,128)S(1)}, f32[9,16,256]{2,1,0:T(8,128)S(1)}, u32[]{:S(2)}, u32[]{:S(2)}) collective-permute-start(f32[9,16,256]{2,1,0:T(8,128)S(1)} %get-tuple-element.96), channel_id=1, source_target_pairs={{0,15},{1,2},{2,1},{3,4},{4,3},{5,6},{6,5},{7,8},{8,7},{9,10},{10,... | collective-permute-start | bytes 442376 | tf_op jit(solution)/shard_map/ppermute | solution.py:684
  11.7 0.0 collective-permute-start.3
  11.7 4.2 %collide.1 = (f32[19,16,16,256]{3,2,1,0:T(8,128)S(1)}, f32[4,16,16,256]{3,2,1,0:T(8,128)S(1)}, f32[19,16,256]{2,1,0:T(8,128)S(1)}, f32[19,16,256]{2,1,0:T(8,128)...) custom-call(f32[19,16,16,256]{3,2,1,0:T(8,128)} %pops.1, f32[9,16,256]{2,1,0:T(8,128)S(1)} %get-tuple-element.48.gx_hi, ...), custom_call_target="tpu_custom_call" | custom-call | flops 20000000 | bytes 14000000 | tf_op jit(solution)/shard_map/collide/pallas_call | solution.py:700
  15.9 0.0 copy-start
  15.9 0.0 copy-start.1
  15.9 0.0 copy-start.2
  15.9 0.0 copy-start.3
  16.0 0.0 copy-start.4
  16.0 0.0 copy-start.5
  16.0 0.0 collective-permute-done
  16.0 0.7 %collective-permute-done.1 = f32[9,16,256]{2,1,0:T(8,128)S(1)} collective-permute-done((f32[9,16,256]{2,1,0:T(8,128)S(1)}, f32[9,16,256]{2,1,0:T(8,128)S(1)}, u32[]{:S(2)}, u32[]{:S(2)}) %collective-permute-start.1) | collective-permute-done | bytes 147488 | tf_op jit(solution)/shard_map/ppermute | solution.py:683
  16.7 0.8 %collective-permute-done.2 = f32[9,16,256]{2,1,0:T(8,128)S(1)} collective-permute-done((f32[9,16,256]{2,1,0:T(8,128)S(1)}, f32[9,16,256]{2,1,0:T(8,128)S(1)}, u32[]{:S(2)}, u32[]{:S(2)}) %collective-permute-start.2) | collective-permute-done | bytes 147488 | tf_op jit(solution)/shard_map/ppermute | solution.py:684
  17.5 1.0 %edge.1 = (f32[4,16,16,256]{3,2,1,0:T(8,128)S(1)}, f32[19,16,256]{2,1,0:T(8,128)S(1)}, f32[19,16,256]{2,1,0:T(8,128)S(1)}, f32[19,16,256]{2,1,0:T(8,128)S(1)}, f...) custom-call(f32[19,16,256]{2,1,0:T(8,128)S(1)} %get-tuple-element.53.px_lo, ...), custom_call_target="tpu_custom_call" | custom-call | bytes 3000000 | tf_op jit(solution)/shard_map/edge/pallas_call | solution.py:704
  18.5 1.3 %collective-permute-start.4 = (f32[120,256]{1,0:T(8,128)S(1)}, f32[120,256]{1,0:T(8,128)S(1)}, u32[]{:S(2)}, u32[]{:S(2)}) collective-permute-start(f32[120,256]{1,0:T(8,128)S(1)} %get-tuple-element.112), channel_id=1, source_target_pairs={{0,15},{1,2},{2,1},{3,4},{4,3},{5,6},{6,5},{7,8},{8,7},{9,10},{10,... | collective-permute-start | bytes 368648 | tf_op jit(solution)/shard_map/ppermute | solution.py:684
  19.9 5.2 %collective-permute-done.4 = f32[120,256]{1,0:T(8,128)S(1)} collective-permute-done((f32[120,256]{1,0:T(8,128)S(1)}, f32[120,256]{1,0:T(8,128)S(1)}, u32[]{:S(2)}, u32[]{:S(2)}) %collective-permute-start.4) | collective-permute-done | bytes 122912 | tf_op jit(solution)/shard_map/ppermute | solution.py:684
  25.1 4.5 %collective-permute-start.6 = (f32[120,256]{1,0:T(8,128)S(1)}, f32[120,256]{1,0:T(8,128)S(1)}, u32[]{:S(2)}, u32[]{:S(2)}) collective-permute-start(f32[120,256]{1,0:T(8,128)S(1)} %get-tuple-element.108), channel_id=1, source_target_pairs={{0,240},{16,32},{32,16},{48,64},{64,48},{80,96},{96,80},{112,128},... | collective-permute-start | bytes 368648 | tf_op jit(solution)/shard_map/ppermute | solution.py:684
  29.6 2.3 %inner.1 = (f32[2,16,16,256]{3,2,1,0:T(8,128)S(1)}, f32[2,4,16,256]{3,2,1,0:T(8,128)S(1)}, f32[2,2,16,256]{3,2,1,0:T(8,128)S(1)}, f32[2,16,256]{2,1,0:T(8,128)S(...) custom-call(f32[4]{0:T(128)S(1)} %copy-done.5, ...), custom_call_target="tpu_custom_call" | custom-call | flops 10000000 | bytes 6000000 | tf_op jit(solution)/shard_map/inner/pallas_call | solution.py:713
  32.0 1.2 %collective-permute-done.6 = f32[120,256]{1,0:T(8,128)S(1)} collective-permute-done((f32[120,256]{1,0:T(8,128)S(1)}, f32[120,256]{1,0:T(8,128)S(1)}, u32[]{:S(2)}, u32[]{:S(2)}) %collective-permute-start.6) | collective-permute-done | bytes 122912 | tf_op jit(solution)/shard_map/ppermute | solution.py:684
  33.2 3.1 %collective-permute-done.7 = f32[120,256]{1,0:T(8,128)S(1)} collective-permute-done((f32[120,256]{1,0:T(8,128)S(1)}, f32[120,256]{1,0:T(8,128)S(1)}, u32[]{:S(2)}, u32[]{:S(2)}) %collective-permute-start.7) | collective-permute-done | bytes 122912 | tf_op jit(solution)/shard_map/ppermute | solution.py:683
  36.3 0.3 transport.1
  36.6 1.8 %collective-permute-start.8 = (f32[5,16,256]{2,1,0:T(8,128)S(1)}, f32[5,16,256]{2,1,0:T(8,128)S(1)}, u32[]{:S(2)}, u32[]{:S(2)}) collective-permute-start(f32[5,16,256]{2,1,0:T(8,128)S(1)} %get-tuple-element.116), channel_id=1, source_target_pairs={{0,15},{1,2},{2,1},{3,4},{4,3},{5,6},{6,5},{7,8},{8,7},{9,10},{10,... | collective-permute-start | bytes 245768 | tf_op jit(solution)/shard_map/ppermute | solution.py:684
  38.4 0.0 collective-permute-start.9
  38.4 4.2 %collective-permute-done.8 = f32[5,16,256]{2,1,0:T(8,128)S(1)} collective-permute-done((f32[5,16,256]{2,1,0:T(8,128)S(1)}, f32[5,16,256]{2,1,0:T(8,128)S(1)}, u32[]{:S(2)}, u32[]{:S(2)}) %collective-permute-start.8) | collective-permute-done | bytes 81952 | tf_op jit(solution)/shard_map/ppermute | solution.py:684
  42.7 0.1 pack_src.1
  42.8 3.0 %collective-permute-start.10 = (f32[120,256]{1,0:T(8,128)S(1)}, f32[120,256]{1,0:T(8,128)S(1)}, u32[]{:S(2)}, u32[]{:S(2)}) collective-permute-start(f32[120,256]{1,0:T(8,128)S(1)} %get-tuple-element.104), channel_id=1, source_target_pairs={{0,240},{16,32},{32,16},{48,64},{64,48},{80,96},{96,80},{112,128},... | collective-permute-start | bytes 368648 | tf_op jit(solution)/shard_map/ppermute | solution.py:684
  45.8 2.6 %patch.1 = (f32[19,16,16,256]{3,2,1,0:T(8,128)}, f32[2,16,16,256]{3,2,1,0:T(8,128)}) custom-call(f32[19,16,16,256]{3,2,1,0:T(8,128)S(1)} %get-tuple-element.52.buf, f32[19,16,256]{2,1,0:T(8,128)S(1)} %get-tuple-element.60.ex_lo, f32[19,16,256]{2,1,0:T(8,128)S(1)} %get-tuple-element.61.ex_hi, f32[19,16,256]{2,1,0:T(8,128)S(1)} %get-tuple-element.62.ey_lo, ...), custom_call_target="tpu_custom_call" | custom-call | bytes 10000000 | tf_op jit(solution)/shard_map/patch/pallas_call | solution.py:734
  48.4 0.3 prepare.1
  48.6 1.9 %collective-permute-done.10 = f32[120,256]{1,0:T(8,128)S(1)} collective-permute-done((f32[120,256]{1,0:T(8,128)S(1)}, f32[120,256]{1,0:T(8,128)S(1)}, u32[]{:S(2)}, u32[]{:S(2)}) %collective-permute-start.10) | collective-permute-done | bytes 122912 | tf_op jit(solution)/shard_map/ppermute | solution.py:684
  50.6 2.7 %collective-permute-done.11 = f32[120,256]{1,0:T(8,128)S(1)} collective-permute-done((f32[120,256]{1,0:T(8,128)S(1)}, f32[120,256]{1,0:T(8,128)S(1)}, u32[]{:S(2)}, u32[]{:S(2)}) %collective-permute-start.11) | collective-permute-done | bytes 122912 | tf_op jit(solution)/shard_map/ppermute | solution.py:683
  53.3 2.0 %sweep.1 = f32[16,16,256]{2,1,0:T(8,128)} custom-call(f32[8,32,256]{2,1,0:T(8,128)S(1)} %get-tuple-element.87.even_in, f32[8,32,256]{2,1,0:T(8,128)S(1)} %get-tuple-element.88.odd_in, f32[8,32,256]{2,1,0:T(8,128)S(1)} %get-tuple-element.89.s_even_in, f32[8,32,256]{2,1,0:T(8,128)S(1)} %get-tuple-element.90.s_odd_in, ...), custom_call_target="tpu_custom_call" | custom-call | flops 20000000 | bytes 4000000 | tf_op jit(solution)/shard_map/sweep/pallas_call | solution.py:730
  (26 shorter events, 0.3 us)
Async XLA Ops:
  2.1 13.9 %collective-permute-start = (f32[9,16,256]{2,1,0:T(8,128)S(1)}, f32[9,16,256]{2,1,0:T(8,128)S(1)}, u32[]{:S(2)}, u32[]{:S(2)}) collective-permute-start(f32[9,16,256]{2,1,0:T(8,128)S(1)} %get-tuple-element.100), channel_id=1, source_target_pairs={{0,240},{16,32},{32,16},{48,64},{64,48},{80,96},{96,80},{112,128},... | collective-permute-start | bytes 442376 | tf_op jit(solution)/shard_map/ppermute | solution.py:684
  10.4 6.3 %collective-permute-start.1 = (f32[9,16,256]{2,1,0:T(8,128)S(1)}, f32[9,16,256]{2,1,0:T(8,128)S(1)}, u32[]{:S(2)}, u32[]{:S(2)}) collective-permute-start(f32[9,16,256]{2,1,0:T(8,128)S(1)} %get-tuple-element.99), channel_id=1, source_target_pairs={{0,16},{16,0},{32,48},{48,32},{64,80},{80,64},{96,112},{112,96},{1... | collective-permute-start | bytes 442376 | tf_op jit(solution)/shard_map/ppermute | solution.py:683
  10.4 7.1 %collective-permute-start.2 = (f32[9,16,256]{2,1,0:T(8,128)S(1)}, f32[9,16,256]{2,1,0:T(8,128)S(1)}, u32[]{:S(2)}, u32[]{:S(2)}) collective-permute-start(f32[9,16,256]{2,1,0:T(8,128)S(1)} %get-tuple-element.96), channel_id=1, source_target_pairs={{0,15},{1,2},{2,1},{3,4},{4,3},{5,6},{6,5},{7,8},{8,7},{9,10},{10,... | collective-permute-start | bytes 442376 | tf_op jit(solution)/shard_map/ppermute | solution.py:684
  11.7 5.8 %collective-permute-start.3 = (f32[9,16,256]{2,1,0:T(8,128)S(1)}, f32[9,16,256]{2,1,0:T(8,128)S(1)}, u32[]{:S(2)}, u32[]{:S(2)}) collective-permute-start(f32[9,16,256]{2,1,0:T(8,128)S(1)} %get-tuple-element.95), channel_id=1, source_target_pairs={{0,1},{1,0},{2,3},{3,2},{4,5},{5,4},{6,7},{7,6},{8,9},{9,8},{10,11... | collective-permute-start | bytes 442376 | tf_op jit(solution)/shard_map/ppermute | solution.py:683
  15.9 13.7 %copy-start = (f32[16,16,256]{2,1,0:T(8,128)S(1)}, f32[16,16,256]{2,1,0:T(8,128)}, u32[]{:S(2)}) copy-start(f32[16,16,256]{2,1,0:T(8,128)} %pot.3) | copy-start | bytes 786436
  15.9 13.7 %copy-start.1 = (f32[2,16,16,256]{3,2,1,0:T(8,128)S(1)}, f32[2,16,16,256]{3,2,1,0:T(8,128)}, u32[]{:S(2)}) copy-start(f32[2,16,16,256]{3,2,1,0:T(8,128)} %conc.1) | copy-start | bytes 1572868
  15.9 13.7 %copy-start.2 = (f32[16,16,256]{2,1,0:T(8,128)S(1)}, f32[16,16,256]{2,1,0:T(8,128)}, u32[]{:S(2)}) copy-start(f32[16,16,256]{2,1,0:T(8,128)} %mob.1) | copy-start | bytes 786436
  15.9 13.7 %copy-start.3 = (s32[16,16,256]{2,1,0:T(8,128)S(1)}, s32[16,16,256]{2,1,0:T(8,128)}, u32[]{:S(2)}) copy-start(s32[16,16,256]{2,1,0:T(8,128)} %solid.1) | copy-start | bytes 786436
  16.0 13.7 %copy-start.4 = (s32[16,16,256]{2,1,0:T(8,128)S(1)}, s32[16,16,256]{2,1,0:T(8,128)}, u32[]{:S(2)}) copy-start(s32[16,16,256]{2,1,0:T(8,128)} %classes_h.1) | copy-start | bytes 786436
  16.0 13.7 %copy-start.5 = (f32[4]{0:T(128)S(1)}, f32[4]{0:T(128)}, u32[]{:S(2)}) copy-start(f32[4]{0:T(128)} %charge.1) | copy-start | bytes 52
  18.5 6.5 %collective-permute-start.4 = (f32[120,256]{1,0:T(8,128)S(1)}, f32[120,256]{1,0:T(8,128)S(1)}, u32[]{:S(2)}, u32[]{:S(2)}) collective-permute-start(f32[120,256]{1,0:T(8,128)S(1)} %get-tuple-element.112), channel_id=1, source_target_pairs={{0,15},{1,2},{2,1},{3,4},{4,3},{5,6},{6,5},{7,8},{8,7},{9,10},{10,... | collective-permute-start | bytes 368648 | tf_op jit(solution)/shard_map/ppermute | solution.py:684
  19.9 5.2 %collective-permute-start.5 = (f32[120,256]{1,0:T(8,128)S(1)}, f32[120,256]{1,0:T(8,128)S(1)}, u32[]{:S(2)}, u32[]{:S(2)}) collective-permute-start(f32[120,256]{1,0:T(8,128)S(1)} %get-tuple-element.111), channel_id=1, source_target_pairs={{0,1},{1,0},{2,3},{3,2},{4,5},{5,4},{6,7},{7,6},{8,9},{9,8},{10,11... | collective-permute-start | bytes 368648 | tf_op jit(solution)/shard_map/ppermute | solution.py:683
  25.1 8.0 %collective-permute-start.6 = (f32[120,256]{1,0:T(8,128)S(1)}, f32[120,256]{1,0:T(8,128)S(1)}, u32[]{:S(2)}, u32[]{:S(2)}) collective-permute-start(f32[120,256]{1,0:T(8,128)S(1)} %get-tuple-element.108), channel_id=1, source_target_pairs={{0,240},{16,32},{32,16},{48,64},{64,48},{80,96},{96,80},{112,128},... | collective-permute-start | bytes 368648 | tf_op jit(solution)/shard_map/ppermute | solution.py:684
  29.6 6.7 %collective-permute-start.7 = (f32[120,256]{1,0:T(8,128)S(1)}, f32[120,256]{1,0:T(8,128)S(1)}, u32[]{:S(2)}, u32[]{:S(2)}) collective-permute-start(f32[120,256]{1,0:T(8,128)S(1)} %get-tuple-element.107), channel_id=1, source_target_pairs={{0,16},{16,0},{32,48},{48,32},{64,80},{80,64},{96,112},{112,96},{1... | collective-permute-start | bytes 368648 | tf_op jit(solution)/shard_map/ppermute | solution.py:683
  36.6 6.1 %collective-permute-start.8 = (f32[5,16,256]{2,1,0:T(8,128)S(1)}, f32[5,16,256]{2,1,0:T(8,128)S(1)}, u32[]{:S(2)}, u32[]{:S(2)}) collective-permute-start(f32[5,16,256]{2,1,0:T(8,128)S(1)} %get-tuple-element.116), channel_id=1, source_target_pairs={{0,15},{1,2},{2,1},{3,4},{4,3},{5,6},{6,5},{7,8},{8,7},{9,10},{10,... | collective-permute-start | bytes 245768 | tf_op jit(solution)/shard_map/ppermute | solution.py:684
  38.4 4.2 %collective-permute-start.9 = (f32[5,16,256]{2,1,0:T(8,128)S(1)}, f32[5,16,256]{2,1,0:T(8,128)S(1)}, u32[]{:S(2)}, u32[]{:S(2)}) collective-permute-start(f32[5,16,256]{2,1,0:T(8,128)S(1)} %get-tuple-element.115), channel_id=1, source_target_pairs={{0,1},{1,0},{2,3},{3,2},{4,5},{5,4},{6,7},{7,6},{8,9},{9,8},{10,11... | collective-permute-start | bytes 245768 | tf_op jit(solution)/shard_map/ppermute | solution.py:683
  42.8 7.8 %collective-permute-start.10 = (f32[120,256]{1,0:T(8,128)S(1)}, f32[120,256]{1,0:T(8,128)S(1)}, u32[]{:S(2)}, u32[]{:S(2)}) collective-permute-start(f32[120,256]{1,0:T(8,128)S(1)} %get-tuple-element.104), channel_id=1, source_target_pairs={{0,240},{16,32},{32,16},{48,64},{64,48},{80,96},{96,80},{112,128},... | collective-permute-start | bytes 368648 | tf_op jit(solution)/shard_map/ppermute | solution.py:684
  45.8 7.5 %collective-permute-start.11 = (f32[120,256]{1,0:T(8,128)S(1)}, f32[120,256]{1,0:T(8,128)S(1)}, u32[]{:S(2)}, u32[]{:S(2)}) collective-permute-start(f32[120,256]{1,0:T(8,128)S(1)} %get-tuple-element.103), channel_id=1, source_target_pairs={{0,16},{16,0},{32,48},{48,32},{64,80},{80,64},{96,112},{112,96},{1... | collective-permute-start | bytes 368648 | tf_op jit(solution)/shard_map/ppermute | solution.py:683
